TPU v7x, 32 devices: a whole 2x2x4 slice. The times are simulated.
32 devices in a mesh: batch: 8 (over z, core), seq: 4 (over y, x).
Axes of the slice: x: 2, y: 2, z: 4, core: 2. Of those that a mesh axis runs over, the one named last changes fastest.
Arguments:
- frames_in: bfloat16 [8, 1024, 1024], P('batch', 'seq'), may hold values from -6 to 6
- cotangent: bfloat16 [8, 1024, 1024], P('batch', 'seq'), may hold values from -6 to 6
- levels: int32 [8], P('batch'), may hold values from 1 to 12
- lengths: int32 [8], replicated, may hold values from 256 to 1024, as said below
- token_mask: int32 [8, 1024], P('batch', 'seq'), may hold values 0 or 1
- cond_table: bfloat16 [13, 1024], replicated, may hold values from -3 to 3
- norm_gains: bfloat16 [5, 1024], replicated, may hold values from 0.25 to 1.75
- w_ffn1_up: bfloat16 [1024, 4096], replicated, may hold values from -0.1875 to 0.1875
- w_ffn1_down: bfloat16 [4096, 1024], replicated, may hold values from -0.1875 to 0.1875
- w_qkv: bfloat16 [1024, 3072], replicated, may hold values from -0.25 to 0.25
- w_out: bfloat16 [1024, 1024], replicated, may hold values from -1.5 to 1.5
- w_glu: bfloat16 [1024, 2048], replicated, may hold values from -0.1875 to 0.1875
- conv_kernel: bfloat16 [5, 1024], replicated, may hold values from -2.5 to 2.5
- bn_gain: bfloat16 [1024], replicated, may hold values from 0.25 to 1.75
- batchnorm_shift_bias: bfloat16 [1024], replicated, may hold values from -3 to 3
- w_conv_out: bfloat16 [1024, 1024], replicated, may hold values from -0.1875 to 0.1875
- w_ffn2_up: bfloat16 [1024, 4096], replicated, may hold values from -0.1875 to 0.1875
- w_ffn2_down: bfloat16 [4096, 1024], replicated, may hold values from -0.1875 to 0.1875
- running_mean: float32 [1024], replicated, may hold values from -0.24 to 0.24
- running_var: float32 [1024], replicated, may hold values from 0.02 to 0.1
Outputs:
- out: bfloat16 [8, 1024, 1024], P('batch', 'seq')
- input_grad: bfloat16 [8, 1024, 1024], P('batch', 'seq')
- cond_grad: float32 [13, 1024], P(None, 'seq')
- gains_grad: float32 [5, 1024], P(None, 'seq')
- w_ffn1_up_grad: float32 [1024, 4096], P('seq', 'batch')
- w_ffn1_down_grad: float32 [4096, 1024], P(('batch', 'seq'))
- w_qkv_grad: float32 [1024, 3072], P('seq', 'batch')
- w_out_grad: float32 [1024, 1024], P('seq', 'batch')
- w_glu_grad: float32 [1024, 2048], P('seq', 'batch')
- kernel_grad: float32 [5, 1024], P(None, 'seq')
- bn_gain_grad: float32 [1024], replicated
- bn_bias_grad: float32 [1024], replicated
- w_conv_out_grad: float32 [1024, 1024], P('seq', 'batch')
- w_ffn2_up_grad: float32 [1024, 4096], P('seq', 'batch')
- w_ffn2_down_grad: float32 [4096, 1024], P(('batch', 'seq'))
- new_running_mean: float32 [1024], replicated
- new_running_var: float32 [1024], replicated
Inputs may be any that keep to these rules, and one draw needn't show every extreme that they name: `lengths`: each item has between 256 and 1024 valid frames, a prefix of the item; at least one item is valid throughout.
All inputs are finite; a program needn't handle non-finite values. No bound on the sum of `token_mask` on one device may be relied on, other than what follows from the above.
Results may differ from a plain program's by a relative error of at most 0.024.
Values may be sent and summed in bfloat16 or wider, within the bound.
A program may use at most 448 MiB of HBM per device.

v0:
```python
import math

import jax
import jax.numpy as jnp
from jax import lax
from jax.sharding import PartitionSpec as P

HEADS = 16
HD = 64


EPSILON = 1e-05
MASKED_SCORE = -1000000000.0


def extended(array, sides, width):
    for axis, dim in sides:
        devices, length = (lax.axis_size(axis), array.shape[dim])
        up = [(i, (i + 1) % devices) for i in range(devices - 1)]
        down = [(j, i) for i, j in up]
        last = lax.slice_in_dim(array, length - width, length, axis=dim)
        leading = lax.slice_in_dim(array, 0, width, axis=dim)
        before = lax.ppermute(last, axis, up)
        after = lax.ppermute(leading, axis, down)
        array = jnp.concatenate([before, array, after], axis=dim)
    return array


def layer_norm(values, gain_row):
    centre = values - jnp.mean(values, axis=-1, keepdims=True)
    spread = jnp.mean(centre * centre, axis=-1, keepdims=True)
    return centre * lax.rsqrt(spread + EPSILON) * gain_row


def rope_tables(positions, head_size):
    half_size = head_size // 2
    inv_freqs = jnp.exp(
        jnp.arange(half_size).astype(jnp.float32) * (-2.0 * math.log(10000.0) / head_size)
    )
    angles = positions.astype(jnp.float32)[:, None] * inv_freqs[None, :]
    return (jnp.cos(angles), jnp.sin(angles))


def rotate(values, cosine, sine_table):
    half_size = values.shape[-1] // 2
    first_half = values[..., :half_size]
    second_half = values[..., half_size:]
    return jnp.concatenate(
        [
            first_half * cosine - second_half * sine_table,
            second_half * cosine + first_half * sine_table,
        ],
        axis=-1,
    )


def unrotate(grads, cosine, sine_table):
    half_size = grads.shape[-1] // 2
    first_half = grads[..., :half_size]
    second_half = grads[..., half_size:]
    return jnp.concatenate(
        [
            first_half * cosine + second_half * sine_table,
            second_half * cosine - first_half * sine_table,
        ],
        axis=-1,
    )


def times_transposed(left_side, weight):
    return lax.dot_general(
        left_side, weight, (((1,), (1,)), ((), ())), preferred_element_type=jnp.float32
    )


def pair_frames(rows_in):
    frames, groups, group_width = rows_in.shape
    paired = rows_in.reshape(frames // 2, 2, groups, group_width).transpose(0, 2, 1, 3)
    return paired.reshape(frames // 2, groups, 2 * group_width)


def unpair_frames(rows_in):
    pairs, groups, double_width = rows_in.shape
    split_rows = rows_in.reshape(pairs, groups, 2, double_width // 2).transpose(0, 2, 1, 3)
    return split_rows.reshape(2 * pairs, groups * (double_width // 2))


def ffn_forward(values, gain_row, up_weight, down_weight):
    normed, ln_pull = jax.vjp(layer_norm, values, gain_row)
    lowered = normed.astype(jnp.bfloat16)
    hidden = jnp.dot(lowered, up_weight, preferred_element_type=jnp.float32)
    act_rows = (hidden * jax.nn.sigmoid(hidden)).astype(jnp.bfloat16)
    branch = jnp.dot(act_rows, down_weight, preferred_element_type=jnp.float32)
    return (values + 0.5 * branch, (ln_pull, lowered, hidden, act_rows))


def ffn_backward(grad_in, saved_state, up_weight, down_weight):
    ln_pull, lowered, hidden, act_rows = saved_state
    grad_branch = (0.5 * grad_in).astype(jnp.bfloat16)
    grad_act = times_transposed(grad_branch, down_weight)
    gate_sig = jax.nn.sigmoid(hidden)
    grad_hidden = (grad_act * gate_sig * (1.0 + hidden * (1.0 - gate_sig))).astype(jnp.bfloat16)
    grad_normed = times_transposed(grad_hidden, up_weight)
    grad_values, grad_gain = ln_pull(grad_normed)
    return (grad_in + grad_values, grad_gain, (lowered, grad_hidden), (act_rows, grad_branch))


def shards(
    frames_in,
    cotangent,
    levels,
    lengths,
    token_mask,
    cond_table,
    norm_gains,
    w_ffn1_up,
    w_ffn1_down,
    w_qkv,
    w_out,
    w_glu,
    conv_kernel,
    bn_gain,
    batchnorm_shift_bias,
    w_conv_out,
    w_ffn2_up,
    w_ffn2_down,
    running_mean,
    running_var,
):
    frames = frames_in.shape[1]
    model_width = frames_in.shape[2]
    ff_width = w_ffn1_up.shape[1]
    groups = lax.axis_size("seq")
    batches = lax.axis_size("batch")
    seq_index = lax.axis_index("seq")
    item_index = lax.axis_index("batch")
    seq_length = frames * groups
    local_heads = HEADS // groups
    head_width = local_heads * HD
    level_count = cond_table.shape[0] - 1
    cond_rows = cond_table.astype(jnp.float32)
    gain_rows = norm_gains.astype(jnp.float32)
    level_hot = (jnp.arange(level_count) == levels[0] - 1).astype(jnp.float32)
    level_vector = jnp.sum(level_hot[:, None] * cond_rows[:level_count], axis=0)
    mask_column = token_mask[0].astype(jnp.float32)[:, None]
    start_rows = (
        frames_in[0].astype(jnp.float32)
        + level_vector[None, :]
        + mask_column * cond_rows[level_count][None, :]
    )
    length = lax.dynamic_slice_in_dim(lengths, item_index, 1)[0]
    positions = seq_index * frames + jnp.arange(frames)
    unpadded_rows = (positions < length).astype(jnp.float32)[:, None]
    rows_one, ffn1_state = ffn_forward(start_rows, gain_rows[0], w_ffn1_up, w_ffn1_down)
    normed_attn, attn_pull = jax.vjp(layer_norm, rows_one, gain_rows[1])
    attn_in = normed_attn.astype(jnp.bfloat16)
    qkv_rows = jnp.dot(attn_in, w_qkv, preferred_element_type=jnp.float32).reshape(
        frames, HEADS, 3, HD
    )
    cosine, sine_table = rope_tables(positions, HD)
    query_rot = rotate(qkv_rows[:, :, 0], cosine[:, None], sine_table[:, None]) * 0.125
    key_rot = rotate(qkv_rows[:, :, 1], cosine[:, None], sine_table[:, None])
    packed = jnp.stack([query_rot, key_rot, qkv_rows[:, :, 2]], axis=2).astype(jnp.bfloat16)
    incoming = lax.all_to_all(
        pair_frames(packed.reshape(frames, groups, local_heads * 3 * HD)),
        "seq",
        split_axis=1,
        concat_axis=0,
        tiled=True,
    )
    whole_heads = incoming.reshape(seq_length, local_heads, 3, HD)
    query_all = whole_heads[:, :, 0]
    key_all = whole_heads[:, :, 1]
    value_all = whole_heads[:, :, 2]
    key_valid = (jnp.arange(seq_length) < length)[None, None, :]
    block_rows = min(512, seq_length)
    block_count = seq_length // block_rows
    query_blocks = query_all.reshape(block_count, block_rows, local_heads, HD)

    def attend_block(query_block):
        scores = jnp.einsum(
            "qhd,khd->hqk", query_block, key_all, preferred_element_type=jnp.float32
        )
        scores = jnp.where(key_valid, scores, MASKED_SCORE)
        row_peak = jnp.max(scores, axis=-1, keepdims=True)
        exp_scores = jnp.exp(scores - row_peak)
        row_total = jnp.sum(exp_scores, axis=-1, keepdims=True)
        probs_low = (exp_scores / row_total).astype(jnp.bfloat16)
        mixed_block = jnp.einsum(
            "hqk,khd->qhd", probs_low, value_all, preferred_element_type=jnp.float32
        )
        return (mixed_block.astype(jnp.bfloat16), (row_peak + jnp.log(row_total))[:, :, 0])

    mixed_blocks, lse_blocks = lax.map(attend_block, query_blocks)
    mixed_rows = mixed_blocks.reshape(seq_length // 2, 1, 2 * head_width)
    attn_out = unpair_frames(
        lax.all_to_all(mixed_rows, "seq", split_axis=0, concat_axis=1, tiled=True)
    )
    rows_two = rows_one + jnp.dot(attn_out, w_out, preferred_element_type=jnp.float32)
    normed_conv, conv_pull = jax.vjp(layer_norm, rows_two, gain_rows[2])
    conv_in = normed_conv.astype(jnp.bfloat16)
    glu_pre = jnp.dot(conv_in, w_glu, preferred_element_type=jnp.float32)
    up_half = glu_pre[:, :model_width]
    glu_sig = jax.nn.sigmoid(glu_pre[:, model_width:])
    glu_low = (up_half * glu_sig * unpadded_rows).astype(jnp.bfloat16)
    taps = conv_kernel.shape[0]
    half_size = taps // 2
    kernel_rows = conv_kernel.astype(jnp.float32)
    padded = extended(glu_low, (("seq", 0),), half_size)
    convolved_rows = jnp.zeros((frames, model_width), jnp.float32)
    for tap_index in range(taps):
        convolved_rows = (
            convolved_rows + kernel_rows[tap_index] * padded[tap_index : tap_index + frames]
        )
    sum_rows = jnp.sum(convolved_rows * unpadded_rows, axis=0)
    sum_squares = jnp.sum(convolved_rows * convolved_rows * unpadded_rows, axis=0)
    total_sum, total_squares = lax.psum((sum_rows, sum_squares), ("batch", "seq"))
    count_of_frames = jnp.sum(lengths).astype(jnp.float32)
    batchnorm_frame_mean = total_sum / count_of_frames
    bn_var = total_squares / count_of_frames - batchnorm_frame_mean * batchnorm_frame_mean
    batchnorm_inverse_deviation = lax.rsqrt(bn_var + EPSILON)
    batchnorm_scale_factor = bn_gain.astype(jnp.float32)
    normalized_rows = (convolved_rows - batchnorm_frame_mean) * batchnorm_inverse_deviation
    batchnorm_input_rows = normalized_rows * batchnorm_scale_factor + batchnorm_shift_bias.astype(
        jnp.float32
    )
    bn_sig = jax.nn.sigmoid(batchnorm_input_rows)
    conv_act = (batchnorm_input_rows * bn_sig).astype(jnp.bfloat16)
    rows_three = rows_two + jnp.dot(conv_act, w_conv_out, preferred_element_type=jnp.float32)
    rows_four, ffn2_state = ffn_forward(rows_three, gain_rows[3], w_ffn2_up, w_ffn2_down)
    normed_out, out_pull = jax.vjp(layer_norm, rows_four, gain_rows[4])
    out_rows = normed_out.astype(jnp.bfloat16)
    grad_four, grad_gain_four = out_pull(cotangent[0].astype(jnp.float32))
    grad_three, grad_gain_three, ffn2_up_pair, ffn2_down_pair = ffn_backward(
        grad_four, ffn2_state, w_ffn2_up, w_ffn2_down
    )
    grad_r2 = grad_three.astype(jnp.bfloat16)
    batchnorm_gradient = (
        times_transposed(grad_r2, w_conv_out)
        * bn_sig
        * (1.0 + batchnorm_input_rows * (1.0 - bn_sig))
    )
    gradient_sum_total, gradient_normalized_sum = lax.psum(
        (
            jnp.sum(batchnorm_gradient, axis=0),
            jnp.sum(batchnorm_gradient * normalized_rows, axis=0),
        ),
        ("batch", "seq"),
    )
    grad_conv = (
        batchnorm_scale_factor
        * batchnorm_inverse_deviation
        * (
            batchnorm_gradient
            - unpadded_rows
            * (gradient_sum_total + normalized_rows * gradient_normalized_sum)
            / count_of_frames
        )
    ).astype(jnp.bfloat16)
    grad_pad = extended(grad_conv, (("seq", 0),), half_size)
    grad_glu = jnp.zeros((frames, model_width), jnp.float32)
    kernel_terms = []
    for tap_index in range(taps):
        offset = 2 * half_size - tap_index
        grad_glu = grad_glu + kernel_rows[tap_index] * grad_pad[offset : offset + frames]
        kernel_terms.append(
            jnp.einsum(
                "fd,fd->d",
                padded[tap_index : tap_index + frames],
                grad_conv,
                preferred_element_type=jnp.float32,
            )
        )
    kernel_grads = jnp.stack(kernel_terms, axis=0)
    grad_glu = grad_glu * unpadded_rows
    grad_gl = jnp.concatenate(
        [grad_glu * glu_sig, grad_glu * up_half * glu_sig * (1.0 - glu_sig)], axis=1
    ).astype(jnp.bfloat16)
    grad_conv_in, grad_gain_two = conv_pull(times_transposed(grad_gl, w_glu))
    grad_two = grad_three + grad_conv_in
    grad_r = grad_two.astype(jnp.bfloat16)
    grad_attn_out = times_transposed(grad_r, w_out).astype(jnp.bfloat16)
    grad_heads = lax.all_to_all(
        pair_frames(grad_attn_out.reshape(frames, groups, head_width)),
        "seq",
        split_axis=1,
        concat_axis=0,
        tiled=True,
    )
    grad_blocks = grad_heads.reshape(block_count, block_rows, local_heads, HD)

    def attend_back(carry_pair, pieces):
        grad_key, grad_value = carry_pair
        query_block, grad_block, lse_block = pieces
        scores = jnp.einsum(
            "qhd,khd->hqk", query_block, key_all, preferred_element_type=jnp.float32
        )
        scores = jnp.where(key_valid, scores, MASKED_SCORE)
        probs_row = jnp.exp(scores - lse_block[:, :, None])
        probs_low = probs_row.astype(jnp.bfloat16)
        grad_value = grad_value + jnp.einsum(
            "hqk,qhd->khd", probs_low, grad_block, preferred_element_type=jnp.float32
        )
        grad_probs = jnp.einsum(
            "qhd,khd->hqk", grad_block, value_all, preferred_element_type=jnp.float32
        )
        grad_scores = (
            probs_row * (grad_probs - jnp.sum(probs_row * grad_probs, axis=-1, keepdims=True))
        ).astype(jnp.bfloat16)
        grad_query = jnp.einsum(
            "hqk,khd->qhd", grad_scores, key_all, preferred_element_type=jnp.float32
        )
        grad_key = grad_key + jnp.einsum(
            "hqk,qhd->khd", grad_scores, query_block, preferred_element_type=jnp.float32
        )
        return ((grad_key, grad_value), grad_query)

    zero_heads = jnp.zeros((seq_length, local_heads, HD), jnp.float32)
    key_value_grads, query_grads = lax.scan(
        attend_back, (zero_heads, zero_heads), (query_blocks, grad_blocks, lse_blocks)
    )
    cos_all, sin_all = rope_tables(jnp.arange(seq_length), HD)
    grad_query_pre = (
        unrotate(
            query_grads.reshape(seq_length, local_heads, HD), cos_all[:, None], sin_all[:, None]
        )
        * 0.125
    )
    grad_key_pre = unrotate(key_value_grads[0], cos_all[:, None], sin_all[:, None])
    stacked = jnp.stack([grad_query_pre, grad_key_pre, key_value_grads[1]], axis=2).astype(
        jnp.bfloat16
    )
    returned = lax.all_to_all(
        stacked.reshape(seq_length // 2, 1, 2 * local_heads * 3 * HD),
        "seq",
        split_axis=0,
        concat_axis=1,
        tiled=True,
    )
    grad_qkv = unpair_frames(returned)
    grad_attn_part, grad_gain_one = attn_pull(times_transposed(grad_qkv, w_qkv))
    grad_one = grad_two + grad_attn_part
    grad_zero, grad_gain_zero, ffn1_up_pair, ffn1_down_pair = ffn_backward(
        grad_one, ffn1_state, w_ffn1_up, w_ffn1_down
    )
    column_total = jnp.sum(grad_zero, axis=0)
    cond_grad_rows = jnp.concatenate(
        [
            level_hot[:, None] * column_total[None, :],
            jnp.sum(mask_column * grad_zero, axis=0)[None, :],
        ],
        axis=0,
    )
    gain_grads = jnp.stack(
        [grad_gain_zero, grad_gain_one, grad_gain_two, grad_gain_three, grad_gain_four], axis=0
    )
    small_rows = jnp.concatenate([gain_grads, cond_grad_rows, kernel_grads], axis=0)
    small_cols = jnp.pad(small_rows, ((0, 128 - small_rows.shape[0]), (0, 0))).T
    model_pairs = [
        ffn1_up_pair,
        (attn_in, grad_qkv),
        (attn_out, grad_r),
        (conv_in, grad_gl),
        (conv_act, grad_r2),
        ffn2_up_pair,
    ]
    hidden_pairs = [ffn1_down_pair, ffn2_down_pair]
    block_parts = [
        jnp.einsum("fr,fc->rc", left_side, right_side, preferred_element_type=jnp.float32).reshape(
            model_width, batches, -1
        )
        for left_side, right_side in model_pairs
    ]
    block_parts.append(jnp.broadcast_to(small_cols[:, None, :], (model_width, batches, 128)))
    model_full = (
        jnp.concatenate(block_parts, axis=2).transpose(1, 0, 2).reshape(batches * model_width, -1)
    )
    model_grad = lax.psum_scatter(model_full, ("batch", "seq"), scatter_dimension=0, tiled=True)
    column_parts = [
        jnp.einsum("fr,fc->rc", left_side, right_side, preferred_element_type=jnp.float32)
        for left_side, right_side in hidden_pairs
    ]
    hidden_grad = lax.psum_scatter(
        jnp.concatenate(column_parts, axis=1), ("batch", "seq"), scatter_dimension=0, tiled=True
    )
    edge_one = ff_width // batches
    edge_two = edge_one + 3 * model_width // batches
    edge_three = edge_two + model_width // batches
    edge_four = edge_three + 2 * model_width // batches
    edge_five = edge_four + model_width // batches
    edge_six = edge_five + ff_width // batches
    small_piece = model_grad[:, edge_six : edge_six + 128]
    cond_end = 5 + level_count + 1
    new_mean = 0.9 * running_mean + 0.1 * batchnorm_frame_mean
    new_var = 0.9 * running_var + 0.1 * bn_var * count_of_frames / (count_of_frames - 1.0)
    return (
        out_rows[None],
        grad_zero.astype(jnp.bfloat16)[None],
        small_piece[:, 5:cond_end].T,
        small_piece[:, 0:5].T,
        model_grad[:, 0:edge_one],
        hidden_grad[:, 0:model_width],
        model_grad[:, edge_one:edge_two],
        model_grad[:, edge_two:edge_three],
        model_grad[:, edge_three:edge_four],
        small_piece[:, cond_end : cond_end + taps].T,
        gradient_normalized_sum,
        gradient_sum_total,
        model_grad[:, edge_four:edge_five],
        model_grad[:, edge_five:edge_six],
        hidden_grad[:, model_width : 2 * model_width],
        new_mean,
        new_var,
    )


def solution(mesh):
    in_specs = (
        P("batch", "seq", None),
        P("batch", "seq", None),
        P("batch"),
        P(),
        P("batch", "seq"),
        P(),
        P(),
        P(),
        P(),
        P(),
        P(),
        P(),
        P(),
        P(),
        P(),
        P(),
        P(),
        P(),
        P(),
        P(),
    )
    out_specs = (
        P("batch", "seq", None),
        P("batch", "seq", None),
        P(None, "seq"),
        P(None, "seq"),
        P("seq", "batch"),
        P(("batch", "seq"), None),
        P("seq", "batch"),
        P("seq", "batch"),
        P("seq", "batch"),
        P(None, "seq"),
        P(),
        P(),
        P("seq", "batch"),
        P("seq", "batch"),
        P(("batch", "seq"), None),
        P(),
        P(),
    )
    return jax.shard_map(shards, mesh=mesh, in_specs=in_specs, out_specs=out_specs, check_vma=False)
```

profile of v0, /device:TPU:0, one launch (start us, length us, event | category | flops | bytes accessed | tf_op | source)
XLA Modules:
  0.0 2651.1 jit_solution(16180905625376335812)
XLA Ops:
  15.8 6.2 fusion.84
  33.7 7.4 copy.117
  41.1 8.6 convert_element_type.247
  59.8 19.3 all-to-all-done
  81.7 9.0 reshape.553
  90.6 11.0 fusion.133
  114.7 15.8 while.28
  150.8 7.1 all-to-all-done.1
  186.9 50.3 %all-reduce.2 = (f32[1024]{0:T(1024)S(1)}, f32[1024]{0:T(1024)S(1)}) all-reduce(f32[1024]{0:T(1024)S(1)} %get-tuple-element.301, f32[1024]{0:T(1024)S(1)} %get-tuple-element.300), channel_id=1, replica_groups=mesh['batch'=8,'seq'=4] {'batch','seq'}, use_global_device_ids=true, to_apply=%region_12.13 | all-reduce | flops 2048 | bytes 16384 | tf_op jit(solution)/shard_map/psum | solution.py:217
  240.8 6.0 fusion.126
  257.7 7.3 multiply_reduce_fusion.2
  268.4 41.7 %all-reduce.1 = (f32[1024]{0:T(1024)S(1)}, f32[1024]{0:T(1024)S(1)}) all-reduce(f32[1024]{0:T(1024)S(1)} %get-tuple-element.308, f32[1024]{0:T(1024)S(1)} %get-tuple-element.307), channel_id=1, replica_groups=mesh['batch'=8,'seq'=4] {'batch','seq'}, use_global_device_ids=true, to_apply=%region_27.28 | all-reduce | flops 2048 | bytes 16384 | tf_op jit(solution)/shard_map/psum | solution.py:243
  339.9 6.1 all-to-all-done.2
  350.4 61.0 %while.29 = (s32[]{:T(128)}, f32[1024,4,64]{0,2,1:T(8,128)S(1)}, f32[1024,4,64]{0,2,1:T(8,128)}, f32[2,512,4,64]{1,0,3,2:T(2,128)}, bf16[2,512,4,64]{1,3,2,0:T(8...) while((s32[]{:T(128)}, f32[1024,4,64]{0,2,1:T(8,128)S(1)}, ...), condition=%wide.region_32.33_spmd.clone, body=%wide.region_30.32_spmd.clone.sunk | while | flops 1368390656 | bytes 156299504 | solution.py:319
  370.3 10.4 dynamic_update_slice.22
  401.0 10.4 dynamic_update_slice.22
  421.1 14.2 convert_element_type.293
  435.4 11.2 reduce.15
  452.9 10.5 fusion.122
  490.0 10.1 fusion.107
  500.1 18.7 pad_maximum_fusion
  525.7 8.3 fusion.125
  536.1 6.0 fusion.78
  542.1 9.2 fusion.49
  558.3 10.9 multiply_reduce_fusion.5
  571.5 10.2 convolution_dynamic-update-slice_fusion
  581.7 6.6 convolution_dynamic-update-slice_fusion.1
  591.1 9.1 constant_dynamic-update-slice_fusion.2
  604.1 6.2 constant_dynamic-update-slice_fusion
  612.9 66.9 %copy.141 = f32[8,1024,2048]{2,1,0:T(8,128)} copy(f32[8,1024,2048]{1,2,0:T(8,128)} %bitcast.80) | data formatting | bytes 134217728 | tf_op jit(solution)/shard_map/transpose | solution.py:376
  681.1 544.7 %reduce-scatter.5.cloned.1.call-done = f32[128,2048]{0,1:T(8,128)} async-done(((f32[4096,2048]{0,1:T(8,128)}), f32[128,2048]{0,1:T(8,128)}) %reduce-scatter.5.cloned.1.call-update) | async-done | bytes 1048592 | tf_op jit(solution)/shard_map/reduce_scatter | solution.py:383
  1229.1 1403.6 %reduce-scatter.3.cloned.1.call-done = f32[256,2048]{1,0:T(8,128)} async-done(((f32[8192,2048]{1,0:T(8,128)}), f32[256,2048]{1,0:T(8,128)}) %reduce-scatter.3.cloned.1.call-update) | async-done | bytes 2097168 | tf_op jit(solution)/shard_map/reduce_scatter | solution.py:378
  (450 shorter events, 286.6 us)
Async XLA Ops:
  7.2 230.6 %copy-start = (bf16[1024,1024]{1,0:T(8,128)(2,1)S(1)}, bf16[1024,1024]{1,0:T(8,128)(2,1)}, u32[]{:S(2)}) copy-start(bf16[1024,1024]{1,0:T(8,128)(2,1)} %param.39) | copy-start | bytes 6291460
  8.1 13.8 copy-start.45
  10.4 15.1 copy-start.60
  10.4 254.7 %copy-start.41 = (f32[1,1024]{1,0:T(1,128)}, f32[1,1024]{1,0:T(1,128)S(1)}, u32[]{:S(2)}) copy-start(f32[1,1024]{1,0:T(1,128)S(1)} %get-tuple-element.402) | copy-start | bytes 12292
  10.4 320.6 %copy-start.43 = (f32[1,1024]{1,0:T(1,128)}, f32[1,1024]{1,0:T(1,128)S(1)}, u32[]{:S(2)}) copy-start(f32[1,1024]{1,0:T(1,128)S(1)} %get-tuple-element.403) | copy-start | bytes 12292
  53.6 25.4 all-to-all-start
  146.0 11.9 all-to-all-start.1
  171.9 159.1 %copy-start.51 = (f32[256]{0:T(256)}, f32[256]{0:T(256)S(1)}, u32[]{:S(2)}) copy-start(f32[256]{0:T(256)S(1)} %broadcast_multiply_fusion.3) | copy-start | bytes 3076
  172.2 158.8 %copy-start.64 = (f32[256]{0:T(256)}, f32[256]{0:T(256)S(1)}, u32[]{:S(2)}) copy-start(f32[256]{0:T(256)S(1)} %fusion.114) | copy-start | bytes 3076
  172.2 65.0 %copy-start.90 = (f32[1024]{0:T(1024)S(1)}, f32[1024]{0:T(1024)}, u32[]{:S(2)}) copy-start(f32[1024]{0:T(1024)} %param.43) | copy-start | bytes 12292
  175.8 7.2 collective-permute-start.1
  177.1 5.9 collective-permute-start
  182.3 83.6 %copy-start.94 = (f32[1024]{0:T(1024)}, f32[1024]{0:T(1024)S(1)}, u32[]{:S(2)}) copy-start(f32[1024]{0:T(1024)S(1)} %convert_element_type.259) | copy-start | bytes 12292
  182.3 83.6 %copy-start.96 = (f32[1024]{0:T(1024)}, f32[1024]{0:T(1024)S(1)}, u32[]{:S(2)}) copy-start(f32[1024]{0:T(1024)S(1)} %convert_element_type.258) | copy-start | bytes 12292
  237.8 72.3 %copy-start.58 = (f32[1024]{0:T(1024)}, f32[1024]{0:T(1024)S(1)}, u32[]{:S(2)}) copy-start(f32[1024]{0:T(1024)S(1)} %get-tuple-element.349) | copy-start | bytes 12292
  237.8 72.3 %copy-start.70 = (f32[1024]{0:T(1024)}, f32[1024]{0:T(1024)S(1)}, u32[]{:S(2)}) copy-start(f32[1024]{0:T(1024)S(1)} %get-tuple-element.414) | copy-start | bytes 12292
  240.5 24.6 copy-start.11
  240.5 24.6 copy-start.49
  240.8 24.3 copy-start.55
  252.0 13.5 copy-start.24
  310.1 18.7 copy-start.88
  310.1 18.7 copy-start.89
  314.6 14.2 copy-start.6
  314.6 14.2 copy-start.104
  314.6 5.8 collective-permute-start.3
  319.1 5.5 collective-permute-start.2
  335.3 10.8 all-to-all-start.2
  449.1 18.6 all-to-all-start.3
  452.6 773.2 %reduce-scatter.5.cloned.1.call-start = ((), (), s32[]{:S(2)}) async-start(), calls=%async_computation.7 | async-start | bytes 34603008 | tf_op jit(solution)/shard_map/reduce_scatter | solution.py:383
  518.9 2113.7 %reduce-scatter.3.cloned.1.call-start = ((), (), s32[]{:S(2)}) async-start(), calls=%async_computation.6 | async-start | bytes 69206016 | tf_op jit(solution)/shard_map/reduce_scatter | solution.py:378
  588.3 14.4 slice-start
  680.5 1963.6 %copy-start.1 = (bf16[1024,1024]{1,0:T(8,128)(2,1)S(1)}, bf16[1024,1024]{1,0:T(8,128)(2,1)}, u32[]{:S(2)}) copy-start(bf16[1024,1024]{1,0:T(8,128)(2,1)} %param.39) | copy-start | bytes 6291460
  (107 other events, 565.2 us)
Sparse Core Ops, SparseCore 0:
  519.0 706.7 reduce-scatter.4
  1228.1 1404.4 reduce-scatter.2
where the time goes:
time: 2670 us; the launch traced here: 2650 us
  waiting for transfers between devices  1990 us (75%)
  local copies, waits for them, and re-layouts  274 us (10%)
  matrix products  167 us (6%)
  blocking collectives  91.9 us (3%)
  other arithmetic  82 us (3%)
  starting transfers between devices  29.5 us (1%)
    reduce_scatter x1, waiting for transfers between devices, shards(): lax.psum_scatter(model_full, ('batch', 'seq'), scatter_dimension=0, tiled...  1400 us
    reduce_scatter x1, waiting for transfers between devices, shards(): lax.psum_scatter(jnp.concatenate(column_parts, axis=1), ('batch', 'seq'),...  545 us
    transpose x1, local copies, waits for them, and re-layouts, shards(): jnp.concatenate(block_parts, axis=2).transpose(1, 0, 2)  66.9 us
    dot_general x8, matrix products, shards(): jnp.einsum('fr,fc->rc', left_side, right_side, preferred_element_type=jnp...  59.1 us
    unnamed x257, local copies, waits for them, and re-layouts  54.7 us
  transfers between devices with their start and end apart: 10, of which 7 were waited for; matrix products, arithmetic and copies ran while one was open for 7% of the time, Pallas kernels for 0%

commit v1 on v0

--- a/solution.py
+++ b/solution.py
@@ -1,9 +1,14 @@
+import functools
 import math
 
 import jax
 import jax.numpy as jnp
 from jax import lax
+from jax.experimental import pallas as pl
+from jax.experimental.pallas import tpu as pltpu
 from jax.sharding import PartitionSpec as P
+
+MESH = pl.DeviceIdType.MESH
 
 HEADS = 16
 HD = 64
@@ -103,6 +108,154 @@
     grad_normed = times_transposed(grad_hidden, up_weight)
     grad_values, grad_gain = ln_pull(grad_normed)
     return (grad_in + grad_values, grad_gain, (lowered, grad_hidden), (act_rows, grad_branch))
+
+
+def sum_kernel(groups, batches, rows_ref, total_ref, seq_slots, part, batch_slots, sends, arrivals):
+    s, b = lax.axis_index("seq"), lax.axis_index("batch")
+    peers = [(b, lax.rem(s + k, groups)) for k in range(1, groups)]
+    peers += [(lax.rem(b + k, batches), s) for k in range(1, batches)]
+    barrier = pltpu.get_barrier_semaphore()
+    for peer in peers:
+        pl.semaphore_signal(barrier, inc=1, device_id=peer, device_id_type=MESH)
+    pl.semaphore_wait(barrier, len(peers))
+
+    def spread(source, slots, mine, first, count):
+        slots[mine] = source[...]
+        copies = []
+        for k in range(first, first + count):
+            copies.append(
+                pltpu.make_async_remote_copy(
+                    src_ref=source,
+                    dst_ref=slots.at[mine],
+                    send_sem=sends.at[k],
+                    recv_sem=arrivals.at[k],
+                    device_id=peers[k],
+                    device_id_type=MESH,
+                )
+            )
+            copies[-1].start()
+        for copy in copies:
+            copy.wait()
+        total = slots[0]
+        for i in range(1, count + 1):
+            total = total + slots[i]
+        return total
+
+    part[...] = spread(rows_ref, seq_slots, s, 0, groups - 1)
+    total_ref[...] = spread(part, batch_slots, b, groups - 1, batches - 1)
+
+
+def sum_everywhere(rows, collective_id):
+    groups, batches = lax.axis_size("seq"), lax.axis_size("batch")
+    copies = groups + batches - 2
+    return pl.pallas_call(
+        functools.partial(sum_kernel, groups, batches),
+        out_shape=jax.ShapeDtypeStruct(rows.shape, jnp.float32),
+        in_specs=[pl.BlockSpec(memory_space=pltpu.VMEM)],
+        out_specs=pl.BlockSpec(memory_space=pltpu.VMEM),
+        scratch_shapes=[
+            pltpu.VMEM((groups, *rows.shape), jnp.float32),
+            pltpu.VMEM(rows.shape, jnp.float32),
+            pltpu.VMEM((batches, *rows.shape), jnp.float32),
+            pltpu.SemaphoreType.DMA((copies,)),
+            pltpu.SemaphoreType.DMA((copies,)),
+        ],
+        compiler_params=pltpu.CompilerParams(
+            collective_id=collective_id, has_side_effects=True, vmem_limit_bytes=32 << 20
+        ),
+    )(rows)
+
+
+def halving_steps(first_seq):
+    seq_bits = [("seq", k) for k in range(lax.axis_size("seq").bit_length() - 1)]
+    batch_bits = [("batch", k) for k in range(1, lax.axis_size("batch").bit_length() - 1)]
+    if first_seq:
+        seq_bits = seq_bits[::-1]
+    return [("batch", 0)] + seq_bits + batch_bits
+
+
+def relative_place(place, steps, axis):
+    flips = 0
+    for order, (name, bit) in enumerate(steps):
+        if name == axis:
+            flips = flips | (((place >> (len(steps) - 1 - order)) & 1) << bit)
+    return flips
+
+
+def product_kernel(steps, tall, rows, cols, group, where, left_ref, right_ref, out_ref):
+    step = pl.program_id(0)
+    for inner in range(group):
+        place = step * group + inner
+        b = where[0] ^ relative_place(place, steps, "batch")
+        s = where[1] ^ relative_place(place, steps, "seq")
+        if tall:
+            left = left_ref[:, pl.ds(pl.multiple_of((b * lax.axis_size("seq") + s) * rows, rows), rows)]
+            right = right_ref[...]
+        else:
+            left = left_ref[:, pl.ds(pl.multiple_of(s * rows, rows), rows)]
+            right = right_ref[:, pl.ds(pl.multiple_of(b * cols, cols), cols)]
+        out_ref[inner] = lax.dot_general(
+            left, right, (((0,), (0,)), ((), ())), preferred_element_type=jnp.float32
+        ).astype(jnp.bfloat16)
+
+
+def block_products(left, right, tall, steps):
+    batches, groups = lax.axis_size("batch"), lax.axis_size("seq")
+    places = batches * groups
+    if tall:
+        rows, cols = left.shape[1] // places, right.shape[1]
+    else:
+        rows, cols = left.shape[1] // groups, right.shape[1] // batches
+    me = jnp.stack([lax.axis_index("batch"), lax.axis_index("seq")]).astype(jnp.int32)
+    if rows % 128 == 0 and cols % 128 == 0:
+        group = 4
+        return pl.pallas_call(
+            functools.partial(product_kernel, steps, tall, rows, cols, group),
+            out_shape=jax.ShapeDtypeStruct((places, rows, cols), jnp.bfloat16),
+            grid_spec=pltpu.PrefetchScalarGridSpec(
+                num_scalar_prefetch=1,
+                grid=(places // group,),
+                in_specs=[
+                    pl.BlockSpec(left.shape, lambda i, where: (0, 0)),
+                    pl.BlockSpec(right.shape, lambda i, where: (0, 0)),
+                ],
+                out_specs=pl.BlockSpec((group, rows, cols), lambda i, where: (i, 0, 0)),
+            ),
+            compiler_params=pltpu.CompilerParams(vmem_limit_bytes=40 << 20),
+            cost_estimate=pl.CostEstimate(
+                flops=2 * left.shape[0] * left.shape[1] * right.shape[1],
+                bytes_accessed=2 * (left.size + right.size + left.shape[1] * right.shape[1]),
+                transcendentals=0,
+            ),
+        )(me, left, right)
+    whole = lax.dot_general(
+        left, right, (((0,), (0,)), ((), ())), preferred_element_type=jnp.float32
+    ).astype(jnp.bfloat16)
+    if tall:
+        blocks = whole.reshape(batches, groups, rows, cols)
+    else:
+        blocks = whole.reshape(groups, rows, batches, cols).transpose(2, 0, 1, 3)
+    batch_bits, seq_bits = batches.bit_length() - 1, groups.bit_length() - 1
+    blocks = blocks.reshape((2,) * (batch_bits + seq_bits) + (rows, cols))
+    dims = []
+    for name, bit in steps:
+        dim = batch_bits - 1 - bit if name == "batch" else batch_bits + seq_bits - 1 - bit
+        mine = (me[0] if name == "batch" else me[1]) >> bit & 1
+        blocks = jnp.where(mine == 1, jnp.flip(blocks, dim), blocks)
+        dims.append(dim)
+    return blocks.transpose(*dims, len(dims), len(dims) + 1).reshape(places, rows, cols)
+
+
+def owned_sum(left, right, tall, first_seq):
+    steps = halving_steps(first_seq)
+    blocks = block_products(left, right, tall, steps)
+    for axis, bit in steps:
+        half = blocks.shape[0] // 2
+        pairs = [(i, i ^ (1 << bit)) for i in range(lax.axis_size(axis))]
+        arrived = lax.ppermute(blocks[half:], axis, pairs)
+        total = blocks[:half].astype(jnp.float32) + arrived.astype(jnp.float32)
+        blocks = total.astype(jnp.bfloat16) if half > 1 else total
+    return blocks[0]
 
 
 def shards(
@@ -214,7 +367,8 @@
         )
     sum_rows = jnp.sum(convolved_rows * unpadded_rows, axis=0)
     sum_squares = jnp.sum(convolved_rows * convolved_rows * unpadded_rows, axis=0)
-    total_sum, total_squares = lax.psum((sum_rows, sum_squares), ("batch", "seq"))
+    totals = sum_everywhere(jnp.stack([sum_rows, sum_squares]), 1)
+    total_sum, total_squares = totals[0], totals[1]
     count_of_frames = jnp.sum(lengths).astype(jnp.float32)
     batchnorm_frame_mean = total_sum / count_of_frames
     bn_var = total_squares / count_of_frames - batchnorm_frame_mean * batchnorm_frame_mean
@@ -240,13 +394,16 @@
         * bn_sig
         * (1.0 + batchnorm_input_rows * (1.0 - bn_sig))
     )
-    gradient_sum_total, gradient_normalized_sum = lax.psum(
-        (
-            jnp.sum(batchnorm_gradient, axis=0),
-            jnp.sum(batchnorm_gradient * normalized_rows, axis=0),
+    gradient_totals = sum_everywhere(
+        jnp.stack(
+            [
+                jnp.sum(batchnorm_gradient, axis=0),
+                jnp.sum(batchnorm_gradient * normalized_rows, axis=0),
+            ]
         ),
-        ("batch", "seq"),
-    )
+        2,
+    )
+    gradient_sum_total, gradient_normalized_sum = gradient_totals[0], gradient_totals[1]
     grad_conv = (
         batchnorm_scale_factor
         * batchnorm_inverse_deviation
@@ -355,60 +512,28 @@
         [grad_gain_zero, grad_gain_one, grad_gain_two, grad_gain_three, grad_gain_four], axis=0
     )
     small_rows = jnp.concatenate([gain_grads, cond_grad_rows, kernel_grads], axis=0)
-    small_cols = jnp.pad(small_rows, ((0, 128 - small_rows.shape[0]), (0, 0))).T
-    model_pairs = [
-        ffn1_up_pair,
-        (attn_in, grad_qkv),
-        (attn_out, grad_r),
-        (conv_in, grad_gl),
-        (conv_act, grad_r2),
-        ffn2_up_pair,
-    ]
-    hidden_pairs = [ffn1_down_pair, ffn2_down_pair]
-    block_parts = [
-        jnp.einsum("fr,fc->rc", left_side, right_side, preferred_element_type=jnp.float32).reshape(
-            model_width, batches, -1
-        )
-        for left_side, right_side in model_pairs
-    ]
-    block_parts.append(jnp.broadcast_to(small_cols[:, None, :], (model_width, batches, 128)))
-    model_full = (
-        jnp.concatenate(block_parts, axis=2).transpose(1, 0, 2).reshape(batches * model_width, -1)
-    )
-    model_grad = lax.psum_scatter(model_full, ("batch", "seq"), scatter_dimension=0, tiled=True)
-    column_parts = [
-        jnp.einsum("fr,fc->rc", left_side, right_side, preferred_element_type=jnp.float32)
-        for left_side, right_side in hidden_pairs
-    ]
-    hidden_grad = lax.psum_scatter(
-        jnp.concatenate(column_parts, axis=1), ("batch", "seq"), scatter_dimension=0, tiled=True
-    )
-    edge_one = ff_width // batches
-    edge_two = edge_one + 3 * model_width // batches
-    edge_three = edge_two + model_width // batches
-    edge_four = edge_three + 2 * model_width // batches
-    edge_five = edge_four + model_width // batches
-    edge_six = edge_five + ff_width // batches
-    small_piece = model_grad[:, edge_six : edge_six + 128]
+    small_sums = sum_everywhere(small_rows, 3)
+    seq_width = model_width // groups
+    small_piece = lax.dynamic_slice_in_dim(small_sums, seq_index * seq_width, seq_width, axis=1)
     cond_end = 5 + level_count + 1
     new_mean = 0.9 * running_mean + 0.1 * batchnorm_frame_mean
     new_var = 0.9 * running_var + 0.1 * bn_var * count_of_frames / (count_of_frames - 1.0)
     return (
         out_rows[None],
         grad_zero.astype(jnp.bfloat16)[None],
-        small_piece[:, 5:cond_end].T,
-        small_piece[:, 0:5].T,
-        model_grad[:, 0:edge_one],
-        hidden_grad[:, 0:model_width],
-        model_grad[:, edge_one:edge_two],
-        model_grad[:, edge_two:edge_three],
-        model_grad[:, edge_three:edge_four],
-        small_piece[:, cond_end : cond_end + taps].T,
+        small_piece[5:cond_end],
+        small_piece[0:5],
+        owned_sum(*ffn1_up_pair, False, False),
+        owned_sum(*ffn1_down_pair, True, True),
+        owned_sum(attn_in, grad_qkv, False, True),
+        owned_sum(attn_out, grad_r, False, False),
+        owned_sum(conv_in, grad_gl, False, True),
+        small_piece[cond_end : cond_end + taps],
         gradient_normalized_sum,
         gradient_sum_total,
-        model_grad[:, edge_four:edge_five],
-        model_grad[:, edge_five:edge_six],
-        hidden_grad[:, model_width : 2 * model_width],
+        owned_sum(conv_act, grad_r2, False, False),
+        owned_sum(*ffn2_up_pair, False, False),
+        owned_sum(*ffn2_down_pair, True, True),
         new_mean,
         new_var,
     )

time: 2670 us -> 858 us (0.32)
  waiting for transfers between devices: 1990 us -> 276 us
  blocking collectives: 91.9 us -> 0 us
  local copies, waits for them, and re-layouts: 274 us -> 190 us
  Pallas kernels: 0 us -> 77.6 us
  matrix products: 167 us -> 110 us
  starting transfers between devices: 29.5 us -> 73.1 us
  other arithmetic: 82 us -> 113 us
    reduce_scatter x2 -> x0, waiting for transfers between devices: 1950 us -> none  [the longest x1 1400 us: shards(): lax.psum_scatter(model_full, ('batch', 'seq'), scatter_dimension=0, tiled...]
    ppermute x0 -> x40, waiting for transfers between devices: none -> 246 us  [owned_sum(): arrived = lax.ppermute(blocks[half:], axis, pairs)]
    psum x2 -> x0, blocking collectives: 91.9 us -> none  [the longest x1 50.3 us: shards(): lax.psum((sum_rows, sum_squares), ('batch', 'seq'))]
    pallas_call x0 -> x11, Pallas kernels: none -> 77.6 us  [the longest x3 42.8 us: sum_everywhere(): pl.pallas_call(functools.partial(sum_kernel, groups, batches), out_shape=...]
    transpose x4 -> x0, local copies, waits for them, and re-layouts: 69 us -> none  [the longest x1 66.9 us: shards(): jnp.concatenate(block_parts, axis=2).transpose(1, 0, 2)]
    dot_general x8 -> x0, matrix products: 59.1 us -> none  [shards(): jnp.einsum('fr,fc->rc', left_side, right_side, preferred_element_type=jnp...]
    convert_element_type x0 -> x41, other arithmetic: none -> 47.7 us  [the longest x32 43.2 us: owned_sum(): blocks = total.astype(jnp.bfloat16) if half > 1 else total]
    ppermute x0 -> x40, starting transfers between devices: none -> 43.7 us  [owned_sum(): arrived = lax.ppermute(blocks[half:], axis, pairs)]
  transfers between devices with their start and end apart: 10 -> 48, of which waited for: 7 -> 21; matrix products, arithmetic and copies ran while one was open for 7% -> 27% of each run, Pallas kernels for 0% -> 6%
where the time goes in v1:
time: 858 us; the launch traced here: 846 us
  waiting for transfers between devices  276 us (32%)
  local copies, waits for them, and re-layouts  190 us (22%)
  other arithmetic  113 us (13%)
  matrix products  110 us (13%)
  Pallas kernels  77.6 us (9%)
  starting transfers between devices  73.1 us (9%)
    ppermute x40, waiting for transfers between devices, owned_sum(): arrived = lax.ppermute(blocks[half:], axis, pairs)  246 us
    ppermute x40, starting transfers between devices, owned_sum(): arrived = lax.ppermute(blocks[half:], axis, pairs)  43.7 us
    convert_element_type x32, other arithmetic, owned_sum(): blocks = total.astype(jnp.bfloat16) if half > 1 else total  43.2 us
    pallas_call x3, Pallas kernels, sum_everywhere(): pl.pallas_call(functools.partial(sum_kernel, groups, batches), out_shape=...  42.8 us
    dot_general x8, matrix products, times_transposed(): lax.dot_general(left_side, weight, (((1,), (1,)), ((), ())), preferred_el...  42.5 us
    unnamed x233, local copies, waits for them, and re-layouts  39 us
    pallas_call x8, Pallas kernels, block_products(): pl.pallas_call(functools.partial(product_kernel, steps, tall, rows, cols,...  34.8 us
    slice x40, local copies, waits for them, and re-layouts, owned_sum(): arrived = lax.ppermute(blocks[half:], axis, pairs)  25.6 us
  transfers between devices with their start and end apart: 48, of which 21 were waited for; matrix products, arithmetic and copies ran while one was open for 27% of the time, Pallas kernels for 6%

profile of v1, /device:TPU:0, one launch (start us, length us, event | category | flops | bytes accessed | tf_op | source)
XLA Modules:
  0.0 845.7 jit_solution(8699640440708615543)
XLA Ops:
  9.7 9.0 %multiply_convert_fusion.2 = (bf16[256,4096]{1,0:T(8,128)(2,1)S(1)}, f32[256,4096]{1,0:T(8,128)}) fusion(bf16[256,1024]{1,0:T(8,128)(2,1)S(1)} %multiply_convert_fusion.14.left_ref, bf16[1024,4096]{1,0:T(8,128)(2,1)} %param.31), kind=kOutput, calls=%fused_computation.65 | convolution fusion | flops 2152726528 | bytes 15204352 | tf_op jit(solution)/shard_map/dot_general | solution.py:96
  30.4 7.5 copy.86
  37.8 8.6 %convert_element_type.570 = bf16[128,2,4,768]{3,2,1,0:T(4,128)(2,1)} reshape(bf16[256,16,3,64]{3,2,1,0:T(4,128)(2,1)} %copy.86) | data formatting | bytes 3145728 | tf_op jit(solution)/shard_map/convert_element_type | solution.py:316
  56.3 19.3 %all-to-all-done = bf16[128,4,1536]{0,2,1:T(8,128)(2,1)} async-done(((bf16[128,4,1536]{0,2,1:T(8,128)(2,1)}), bf16[128,4,1536]{0,2,1:T(8,128)(2,1)}, u32[]{:S(2)}, u32[]{:S(2)}) %all-to-all-start) | async-done | bytes 1572896 | tf_op jit(solution)/shard_map/all_to_all | solution.py:317
  78.3 9.0 %reshape.470 = bf16[1024,4,3,64]{3,2,1,0:T(4,128)(2,1)} reshape(bf16[4,128,1,1536]{3,1,0,2:T(8,128)(2,1)} %copy.88) | data formatting | bytes 3145728 | tf_op jit(solution)/shard_map/reshape | solution.py:324
  87.2 10.8 %fusion.90 = (bf16[1024,4,1,64]{3,2,1,0:T(2,128)(2,1)}, bf16[1024,4,1,64]{3,2,1,0:T(2,128)(2,1)}, bf16[1024,4,1,64]{3,2,1,0:T(2,128)(2,1)S(1)}) fusion(bf16[1024,4,3,64]{3,2,1,0:T(4,128)(2,1)} %reshape.470), kind=kLoop, calls=%fused_computation.274 | loop fusion | bytes 3145728 | tf_op jit(solution)/shard_map/slice | solution.py:327
  111.1 13.4 %while.28 = (s32[]{:T(128)}, bf16[2,512,4,64]{1,3,2,0:T(8,128)(2,1)}, f32[2,4,512]{2,1,0:T(4,128)S(1)}, bf16[2,512,4,64]{1,3,2,0:T(8,128)(2,1)S(1)}, bf16[1024,4...) while((s32[]{:T(128)}, bf16[2,512,4,64]{1,3,2,0:T(8,128)(2,1)}, ...), condition=%wide.region_8.9_spmd.clone, body=%wide.region_5.8_spmd.clone.sunk | while | flops 555875328 | bytes 28906108 | solution.py:347
  179.4 11.1 %shard_map.323 = f32[2,1024]{1,0:T(2,128)S(1)} custom-call(f32[2,1024]{1,0:T(2,128)S(1)} %pad_maximum_fusion.7.rows_ref), custom_call_target="tpu_custom_call" | custom-call | tf_op jit(solution)/shard_map/pallas_call | solution.py:151
  209.7 9.3 %fusion.45.right_ref = bf16[256,4096]{1,0:T(8,128)(2,1)S(1)} fusion(bf16[256,1024]{1,0:T(8,128)(2,1)S(1)} %multiply_convert_fusion.7.right_ref, bf16[4096,1024]{1,0:T(8,128)(2,1)} %param.41, f32[256,4096]{1,0:T(8,128)S(1)} %get-tuple-element.350), kind=kOutput, calls=%fused_computation.57 | convolution fusion | flops 2156920832 | bytes 15204352 | tf_op jit(solution)/shard_map/dot_general | solution.py:76
  223.4 10.5 %multiply_reduce_fusion.2 = (f32[1024]{0:T(1024)}, f32[256]{0:T(256)S(1)}, f32[256,1024]{1,0:T(8,128)}) fusion(f32[256,1024]{1,0:T(8,128)S(1)} %get-tuple-element.348, f32[256]{0:T(256)S(1)} %fusion.80, f32[256]{0:T(256)S(1)} %broadcast_multiply_fusion.3, f32[1024]{0:T(1024)S(1)} %bitcast.345, bf16[256,4096]{1,0:T(8,128)(2,1)S(1)} %fusion.45.right_ref, ...), kind=kOutput, calls=%fused_computation.130 | convolution fusion | flops 2149317376 | bytes 12594176 | tf_op jit(solution)/shard_map/dot_general | solution.py:76
  238.3 9.2 %shard_map.324 = f32[2,1024]{1,0:T(2,128)S(1)} custom-call(f32[2,1024]{1,0:T(2,128)S(1)} %pad_maximum_fusion.8.rows_ref), custom_call_target="tpu_custom_call" | custom-call | tf_op jit(solution)/shard_map/pallas_call | solution.py:151
  292.0 64.1 %while.29 = (s32[]{:T(128)}, f32[1024,4,64]{0,2,1:T(8,128)}, f32[1024,4,64]{0,2,1:T(8,128)}, f32[2,512,4,64]{1,0,3,2:T(2,128)}, bf16[2,512,4,64]{1,3,2,0:T(8,128...) while((s32[]{:T(128)}, f32[1024,4,64]{0,2,1:T(8,128)}, ...), condition=%wide.region_28.29_spmd.clone, body=%wide.region_26.28_spmd.clone.sunk | while | flops 1368390656 | bytes 156300144 | solution.py:476
  305.4 10.4 %dynamic_update_slice.22 = f32[2,512,4,64]{1,0,3,2:T(2,128)} dynamic-update-slice(f32[2,512,4,64]{1,0,3,2:T(2,128)} %get-tuple-element.514, f32[1,512,4,64]{1,0,3,2:T(1,128)S(1)} %copy.185, s32[]{:T(128)} %get-tuple-element.511, s32[]{:T(128)} %constant.90.clone.1..sunk, s32[]{:T(128)} %constant.90.clone.1..sunk, s32[]{:T(128)} %constant.90.clone.1..sunk) | dynamic-update-slice | bytes 1048580 | tf_op jit(solution)/shard_map/while/body/jit(dynamic_update_index_in_dim)/dynamic_update_slice | solution.py:476
  336.9 10.4 %dynamic_update_slice.22 = f32[2,512,4,64]{1,0,3,2:T(2,128)} dynamic-update-slice(f32[2,512,4,64]{1,0,3,2:T(2,128)} %get-tuple-element.514, f32[1,512,4,64]{1,0,3,2:T(1,128)S(1)} %copy.185, s32[]{:T(128)} %get-tuple-element.511, s32[]{:T(128)} %constant.90.clone.1..sunk, s32[]{:T(128)} %constant.90.clone.1..sunk, s32[]{:T(128)} %constant.90.clone.1..sunk) | dynamic-update-slice | bytes 1048580 | tf_op jit(solution)/shard_map/while/body/jit(dynamic_update_index_in_dim)/dynamic_update_slice | solution.py:476
  366.8 14.4 %convert_element_type.724 = bf16[512,1,1536]{2,1,0:T(2,128)(2,1)} reshape(bf16[1024,4,3,64]{3,2,1,0:T(4,128)(2,1)} %copy.101) | data formatting | bytes 3145728 | tf_op jit(solution)/shard_map/convert_element_type | solution.py:487
  381.2 12.4 %reduce.15 = bf16[512,1536]{1,0:T(8,128)(2,1)} reduce(bf16[512,1,1536]{2,1,0:T(2,128)(2,1)} %convert_element_type.724, bf16[]{:T(256)} %broadcast.414), dimensions={1}, to_apply=%convert_element_type.724.reduce_sub_computation | reduce | bytes 3145730 | tf_op jit(solution)/shard_map/convert_element_type | solution.py:487
  413.5 20.7 %collective-permute-done.30 = bf16[8,256,128]{2,1,0:T(8,128)(2,1)S(1)} collective-permute-done((bf16[8,256,128]{2,1,0:T(8,128)(2,1)S(1)}, bf16[8,256,128]{2,1,0:T(8,128)(2,1)S(1)}, u32[]{:S(2)}, u32[]{:S(2)}) %collective-permute-start.30) | collective-permute-done | bytes 524320 | tf_op jit(solution)/shard_map/ppermute | solution.py:255
  436.6 7.7 collective-permute-done.20
  467.5 6.3 multiply_reduce_fusion.4
  489.0 6.4 fusion.44.right_ref
  495.5 16.7 %collective-permute-done.25 = bf16[8,256,256]{2,1,0:T(8,128)(2,1)S(1)} collective-permute-done((bf16[8,256,256]{2,1,0:T(8,128)(2,1)S(1)}, bf16[8,256,256]{2,1,0:T(8,128)(2,1)S(1)}, u32[]{:S(2)}, u32[]{:S(2)}) %collective-permute-start.25) | collective-permute-done | bytes 1048608 | tf_op jit(solution)/shard_map/ppermute | solution.py:255
  520.2 6.7 collective-permute-done.26
  551.2 22.5 %shard_map.325 = f32[23,1024]{1,0:T(8,128)S(1)} custom-call(f32[23,1024]{1,0:T(8,128)S(1)} %concatenate.74.rows_ref), custom_call_target="tpu_custom_call" | custom-call | tf_op jit(solution)/shard_map/pallas_call | solution.py:151
  596.5 6.1 add_convert_fusion.1
  606.7 6.7 add_convert_fusion.2
  619.5 52.4 %collective-permute-done.15 = bf16[8,256,384]{2,1,0:T(8,128)(2,1)} collective-permute-done((bf16[8,256,384]{2,1,0:T(8,128)(2,1)S(1)}, bf16[8,256,384]{2,1,0:T(8,128)(2,1)}, u32[]{:S(2)}, u32[]{:S(2)}) %collective-permute-start.15) | collective-permute-done | bytes 1572896 | tf_op jit(solution)/shard_map/ppermute | solution.py:255
  681.8 58.9 %collective-permute-done.16 = bf16[4,256,384]{2,1,0:T(8,128)(2,1)S(1)} collective-permute-done((bf16[4,256,384]{2,1,0:T(8,128)(2,1)S(1)}, bf16[4,256,384]{2,1,0:T(8,128)(2,1)S(1)}, u32[]{:S(2)}, u32[]{:S(2)}) %collective-permute-start.16) | collective-permute-done | bytes 786464 | tf_op jit(solution)/shard_map/ppermute | solution.py:255
  746.7 13.6 %collective-permute-done.41 = bf16[4,128,1024]{2,1,0:T(8,128)(2,1)S(1)} collective-permute-done((bf16[4,128,1024]{2,1,0:T(8,128)(2,1)S(1)}, bf16[4,128,1024]{2,1,0:T(8,128)(2,1)S(1)}, u32[]{:S(2)}, u32[]{:S(2)}) %collective-permute-start.41) | collective-permute-done | bytes 1048608 | tf_op jit(solution)/shard_map/ppermute | solution.py:255
  770.7 10.8 %collective-permute-done.18 = bf16[1,256,384]{2,1,0:T(8,128)(2,1)S(1)} collective-permute-done((bf16[1,256,384]{2,1,0:T(8,128)(2,1)S(1)}, bf16[1,256,384]{2,1,0:T(8,128)(2,1)S(1)}, u32[]{:S(2)}, u32[]{:S(2)}) %collective-permute-start.18) | collective-permute-done | bytes 196640 | tf_op jit(solution)/shard_map/ppermute | solution.py:255
  800.0 15.7 %collective-permute-done.12 = bf16[2,128,1024]{2,1,0:T(8,128)(2,1)S(1)} collective-permute-done((bf16[2,128,1024]{2,1,0:T(8,128)(2,1)S(1)}, bf16[2,128,1024]{2,1,0:T(8,128)(2,1)S(1)}, u32[]{:S(2)}, u32[]{:S(2)}) %collective-permute-start.12) | collective-permute-done | bytes 524320 | tf_op jit(solution)/shard_map/ppermute | solution.py:255
  816.0 12.7 %collective-permute-done.7 = bf16[2,256,512]{2,1,0:T(8,128)(2,1)S(1)} collective-permute-done((bf16[2,256,512]{2,1,0:T(8,128)(2,1)S(1)}, bf16[2,256,512]{2,1,0:T(8,128)(2,1)S(1)}, u32[]{:S(2)}, u32[]{:S(2)}) %collective-permute-start.7) | collective-permute-done | bytes 524320 | tf_op jit(solution)/shard_map/ppermute | solution.py:255
  830.9 10.1 %collective-permute-done.13 = bf16[1,128,1024]{2,1,0:T(8,128)(2,1)S(1)} collective-permute-done((bf16[1,128,1024]{2,1,0:T(8,128)(2,1)S(1)}, bf16[1,128,1024]{2,1,0:T(8,128)(2,1)S(1)}, u32[]{:S(2)}, u32[]{:S(2)}) %collective-permute-start.13) | collective-permute-done | bytes 262176 | tf_op jit(solution)/shard_map/ppermute | solution.py:255
  (599 shorter events, 415.0 us)
Async XLA Ops:
  50.3 25.3 %all-to-all-start = ((bf16[128,4,1536]{0,2,1:T(8,128)(2,1)}), bf16[128,4,1536]{0,2,1:T(8,128)(2,1)}, u32[]{:S(2)}, u32[]{:S(2)}) async-start(bf16[128,4,1536]{0,2,1:T(8,128)(2,1)} %bitcast.292), calls=%async_computation | async-start | bytes 3145728 | tf_op jit(solution)/shard_map/all_to_all | solution.py:317
  261.6 314.3 %collective-permute-start.39 = (bf16[16,128,1024]{2,1,0:T(8,128)(2,1)}, bf16[16,128,1024]{2,1,0:T(8,128)(2,1)}, u32[]{:S(2)}, u32[]{:S(2)}) collective-permute-start(bf16[16,128,1024]{2,1,0:T(8,128)(2,1)} %slice.635), channel_id=1, source_target_pairs={{0,4},{4,0},{8,12},{12,8},{16,20},{20,16},{24,28},{28,24},{1,5},{5... | collective-permute-start | bytes 12582920 | tf_op jit(solution)/shard_map/ppermute | solution.py:255
  264.0 331.4 %collective-permute-start.34 = (bf16[16,256,512]{2,1,0:T(8,128)(2,1)}, bf16[16,256,512]{2,1,0:T(8,128)(2,1)}, u32[]{:S(2)}, u32[]{:S(2)}) collective-permute-start(bf16[16,256,512]{2,1,0:T(8,128)(2,1)} %slice.625), channel_id=1, source_target_pairs={{0,4},{4,0},{8,12},{12,8},{16,20},{20,16},{24,28},{28,24},{1,5},{5... | collective-permute-start | bytes 12582920 | tf_op jit(solution)/shard_map/ppermute | solution.py:255
  265.6 136.9 %collective-permute-start.29 = (bf16[16,256,128]{2,1,0:T(8,128)(2,1)}, bf16[16,256,128]{2,1,0:T(8,128)(2,1)}, u32[]{:S(2)}, u32[]{:S(2)}) collective-permute-start(bf16[16,256,128]{2,1,0:T(8,128)(2,1)} %slice.615), channel_id=1, source_target_pairs={{0,4},{4,0},{8,12},{12,8},{16,20},{20,16},{24,28},{28,24},{1,5},{5... | collective-permute-start | bytes 3145736 | tf_op jit(solution)/shard_map/ppermute | solution.py:255
  284.6 121.7 %collective-permute-start.19 = (bf16[16,256,128]{2,1,0:T(8,128)(2,1)}, bf16[16,256,128]{2,1,0:T(8,128)(2,1)}, u32[]{:S(2)}, u32[]{:S(2)}) collective-permute-start(bf16[16,256,128]{2,1,0:T(8,128)(2,1)} %slice.595), channel_id=1, source_target_pairs={{0,4},{4,0},{8,12},{12,8},{16,20},{20,16},{24,28},{28,24},{1,5},{5... | collective-permute-start | bytes 3145736 | tf_op jit(solution)/shard_map/ppermute | solution.py:255
  397.9 48.8 %all-to-all-start.3 = ((bf16[4,2,98304]{2,1,0:T(2,128)(2,1)}), bf16[4,2,98304]{2,1,0:T(2,128)(2,1)}, u32[]{:S(2)}, u32[]{:S(2)}) async-start(bf16[4,2,98304]{2,1,0:T(2,128)(2,1)} %reshape.510), calls=%async_computation.3 | async-start | bytes 3145728 | tf_op jit(solution)/shard_map/all_to_all | solution.py:490
  404.2 30.0 %collective-permute-start.30 = (bf16[8,256,128]{2,1,0:T(8,128)(2,1)S(1)}, bf16[8,256,128]{2,1,0:T(8,128)(2,1)S(1)}, u32[]{:S(2)}, u32[]{:S(2)}) collective-permute-start(bf16[8,256,128]{2,1,0:T(8,128)(2,1)S(1)} %slice.617), channel_id=1, source_target_pairs={{0,1},{1,0},{2,3},{3,2},{4,5},{5,4},{6,7},{7,6},{8,9},{9,8},{10,11... | collective-permute-start | bytes 1572872 | tf_op jit(solution)/shard_map/ppermute | solution.py:255
  407.8 36.5 %collective-permute-start.20 = (bf16[8,256,128]{2,1,0:T(8,128)(2,1)S(1)}, bf16[8,256,128]{2,1,0:T(8,128)(2,1)S(1)}, u32[]{:S(2)}, u32[]{:S(2)}) collective-permute-start(bf16[8,256,128]{2,1,0:T(8,128)(2,1)S(1)} %slice.597), channel_id=1, source_target_pairs={{0,1},{1,0},{2,3},{3,2},{4,5},{5,4},{6,7},{7,6},{8,9},{9,8},{10,11... | collective-permute-start | bytes 1572872 | tf_op jit(solution)/shard_map/ppermute | solution.py:255
  413.5 72.4 %collective-permute-start.24 = (bf16[16,256,256]{2,1,0:T(8,128)(2,1)}, bf16[16,256,256]{2,1,0:T(8,128)(2,1)}, u32[]{:S(2)}, u32[]{:S(2)}) collective-permute-start(bf16[16,256,256]{2,1,0:T(8,128)(2,1)} %slice.605), channel_id=1, source_target_pairs={{0,4},{4,0},{8,12},{12,8},{16,20},{20,16},{24,28},{28,24},{1,5},{5... | collective-permute-start | bytes 6291464 | tf_op jit(solution)/shard_map/ppermute | solution.py:255
  435.1 77.4 %collective-permute-start.31 = (bf16[4,256,128]{2,1,0:T(8,128)(2,1)}, bf16[4,256,128]{2,1,0:T(8,128)(2,1)S(1)}, u32[]{:S(2)}, u32[]{:S(2)}) collective-permute-start(bf16[4,256,128]{2,1,0:T(8,128)(2,1)} %slice.619), channel_id=1, source_target_pairs={{0,2},{1,3},{2,0},{3,1},{4,6},{5,7},{6,4},{7,5},{8,10},{9,11},{10,... | collective-permute-start | bytes 786440 | tf_op jit(solution)/shard_map/ppermute | solution.py:255
  445.2 67.9 %collective-permute-start.21 = (bf16[4,256,128]{2,1,0:T(8,128)(2,1)}, bf16[4,256,128]{2,1,0:T(8,128)(2,1)}, u32[]{:S(2)}, u32[]{:S(2)}) collective-permute-start(bf16[4,256,128]{2,1,0:T(8,128)(2,1)} %slice.599), channel_id=1, source_target_pairs={{0,2},{1,3},{2,0},{3,1},{4,6},{5,7},{6,4},{7,5},{8,10},{9,11},{10,... | collective-permute-start | bytes 786440 | tf_op jit(solution)/shard_map/ppermute | solution.py:255
  488.4 23.8 %collective-permute-start.25 = (bf16[8,256,256]{2,1,0:T(8,128)(2,1)S(1)}, bf16[8,256,256]{2,1,0:T(8,128)(2,1)S(1)}, u32[]{:S(2)}, u32[]{:S(2)}) collective-permute-start(bf16[8,256,256]{2,1,0:T(8,128)(2,1)S(1)} %slice.607), channel_id=1, source_target_pairs={{0,2},{1,3},{2,0},{3,1},{4,6},{5,7},{6,4},{7,5},{8,10},{9,11},{10,... | collective-permute-start | bytes 3145736 | tf_op jit(solution)/shard_map/ppermute | solution.py:255
  512.2 78.5 %collective-permute-start.14 = (bf16[16,256,384]{2,1,0:T(8,128)(2,1)}, bf16[16,256,384]{2,1,0:T(8,128)(2,1)}, u32[]{:S(2)}, u32[]{:S(2)}) collective-permute-start(bf16[16,256,384]{2,1,0:T(8,128)(2,1)} %slice.585), channel_id=1, source_target_pairs={{0,4},{4,0},{8,12},{12,8},{16,20},{20,16},{24,28},{28,24},{1,5},{5... | collective-permute-start | bytes 9437192 | tf_op jit(solution)/shard_map/ppermute | solution.py:255
  529.5 76.4 %collective-permute-start.9 = (bf16[16,128,1024]{2,1,0:T(8,128)(2,1)}, bf16[16,128,1024]{2,1,0:T(8,128)(2,1)}, u32[]{:S(2)}, u32[]{:S(2)}) collective-permute-start(bf16[16,128,1024]{2,1,0:T(8,128)(2,1)} %slice.575), channel_id=1, source_target_pairs={{0,4},{4,0},{8,12},{12,8},{16,20},{20,16},{24,28},{28,24},{1,5},{5... | collective-permute-start | bytes 12582920 | tf_op jit(solution)/shard_map/ppermute | solution.py:255
  548.8 66.4 %collective-permute-start.4 = (bf16[16,256,512]{2,1,0:T(8,128)(2,1)}, bf16[16,256,512]{2,1,0:T(8,128)(2,1)}, u32[]{:S(2)}, u32[]{:S(2)}) collective-permute-start(bf16[16,256,512]{2,1,0:T(8,128)(2,1)} %slice.565), channel_id=1, source_target_pairs={{0,4},{4,0},{8,12},{12,8},{16,20},{20,16},{24,28},{28,24},{1,5},{5... | collective-permute-start | bytes 12582920 | tf_op jit(solution)/shard_map/ppermute | solution.py:255
  575.9 99.2 %collective-permute-start.23 = (bf16[1,256,128]{2,1,0:T(8,128)(2,1)S(1)}, bf16[1,256,128]{2,1,0:T(8,128)(2,1)S(1)}, u32[]{:S(2)}, u32[]{:S(2)}) collective-permute-start(bf16[1,256,128]{2,1,0:T(8,128)(2,1)S(1)} %slice.603), channel_id=1, source_target_pairs={{0,16},{4,20},{8,24},{12,28},{16,0},{20,4},{24,8},{28,12},{1,17},{... | collective-permute-start | bytes 196616 | tf_op jit(solution)/shard_map/ppermute | solution.py:255
  590.6 85.0 %collective-permute-start.40 = (bf16[8,128,1024]{2,1,0:T(8,128)(2,1)}, bf16[8,128,1024]{2,1,0:T(8,128)(2,1)}, u32[]{:S(2)}, u32[]{:S(2)}) collective-permute-start(bf16[8,128,1024]{2,1,0:T(8,128)(2,1)} %slice.637), channel_id=1, source_target_pairs={{0,2},{1,3},{2,0},{3,1},{4,6},{5,7},{6,4},{7,5},{8,10},{9,11},{10,... | collective-permute-start | bytes 6291464 | tf_op jit(solution)/shard_map/ppermute | solution.py:255
  595.4 76.5 %collective-permute-start.15 = (bf16[8,256,384]{2,1,0:T(8,128)(2,1)S(1)}, bf16[8,256,384]{2,1,0:T(8,128)(2,1)}, u32[]{:S(2)}, u32[]{:S(2)}) collective-permute-start(bf16[8,256,384]{2,1,0:T(8,128)(2,1)S(1)} %slice.587), channel_id=1, source_target_pairs={{0,2},{1,3},{2,0},{3,1},{4,6},{5,7},{6,4},{7,5},{8,10},{9,11},{10,... | collective-permute-start | bytes 4718600 | tf_op jit(solution)/shard_map/ppermute | solution.py:255
  605.9 137.7 %collective-permute-start.35 = (bf16[8,256,512]{2,1,0:T(8,128)(2,1)}, bf16[8,256,512]{2,1,0:T(8,128)(2,1)}, u32[]{:S(2)}, u32[]{:S(2)}) collective-permute-start(bf16[8,256,512]{2,1,0:T(8,128)(2,1)} %slice.627), channel_id=1, source_target_pairs={{0,1},{1,0},{2,3},{3,2},{4,5},{5,4},{6,7},{7,6},{8,9},{9,8},{10,11... | collective-permute-start | bytes 6291464 | tf_op jit(solution)/shard_map/ppermute | solution.py:255
  615.2 64.7 %collective-permute-start.28 = (bf16[1,256,256]{2,1,0:T(8,128)(2,1)S(1)}, bf16[1,256,256]{2,1,0:T(8,128)(2,1)S(1)}, u32[]{:S(2)}, u32[]{:S(2)}) collective-permute-start(bf16[1,256,256]{2,1,0:T(8,128)(2,1)S(1)} %slice.613), channel_id=1, source_target_pairs={{0,16},{4,20},{8,24},{12,28},{16,0},{20,4},{24,8},{28,12},{1,17},{... | collective-permute-start | bytes 393224 | tf_op jit(solution)/shard_map/ppermute | solution.py:255
  671.9 94.1 %collective-permute-start.10 = (bf16[8,128,1024]{2,1,0:T(8,128)(2,1)S(1)}, bf16[8,128,1024]{2,1,0:T(8,128)(2,1)S(1)}, u32[]{:S(2)}, u32[]{:S(2)}) collective-permute-start(bf16[8,128,1024]{2,1,0:T(8,128)(2,1)S(1)} %slice.577), channel_id=1, source_target_pairs={{0,2},{1,3},{2,0},{3,1},{4,6},{5,7},{6,4},{7,5},{8,10},{9,11},{10,... | collective-permute-start | bytes 6291464 | tf_op jit(solution)/shard_map/ppermute | solution.py:255
  675.1 93.3 %collective-permute-start.5 = (bf16[8,256,512]{2,1,0:T(8,128)(2,1)S(1)}, bf16[8,256,512]{2,1,0:T(8,128)(2,1)S(1)}, u32[]{:S(2)}, u32[]{:S(2)}) collective-permute-start(bf16[8,256,512]{2,1,0:T(8,128)(2,1)S(1)} %slice.567), channel_id=1, source_target_pairs={{0,1},{1,0},{2,3},{3,2},{4,5},{5,4},{6,7},{7,6},{8,9},{9,8},{10,11... | collective-permute-start | bytes 6291464 | tf_op jit(solution)/shard_map/ppermute | solution.py:255
  675.6 65.0 %collective-permute-start.16 = (bf16[4,256,384]{2,1,0:T(8,128)(2,1)S(1)}, bf16[4,256,384]{2,1,0:T(8,128)(2,1)S(1)}, u32[]{:S(2)}, u32[]{:S(2)}) collective-permute-start(bf16[4,256,384]{2,1,0:T(8,128)(2,1)S(1)} %slice.589), channel_id=1, source_target_pairs={{0,1},{1,0},{2,3},{3,2},{4,5},{5,4},{6,7},{7,6},{8,9},{9,8},{10,11... | collective-permute-start | bytes 2359304 | tf_op jit(solution)/shard_map/ppermute | solution.py:255
  679.9 80.4 %collective-permute-start.41 = (bf16[4,128,1024]{2,1,0:T(8,128)(2,1)S(1)}, bf16[4,128,1024]{2,1,0:T(8,128)(2,1)S(1)}, u32[]{:S(2)}, u32[]{:S(2)}) collective-permute-start(bf16[4,128,1024]{2,1,0:T(8,128)(2,1)S(1)} %slice.639), channel_id=1, source_target_pairs={{0,1},{1,0},{2,3},{3,2},{4,5},{5,4},{6,7},{7,6},{8,9},{9,8},{10,11... | collective-permute-start | bytes 3145736 | tf_op jit(solution)/shard_map/ppermute | solution.py:255
  741.1 23.9 %collective-permute-start.17 = (bf16[2,256,384]{2,1,0:T(8,128)(2,1)S(1)}, bf16[2,256,384]{2,1,0:T(8,128)(2,1)S(1)}, u32[]{:S(2)}, u32[]{:S(2)}) collective-permute-start(bf16[2,256,384]{2,1,0:T(8,128)(2,1)S(1)} %slice.591), channel_id=1, source_target_pairs={{0,8},{4,12},{8,0},{12,4},{16,24},{20,28},{24,16},{28,20},{1,9},{5... | collective-permute-start | bytes 1179656 | tf_op jit(solution)/shard_map/ppermute | solution.py:255
  745.9 24.4 %collective-permute-start.36 = (bf16[4,256,512]{2,1,0:T(8,128)(2,1)S(1)}, bf16[4,256,512]{2,1,0:T(8,128)(2,1)S(1)}, u32[]{:S(2)}, u32[]{:S(2)}) collective-permute-start(bf16[4,256,512]{2,1,0:T(8,128)(2,1)S(1)} %slice.629), channel_id=1, source_target_pairs={{0,2},{1,3},{2,0},{3,1},{4,6},{5,7},{6,4},{7,5},{8,10},{9,11},{10,... | collective-permute-start | bytes 3145736 | tf_op jit(solution)/shard_map/ppermute | solution.py:255
  767.1 23.6 %collective-permute-start.11 = (bf16[4,128,1024]{2,1,0:T(8,128)(2,1)S(1)}, bf16[4,128,1024]{2,1,0:T(8,128)(2,1)S(1)}, u32[]{:S(2)}, u32[]{:S(2)}) collective-permute-start(bf16[4,128,1024]{2,1,0:T(8,128)(2,1)S(1)} %slice.579), channel_id=1, source_target_pairs={{0,1},{1,0},{2,3},{3,2},{4,5},{5,4},{6,7},{7,6},{8,9},{9,8},{10,11... | collective-permute-start | bytes 3145736 | tf_op jit(solution)/shard_map/ppermute | solution.py:255
  770.6 28.2 %collective-permute-start.37 = (bf16[2,256,512]{2,1,0:T(8,128)(2,1)S(1)}, bf16[2,256,512]{2,1,0:T(8,128)(2,1)S(1)}, u32[]{:S(2)}, u32[]{:S(2)}) collective-permute-start(bf16[2,256,512]{2,1,0:T(8,128)(2,1)S(1)} %slice.631), channel_id=1, source_target_pairs={{0,8},{4,12},{8,0},{12,4},{16,24},{20,28},{24,16},{28,20},{1,9},{5... | collective-permute-start | bytes 1572872 | tf_op jit(solution)/shard_map/ppermute | solution.py:255
  791.2 24.5 %collective-permute-start.12 = (bf16[2,128,1024]{2,1,0:T(8,128)(2,1)S(1)}, bf16[2,128,1024]{2,1,0:T(8,128)(2,1)S(1)}, u32[]{:S(2)}, u32[]{:S(2)}) collective-permute-start(bf16[2,128,1024]{2,1,0:T(8,128)(2,1)S(1)} %slice.581), channel_id=1, source_target_pairs={{0,8},{4,12},{8,0},{12,4},{16,24},{20,28},{24,16},{28,20},{1,9},{5... | collective-permute-start | bytes 1572872 | tf_op jit(solution)/shard_map/ppermute | solution.py:255
  792.4 36.3 %collective-permute-start.7 = (bf16[2,256,512]{2,1,0:T(8,128)(2,1)S(1)}, bf16[2,256,512]{2,1,0:T(8,128)(2,1)S(1)}, u32[]{:S(2)}, u32[]{:S(2)}) collective-permute-start(bf16[2,256,512]{2,1,0:T(8,128)(2,1)S(1)} %slice.571), channel_id=1, source_target_pairs={{0,8},{4,12},{8,0},{12,4},{16,24},{20,28},{24,16},{28,20},{1,9},{5... | collective-permute-start | bytes 1572872 | tf_op jit(solution)/shard_map/ppermute | solution.py:255
  799.0 31.0 %collective-permute-start.38 = (bf16[1,256,512]{2,1,0:T(8,128)(2,1)S(1)}, bf16[1,256,512]{2,1,0:T(8,128)(2,1)S(1)}, u32[]{:S(2)}, u32[]{:S(2)}) collective-permute-start(bf16[1,256,512]{2,1,0:T(8,128)(2,1)S(1)} %slice.633), channel_id=1, source_target_pairs={{0,16},{4,20},{8,24},{12,28},{16,0},{20,4},{24,8},{28,12},{1,17},{... | collective-permute-start | bytes 786440 | tf_op jit(solution)/shard_map/ppermute | solution.py:255
  815.9 25.1 %collective-permute-start.13 = (bf16[1,128,1024]{2,1,0:T(8,128)(2,1)S(1)}, bf16[1,128,1024]{2,1,0:T(8,128)(2,1)S(1)}, u32[]{:S(2)}, u32[]{:S(2)}) collective-permute-start(bf16[1,128,1024]{2,1,0:T(8,128)(2,1)S(1)} %slice.583), channel_id=1, source_target_pairs={{0,16},{4,20},{8,24},{12,28},{16,0},{20,4},{24,8},{28,12},{1,17},{... | collective-permute-start | bytes 786440 | tf_op jit(solution)/shard_map/ppermute | solution.py:255
  (145 other events, 1908.0 us)

commit v2 on v1

--- a/solution.py
+++ b/solution.py
@@ -46,48 +46,10 @@
     return (jnp.cos(angles), jnp.sin(angles))
 
 
-def rotate(values, cosine, sine_table):
-    half_size = values.shape[-1] // 2
-    first_half = values[..., :half_size]
-    second_half = values[..., half_size:]
-    return jnp.concatenate(
-        [
-            first_half * cosine - second_half * sine_table,
-            second_half * cosine + first_half * sine_table,
-        ],
-        axis=-1,
-    )
-
-
-def unrotate(grads, cosine, sine_table):
-    half_size = grads.shape[-1] // 2
-    first_half = grads[..., :half_size]
-    second_half = grads[..., half_size:]
-    return jnp.concatenate(
-        [
-            first_half * cosine + second_half * sine_table,
-            second_half * cosine - first_half * sine_table,
-        ],
-        axis=-1,
-    )
-
-
 def times_transposed(left_side, weight):
     return lax.dot_general(
         left_side, weight, (((1,), (1,)), ((), ())), preferred_element_type=jnp.float32
     )
-
-
-def pair_frames(rows_in):
-    frames, groups, group_width = rows_in.shape
-    paired = rows_in.reshape(frames // 2, 2, groups, group_width).transpose(0, 2, 1, 3)
-    return paired.reshape(frames // 2, groups, 2 * group_width)
-
-
-def unpair_frames(rows_in):
-    pairs, groups, double_width = rows_in.shape
-    split_rows = rows_in.reshape(pairs, groups, 2, double_width // 2).transpose(0, 2, 1, 3)
-    return split_rows.reshape(2 * pairs, groups * (double_width // 2))
 
 
 def ffn_forward(values, gain_row, up_weight, down_weight):
@@ -258,6 +220,336 @@
     return blocks[0]
 
 
+def attend_kernel(
+    groups, heads, length_ref, qkv_ref, cos_ref, sin_ref, whole_ref, out_ref,
+    stage, result, sends, arrivals, out_sends, out_arrivals, own_sem,
+):
+    s, b = lax.axis_index("seq"), lax.axis_index("batch")
+    frames = qkv_ref.shape[0]
+    total_frames = whole_ref.shape[0]
+    block = heads * 3 * HD
+    width = heads * HD
+    greet_seq(groups, s, b)
+
+    def rows_of(place):
+        return pl.ds(pl.multiple_of(place * frames, frames), frames)
+
+    def heads_copy(target, sender):
+        return pltpu.make_async_remote_copy(
+            src_ref=stage.at[target],
+            dst_ref=whole_ref.at[rows_of(sender)],
+            send_sem=sends.at[target],
+            recv_sem=arrivals.at[sender],
+            device_id=(b, target),
+            device_id_type=MESH,
+        )
+
+    for column in range(0, groups * block, 128):
+        pattern = (column // 128) % 3
+        values = qkv_ref[:, column : column + 128]
+        turned = (values * cos_ref[pattern] + partner_lanes(values) * sin_ref[pattern]).astype(
+            jnp.bfloat16
+        )
+        start = column
+        while start < column + 128:
+            place = start // block
+            end = min(column + 128, (place + 1) * block)
+            stage[place, :, start - place * block : end - place * block] = turned[
+                :, start - column : end - column
+            ]
+            if end == (place + 1) * block:
+
+                @pl.when(s != place)
+                def _():
+                    heads_copy(place, s).start()
+
+                @pl.when(s == place)
+                def _():
+                    whole_ref[rows_of(s), :] = stage[place]
+
+            start = end
+    for k in range(1, groups):
+        heads_copy(s, lax.rem(s + k, groups)).wait_recv()
+
+    valid = lax.broadcasted_iota(jnp.int32, (1, total_frames), 1) < length_ref[0]
+
+    def out_place(owner):
+        if width % 128 == 0:
+            return out_ref.at[:, pl.ds(pl.multiple_of(owner * width, width), width)]
+        return out_ref.at[owner]
+
+    def result_copy(target, sender):
+        return pltpu.make_async_remote_copy(
+            src_ref=result.at[target],
+            dst_ref=out_place(sender),
+            send_sem=out_sends.at[target],
+            recv_sem=out_arrivals.at[sender],
+            device_id=(b, target),
+            device_id_type=MESH,
+        )
+
+    def one_block(k, carry):
+        place = lax.rem(s + k, groups)
+        for h in range(heads):
+            base = h * 3 * HD
+            query = whole_ref[rows_of(place), base : base + HD]
+            key = whole_ref[:, base + HD : base + 2 * HD]
+            value = whole_ref[:, base + 2 * HD : base + 3 * HD]
+            scores = times_transposed(query, key)
+            scores = jnp.where(valid, scores, MASKED_SCORE)
+            exp_scores = jnp.exp(scores - jnp.max(scores, axis=-1, keepdims=True))
+            share = 1.0 / jnp.sum(exp_scores, axis=-1, keepdims=True)
+            probs = (exp_scores * share).astype(jnp.bfloat16)
+            mixed = jnp.dot(probs, value, preferred_element_type=jnp.float32)
+            result[place, :, h * HD : (h + 1) * HD] = mixed.astype(jnp.bfloat16)
+
+        @pl.when(k < groups)
+        def _():
+            result_copy(place, s).start()
+
+        return carry
+
+    lax.fori_loop(1, groups + 1, one_block, 0)
+    own = pltpu.make_async_copy(result.at[s], out_place(s), own_sem)
+    own.start()
+    for k in range(1, groups):
+        other = lax.rem(s + k, groups)
+        heads_copy(other, s).wait_send()
+        result_copy(other, s).wait_send()
+        result_copy(s, other).wait_recv()
+    own.wait()
+
+
+def greet_seq(groups, s, b):
+    barrier = pltpu.get_barrier_semaphore()
+    for k in range(1, groups):
+        pl.semaphore_signal(
+            barrier, inc=1, device_id=(b, lax.rem(s + k, groups)), device_id_type=MESH
+        )
+    pl.semaphore_wait(barrier, groups - 1)
+
+
+def partner_lanes(values):
+    lanes = lax.broadcasted_iota(jnp.int32, values.shape, 1)
+    return jnp.where(
+        lanes % HD < HD // 2,
+        pltpu.roll(values, 128 - HD // 2, 1),
+        pltpu.roll(values, HD // 2, 1),
+    )
+
+
+def attend(qkv_rows, length, cosine, sine):
+    groups = lax.axis_size("seq")
+    frames = qkv_rows.shape[0]
+    heads = HEADS // groups
+    width = heads * HD
+    signs = jnp.where(jnp.arange(HD) < HD // 2, -1.0, 1.0)
+    cos_head = jnp.concatenate([cosine, cosine], axis=1)
+    sin_head = jnp.concatenate([sine, sine], axis=1) * signs
+    ones, zeros = jnp.ones_like(cos_head), jnp.zeros_like(cos_head)
+    cos_pair = jnp.concatenate([cos_head * 0.125, cos_head, ones] * 2, axis=1)
+    sin_pair = jnp.concatenate([sin_head * 0.125, sin_head, zeros] * 2, axis=1)
+    cos_three = jnp.stack([cos_pair[:, 128 * i : 128 * (i + 1)] for i in range(3)])
+    sin_three = jnp.stack([sin_pair[:, 128 * i : 128 * (i + 1)] for i in range(3)])
+    direct = width % 128 == 0
+    out_shape = (frames, groups * width) if direct else (groups, frames, width)
+    total = frames * groups
+    vmem = pl.BlockSpec(memory_space=pltpu.VMEM)
+    whole, out = pl.pallas_call(
+        functools.partial(attend_kernel, groups, heads),
+        out_shape=(
+            jax.ShapeDtypeStruct((total, 3 * width), jnp.bfloat16),
+            jax.ShapeDtypeStruct(out_shape, jnp.bfloat16),
+        ),
+        in_specs=[pl.BlockSpec(memory_space=pltpu.SMEM), vmem, vmem, vmem],
+        out_specs=(vmem, pl.BlockSpec(memory_space=pl.ANY)),
+        scratch_shapes=[
+            pltpu.VMEM((groups, frames, 3 * width), jnp.bfloat16),
+            pltpu.VMEM((groups, frames, width), jnp.bfloat16),
+            pltpu.SemaphoreType.DMA((groups,)),
+            pltpu.SemaphoreType.DMA((groups,)),
+            pltpu.SemaphoreType.DMA((groups,)),
+            pltpu.SemaphoreType.DMA((groups,)),
+            pltpu.SemaphoreType.DMA,
+        ],
+        compiler_params=pltpu.CompilerParams(
+            collective_id=4, has_side_effects=True, vmem_limit_bytes=48 << 20
+        ),
+        cost_estimate=pl.CostEstimate(
+            flops=4 * heads * HD * total * total,
+            bytes_accessed=4 * qkv_rows.size + 2 * total * 4 * width,
+            transcendentals=heads * total * total,
+        ),
+    )(length.reshape(1), qkv_rows, cos_three, sin_three)
+    if not direct:
+        out = out.transpose(1, 0, 2).reshape(frames, groups * width)
+    return whole, out
+
+
+def attend_back_kernel(
+    groups, heads, length_ref, whole_ref, grad_ref, cos_ref, sin_ref, out_ref,
+    stage, grads, result, query_key, value_total, sends, arrivals, out_sends, out_arrivals, own_sem,
+):
+    s, b = lax.axis_index("seq"), lax.axis_index("batch")
+    frames = grad_ref.shape[0]
+    total_frames = whole_ref.shape[0]
+    block = heads * 3 * HD
+    width = heads * HD
+    greet_seq(groups, s, b)
+
+    def rows_of(place):
+        return pl.ds(pl.multiple_of(place * frames, frames), frames)
+
+    def grad_copy(target, sender):
+        return pltpu.make_async_remote_copy(
+            src_ref=stage.at[target],
+            dst_ref=grads.at[rows_of(sender)],
+            send_sem=sends.at[target],
+            recv_sem=arrivals.at[sender],
+            device_id=(b, target),
+            device_id_type=MESH,
+        )
+
+    for place in range(groups):
+        stage[place] = grad_ref[:, place * width : (place + 1) * width]
+
+        @pl.when(s != place)
+        def _():
+            grad_copy(place, s).start()
+
+        @pl.when(s == place)
+        def _():
+            grads[rows_of(s), :] = stage[place]
+
+    part_heads = 2 if heads % 2 == 0 else heads
+    parts = heads // part_heads
+    span = part_heads * 3 * HD
+
+    def out_place(owner, part):
+        if block % 128 == 0:
+            start = pl.multiple_of(owner * block + part * span, 128)
+            return out_ref.at[:, pl.ds(start, span)]
+        return out_ref.at[owner, :, pl.ds(part * span, span)]
+
+    def result_copy(target, sender, part):
+        return pltpu.make_async_remote_copy(
+            src_ref=result.at[part, rows_of(target)],
+            dst_ref=out_place(sender, part),
+            send_sem=out_sends.at[part, target],
+            recv_sem=out_arrivals.at[part, sender],
+            device_id=(b, target),
+            device_id_type=MESH,
+        )
+
+    valid = lax.broadcasted_iota(jnp.int32, (total_frames, 1), 0) < length_ref[0]
+    for h in range(heads):
+        base = h * 3 * HD
+        key = whole_ref[:, base + HD : base + 2 * HD]
+        key_turned = key.T
+        value = whole_ref[:, base + 2 * HD : base + 3 * HD]
+        query_key[...] = jnp.zeros_like(query_key)
+        value_total[...] = jnp.zeros_like(value_total)
+
+        def one_block(k, carry, h=h, base=base, key=key, key_turned=key_turned, value=value):
+            place = lax.rem(s + k, groups)
+            if h == 0:
+
+                @pl.when(k > 0)
+                def _():
+                    grad_copy(s, place).wait_recv()
+
+            query = whole_ref[rows_of(place), base : base + HD]
+            grad = grads[rows_of(place), h * HD : (h + 1) * HD]
+            scores = jnp.where(valid, times_transposed(key, query), MASKED_SCORE)
+            exp_scores = jnp.exp(scores - jnp.max(scores, axis=0, keepdims=True))
+            probs = exp_scores * (1.0 / jnp.sum(exp_scores, axis=0, keepdims=True))
+            value_total[...] += jnp.dot(
+                probs.astype(jnp.bfloat16), grad, preferred_element_type=jnp.float32
+            )
+            grad_probs = times_transposed(value, grad)
+            mean = jnp.sum(probs * grad_probs, axis=0, keepdims=True)
+            grad_scores = (probs * (grad_probs - mean)).astype(jnp.bfloat16)
+            query_key[:, HD:] += jnp.dot(grad_scores, query, preferred_element_type=jnp.float32)
+            query_key[rows_of(place), :HD] = jnp.dot(
+                key_turned, grad_scores, preferred_element_type=jnp.float32
+            ).T
+            return carry
+
+        lax.fori_loop(0, groups, one_block, 0)
+        part, inside = h // part_heads, (h % part_heads) * 3 * HD
+        both = query_key[...]
+        turned = both * cos_ref[...] + partner_lanes(both) * sin_ref[...]
+        result[part, :, inside : inside + 2 * HD] = turned.astype(jnp.bfloat16)
+        result[part, :, inside + 2 * HD : inside + 3 * HD] = value_total[...].astype(jnp.bfloat16)
+        if (h + 1) % part_heads == 0:
+            for k in range(1, groups):
+                result_copy(lax.rem(s + k, groups), s, part).start()
+    owns = []
+    for part in range(parts):
+        owns.append(
+            pltpu.make_async_copy(
+                result.at[part, rows_of(s)], out_place(s, part), own_sem.at[part]
+            )
+        )
+        owns[-1].start()
+    for k in range(1, groups):
+        other = lax.rem(s + k, groups)
+        grad_copy(other, s).wait_send()
+        for part in range(parts):
+            result_copy(other, s, part).wait_send()
+            result_copy(s, other, part).wait_recv()
+    for own in owns:
+        own.wait()
+
+
+def attend_back(whole, grad_attn, length, cosine, sine):
+    groups = lax.axis_size("seq")
+    frames = grad_attn.shape[0]
+    heads = HEADS // groups
+    width = heads * HD
+    block = 3 * width
+    total = frames * groups
+    signs = jnp.where(jnp.arange(HD) < HD // 2, 1.0, -1.0)
+    cos_head = jnp.concatenate([cosine, cosine], axis=1)
+    sin_head = jnp.concatenate([sine, sine], axis=1) * signs
+    cos_both = jnp.concatenate([cos_head * 0.125, cos_head], axis=1)
+    sin_both = jnp.concatenate([sin_head * 0.125, sin_head], axis=1)
+    part_heads = 2 if heads % 2 == 0 else heads
+    parts = heads // part_heads
+    direct = block % 128 == 0
+    out_shape = (frames, groups * block) if direct else (groups, frames, block)
+    vmem = pl.BlockSpec(memory_space=pltpu.VMEM)
+    out = pl.pallas_call(
+        functools.partial(attend_back_kernel, groups, heads),
+        out_shape=jax.ShapeDtypeStruct(out_shape, jnp.bfloat16),
+        in_specs=[pl.BlockSpec(memory_space=pltpu.SMEM), vmem, vmem, vmem, vmem],
+        out_specs=pl.BlockSpec(memory_space=pl.ANY),
+        scratch_shapes=[
+            pltpu.VMEM((groups, frames, width), jnp.bfloat16),
+            pltpu.VMEM((total, width), jnp.bfloat16),
+            pltpu.VMEM((parts, total, part_heads * 3 * HD), jnp.bfloat16),
+            pltpu.VMEM((total, 2 * HD), jnp.float32),
+            pltpu.VMEM((total, HD), jnp.float32),
+            pltpu.SemaphoreType.DMA((groups,)),
+            pltpu.SemaphoreType.DMA((groups,)),
+            pltpu.SemaphoreType.DMA((parts, groups)),
+            pltpu.SemaphoreType.DMA((parts, groups)),
+            pltpu.SemaphoreType.DMA((parts,)),
+        ],
+        compiler_params=pltpu.CompilerParams(
+            collective_id=5, has_side_effects=True, vmem_limit_bytes=48 << 20
+        ),
+        cost_estimate=pl.CostEstimate(
+            flops=10 * heads * HD * total * total,
+            bytes_accessed=2 * total * 8 * width,
+            transcendentals=heads * total * total,
+        ),
+    )(length.reshape(1), whole, grad_attn, cos_both, sin_both)
+    if not direct:
+        out = out.transpose(1, 0, 2).reshape(frames, groups * block)
+    return out
+
+
 def shards(
     frames_in,
     cotangent,
@@ -288,8 +580,6 @@
     seq_index = lax.axis_index("seq")
     item_index = lax.axis_index("batch")
     seq_length = frames * groups
-    local_heads = HEADS // groups
-    head_width = local_heads * HD
     level_count = cond_table.shape[0] - 1
     cond_rows = cond_table.astype(jnp.float32)
     gain_rows = norm_gains.astype(jnp.float32)
@@ -307,48 +597,9 @@
     rows_one, ffn1_state = ffn_forward(start_rows, gain_rows[0], w_ffn1_up, w_ffn1_down)
     normed_attn, attn_pull = jax.vjp(layer_norm, rows_one, gain_rows[1])
     attn_in = normed_attn.astype(jnp.bfloat16)
-    qkv_rows = jnp.dot(attn_in, w_qkv, preferred_element_type=jnp.float32).reshape(
-        frames, HEADS, 3, HD
-    )
+    qkv_rows = jnp.dot(attn_in, w_qkv, preferred_element_type=jnp.float32)
     cosine, sine_table = rope_tables(positions, HD)
-    query_rot = rotate(qkv_rows[:, :, 0], cosine[:, None], sine_table[:, None]) * 0.125
-    key_rot = rotate(qkv_rows[:, :, 1], cosine[:, None], sine_table[:, None])
-    packed = jnp.stack([query_rot, key_rot, qkv_rows[:, :, 2]], axis=2).astype(jnp.bfloat16)
-    incoming = lax.all_to_all(
-        pair_frames(packed.reshape(frames, groups, local_heads * 3 * HD)),
-        "seq",
-        split_axis=1,
-        concat_axis=0,
-        tiled=True,
-    )
-    whole_heads = incoming.reshape(seq_length, local_heads, 3, HD)
-    query_all = whole_heads[:, :, 0]
-    key_all = whole_heads[:, :, 1]
-    value_all = whole_heads[:, :, 2]
-    key_valid = (jnp.arange(seq_length) < length)[None, None, :]
-    block_rows = min(512, seq_length)
-    block_count = seq_length // block_rows
-    query_blocks = query_all.reshape(block_count, block_rows, local_heads, HD)
-
-    def attend_block(query_block):
-        scores = jnp.einsum(
-            "qhd,khd->hqk", query_block, key_all, preferred_element_type=jnp.float32
-        )
-        scores = jnp.where(key_valid, scores, MASKED_SCORE)
-        row_peak = jnp.max(scores, axis=-1, keepdims=True)
-        exp_scores = jnp.exp(scores - row_peak)
-        row_total = jnp.sum(exp_scores, axis=-1, keepdims=True)
-        probs_low = (exp_scores / row_total).astype(jnp.bfloat16)
-        mixed_block = jnp.einsum(
-            "hqk,khd->qhd", probs_low, value_all, preferred_element_type=jnp.float32
-        )
-        return (mixed_block.astype(jnp.bfloat16), (row_peak + jnp.log(row_total))[:, :, 0])
-
-    mixed_blocks, lse_blocks = lax.map(attend_block, query_blocks)
-    mixed_rows = mixed_blocks.reshape(seq_length // 2, 1, 2 * head_width)
-    attn_out = unpair_frames(
-        lax.all_to_all(mixed_rows, "seq", split_axis=0, concat_axis=1, tiled=True)
-    )
+    whole_heads, attn_out = attend(qkv_rows, length, cosine, sine_table)
     rows_two = rows_one + jnp.dot(attn_out, w_out, preferred_element_type=jnp.float32)
     normed_conv, conv_pull = jax.vjp(layer_norm, rows_two, gain_rows[2])
     conv_in = normed_conv.astype(jnp.bfloat16)
@@ -437,64 +688,8 @@
     grad_two = grad_three + grad_conv_in
     grad_r = grad_two.astype(jnp.bfloat16)
     grad_attn_out = times_transposed(grad_r, w_out).astype(jnp.bfloat16)
-    grad_heads = lax.all_to_all(
-        pair_frames(grad_attn_out.reshape(frames, groups, head_width)),
-        "seq",
-        split_axis=1,
-        concat_axis=0,
-        tiled=True,
-    )
-    grad_blocks = grad_heads.reshape(block_count, block_rows, local_heads, HD)
-
-    def attend_back(carry_pair, pieces):
-        grad_key, grad_value = carry_pair
-        query_block, grad_block, lse_block = pieces
-        scores = jnp.einsum(
-            "qhd,khd->hqk", query_block, key_all, preferred_element_type=jnp.float32
-        )
-        scores = jnp.where(key_valid, scores, MASKED_SCORE)
-        probs_row = jnp.exp(scores - lse_block[:, :, None])
-        probs_low = probs_row.astype(jnp.bfloat16)
-        grad_value = grad_value + jnp.einsum(
-            "hqk,qhd->khd", probs_low, grad_block, preferred_element_type=jnp.float32
-        )
-        grad_probs = jnp.einsum(
-            "qhd,khd->hqk", grad_block, value_all, preferred_element_type=jnp.float32
-        )
-        grad_scores = (
-            probs_row * (grad_probs - jnp.sum(probs_row * grad_probs, axis=-1, keepdims=True))
-        ).astype(jnp.bfloat16)
-        grad_query = jnp.einsum(
-            "hqk,khd->qhd", grad_scores, key_all, preferred_element_type=jnp.float32
-        )
-        grad_key = grad_key + jnp.einsum(
-            "hqk,qhd->khd", grad_scores, query_block, preferred_element_type=jnp.float32
-        )
-        return ((grad_key, grad_value), grad_query)
-
-    zero_heads = jnp.zeros((seq_length, local_heads, HD), jnp.float32)
-    key_value_grads, query_grads = lax.scan(
-        attend_back, (zero_heads, zero_heads), (query_blocks, grad_blocks, lse_blocks)
-    )
     cos_all, sin_all = rope_tables(jnp.arange(seq_length), HD)
-    grad_query_pre = (
-        unrotate(
-            query_grads.reshape(seq_length, local_heads, HD), cos_all[:, None], sin_all[:, None]
-        )
-        * 0.125
-    )
-    grad_key_pre = unrotate(key_value_grads[0], cos_all[:, None], sin_all[:, None])
-    stacked = jnp.stack([grad_query_pre, grad_key_pre, key_value_grads[1]], axis=2).astype(
-        jnp.bfloat16
-    )
-    returned = lax.all_to_all(
-        stacked.reshape(seq_length // 2, 1, 2 * local_heads * 3 * HD),
-        "seq",
-        split_axis=0,
-        concat_axis=1,
-        tiled=True,
-    )
-    grad_qkv = unpair_frames(returned)
+    grad_qkv = attend_back(whole_heads, grad_attn_out, length, cos_all, sin_all)
     grad_attn_part, grad_gain_one = attn_pull(times_transposed(grad_qkv, w_qkv))
     grad_one = grad_two + grad_attn_part
     grad_zero, grad_gain_zero, ffn1_up_pair, ffn1_down_pair = ffn_backward(

time: 858 us -> 616 us (0.72)
  local copies, waits for them, and re-layouts: 190 us -> 42.9 us
  waiting for transfers between devices: 276 us -> 188 us
  Pallas kernels: 77.6 us -> 160 us
  matrix products: 110 us -> 72.6 us
  other arithmetic: 113 us -> 81.9 us
  starting transfers between devices: 73.1 us -> 57.8 us
    pallas_call x0 -> x2, Pallas kernels: none -> 82.9 us  [the longest x1 47.4 us: attend_back(): pl.pallas_call(functools.partial(attend_back_kernel, groups, heads), out_...]
    ppermute x40, waiting for transfers between devices: 246 us -> 188 us  [owned_sum(): arrived = lax.ppermute(blocks[half:], axis, pairs)]
    dot_general x15 -> x1, matrix products: 41.4 us -> 1.79 us  [shards(): qkv_rows = jnp.dot(attn_in, w_qkv, preferred_element_type=jnp.float32)]
    unnamed x233 -> x158, local copies, waits for them, and re-layouts: 39 us -> 10 us
    all_to_all x4 -> x0, waiting for transfers between devices: 27.6 us -> none  [the longest x1 19.3 us: shards(): lax.all_to_all(pair_frames(packed.reshape(frames, groups, local_heads * 3...]
    convert_element_type x2 -> x0, local copies, waits for them, and re-layouts: 23 us -> none  [the longest x1 14.4 us: shards(): jnp.stack([grad_query_pre, grad_key_pre, key_value_grads[1]], axis=2)]
    dynamic_update_slice x4 -> x0, local copies, waits for them, and re-layouts: 21.8 us -> none  [shards(): lax.scan(attend_back, (zero_heads, zero_heads), (query_blocks, grad_block...]
    slice x4 -> x0, local copies, waits for them, and re-layouts: 21.8 us -> none  [the longest x2 16.5 us: shards(): value_all = whole_heads[:, :, 2]]
  transfers between devices with their start and end apart: 48 -> 44, of which waited for: 21 -> 16; matrix products, arithmetic and copies ran while one was open for 27% -> 19% of each run, Pallas kernels for 6% -> 16%
where the time goes in v2:
time: 616 us; the launch traced here: 607 us
  waiting for transfers between devices  188 us (31%)
  Pallas kernels  160 us (26%)
  other arithmetic  81.9 us (13%)
  matrix products  72.6 us (12%)
  starting transfers between devices  57.8 us (9%)
  local copies, waits for them, and re-layouts  42.9 us (7%)
    ppermute x40, waiting for transfers between devices, owned_sum(): arrived = lax.ppermute(blocks[half:], axis, pairs)  188 us
    dot_general x8, matrix products, times_transposed(): lax.dot_general(left_side, weight, (((1,), (1,)), ((), ())), preferred_el...  47.5 us
    pallas_call x1, Pallas kernels, attend_back(): pl.pallas_call(functools.partial(attend_back_kernel, groups, heads), out_...  47.4 us
    convert_element_type x32, other arithmetic, owned_sum(): blocks = total.astype(jnp.bfloat16) if half > 1 else total  46.2 us
    ppermute x40, starting transfers between devices, owned_sum(): arrived = lax.ppermute(blocks[half:], axis, pairs)  45.8 us
    pallas_call x3, Pallas kernels, sum_everywhere(): pl.pallas_call(functools.partial(sum_kernel, groups, batches), out_shape=...  42.3 us
    pallas_call x1, Pallas kernels, attend(): pl.pallas_call(functools.partial(attend_kernel, groups, heads), out_shape...  35.5 us
    pallas_call x8, Pallas kernels, block_products(): pl.pallas_call(functools.partial(product_kernel, steps, tall, rows, cols,...  34.4 us
  transfers between devices with their start and end apart: 44, of which 16 were waited for; matrix products, arithmetic and copies ran while one was open for 19% of the time, Pallas kernels for 16%

profile of v2, /device:TPU:0, one launch (start us, length us, event | category | flops | bytes accessed | tf_op | source)
XLA Modules:
  0.0 607.2 jit_solution(2914332046969685382)
XLA Ops:
  11.0 8.0 %multiply_convert_fusion.1 = (bf16[256,4096]{1,0:T(8,128)(2,1)S(1)}, f32[256,4096]{1,0:T(8,128)}) fusion(bf16[256,1024]{1,0:T(8,128)(2,1)S(1)} %multiply_convert_fusion.13.left_ref, bf16[1024,4096]{1,0:T(8,128)(2,1)} %param.27), kind=kOutput, calls=%fused_computation.18 | convolution fusion | flops 2152726528 | bytes 15204352 | tf_op jit(solution)/shard_map/dot_general | solution.py:58
  25.0 35.5 %shard_map.323 = (bf16[1024,768]{1,0:T(8,128)(2,1)S(1)}, bf16[256,1024]{1,0:T(8,128)(2,1)S(1)}) custom-call(s32[1]{0:T(128)} %dynamic_slice.6.length_ref, f32[256,3072]{1,0:T(8,128)S(1)} %fusion.56.qkv_ref, f32[3,256,128]{2,1,0:T(8,128)S(1)} %pad_maximum_fusion.7.cos_ref, f32[3,256,128]{2,1,0:T(8,128)S(1)} %pad_maximum_fusion.8.sin_ref), custom_call_target="tpu_custom_call" | custom-call | flops 1073741824 | bytes 5242880 | tf_op jit(solution)/shard_map/pallas_call | solution.py:358
  65.5 4.8 collective-permute-start
  80.6 11.8 %shard_map.324 = f32[2,1024]{1,0:T(2,128)S(1)} custom-call(f32[2,1024]{1,0:T(2,128)S(1)} %pad_maximum_fusion.9.rows_ref), custom_call_target="tpu_custom_call" | custom-call | tf_op jit(solution)/shard_map/pallas_call | solution.py:113
  95.4 6.3 %multiply_convert_fusion = (bf16[256,4096]{1,0:T(8,128)(2,1)S(1)}, f32[256,4096]{1,0:T(8,128)S(1)}) fusion(bf16[256,1024]{1,0:T(8,128)(2,1)S(1)} %multiply_convert_fusion.8.left_ref, bf16[1024,4096]{1,0:T(8,128)(2,1)} %param.36), kind=kOutput, calls=%fused_computation.16 | convolution fusion | flops 2152726528 | bytes 15204352 | tf_op jit(solution)/shard_map/dot_general | solution.py:58
  106.9 16.4 %fusion.3.right_ref = bf16[256,4096]{1,0:T(8,128)(2,1)S(1)} fusion(bf16[256,1024]{1,0:T(8,128)(2,1)S(1)} %multiply_convert_fusion.6.right_ref, bf16[4096,1024]{1,0:T(8,128)(2,1)} %param.37, f32[256,4096]{1,0:T(8,128)S(1)} %get-tuple-element.108), kind=kOutput, calls=%fused_computation.10 | convolution fusion | flops 2156920832 | bytes 15204352 | tf_op jit(solution)/shard_map/dot_general | solution.py:50
  123.4 6.6 %multiply_reduce_fusion.1 = (f32[1024]{0:T(1024)}, f32[256]{0:T(256)S(1)}, f32[256,1024]{1,0:T(8,128)S(1)}) fusion(f32[256,1024]{1,0:T(8,128)S(1)} %get-tuple-element.106, f32[256]{0:T(256)S(1)} %fusion.36, f32[256]{0:T(256)S(1)} %broadcast_multiply_fusion.5, f32[1024]{0:T(1024)S(1)} %bitcast.190, bf16[256,4096]{1,0:T(8,128)(2,1)S(1)} %fusion.3.right_ref, ...), kind=kOutput, calls=%fused_computation.74 | convolution fusion | flops 2149317376 | bytes 12594176 | tf_op jit(solution)/shard_map/dot_general | solution.py:50
  140.3 9.2 %shard_map.325 = f32[2,1024]{1,0:T(2,128)S(1)} custom-call(f32[2,1024]{1,0:T(2,128)S(1)} %pad_maximum_fusion.10.rows_ref), custom_call_target="tpu_custom_call" | custom-call | tf_op jit(solution)/shard_map/pallas_call | solution.py:113
  152.5 4.5 collective-permute-start.3
  162.3 4.5 shard_map.335
  184.1 47.4 %shard_map.326.right_ref = bf16[256,3072]{1,0:T(8,128)(2,1)S(1)} custom-call(s32[1]{0:T(128)} %dynamic_slice.6.length_ref, bf16[1024,768]{1,0:T(8,128)(2,1)S(1)} %copy-done.16, bf16[256,1024]{1,0:T(8,128)(2,1)S(1)} %convolution_convert_fusion.grad_ref, f32[1024,128]{1,0:T(8,128)S(1)} %copy-done.13, f32[1024,128]{1,0:T(8,128)S(1)} %copy-done.14), custom_call_target="tpu_custom_call" | custom-call | flops 2684354560 | bytes 4194304 | tf_op jit(solution)/shard_map/pallas_call | solution.py:522
  231.6 5.5 multiply_reduce_fusion.3
  244.8 7.4 %fusion.2.right_ref = bf16[256,4096]{1,0:T(8,128)(2,1)S(1)} fusion(bf16[256,1024]{1,0:T(8,128)(2,1)S(1)} %get-tuple-element.51.right_ref, bf16[4096,1024]{1,0:T(8,128)(2,1)} %param.28, f32[256,4096]{1,0:T(8,128)} %get-tuple-element.100), kind=kOutput, calls=%fused_computation.9 | convolution fusion | flops 2156920832 | bytes 15204352 | tf_op jit(solution)/shard_map/dot_general | solution.py:50
  255.4 7.5 %multiply_reduce_fusion.4 = (f32[1024]{0:T(1024)}, f32[256]{0:T(256)S(1)}, f32[256,1024]{1,0:T(8,128)}) fusion(bf16[1,256,1024]{2,1,0:T(8,128)(2,1)S(1)} %copy-done.31, f32[256]{0:T(256)S(1)} %fusion.33, f32[256]{0:T(256)S(1)} %broadcast_multiply_fusion.8, f32[1024]{0:T(1024)S(1)} %bitcast.154, f32[256]{0:T(256)S(1)} %bitcast.167, f32[1024]{0:T(1024)S(1)} %fusion.31, ...), kind=kOutput, calls=%fused_computation.77 | convolution fusion | flops 2150365952 | bytes 12079104 | tf_op jit(solution)/shard_map/dot_general | solution.py:50
  277.4 8.5 %collective-permute-done.20 = bf16[8,256,128]{2,1,0:T(8,128)(2,1)S(1)} collective-permute-done((bf16[8,256,128]{2,1,0:T(8,128)(2,1)S(1)}, bf16[8,256,128]{2,1,0:T(8,128)(2,1)S(1)}, u32[]{:S(2)}, u32[]{:S(2)}) %collective-permute-start.20) | collective-permute-done | bytes 524320 | tf_op jit(solution)/shard_map/ppermute | solution.py:217
  291.5 17.4 %collective-permute-done.21 = bf16[4,256,128]{2,1,0:T(8,128)(2,1)S(1)} collective-permute-done((bf16[4,256,128]{2,1,0:T(8,128)(2,1)S(1)}, bf16[4,256,128]{2,1,0:T(8,128)(2,1)S(1)}, u32[]{:S(2)}, u32[]{:S(2)}) %collective-permute-start.21) | collective-permute-done | bytes 262176 | tf_op jit(solution)/shard_map/ppermute | solution.py:217
  320.3 4.5 shard_map.329
  336.5 21.3 %shard_map.327 = f32[23,1024]{1,0:T(8,128)S(1)} custom-call(f32[23,1024]{1,0:T(8,128)S(1)} %concatenate.82.rows_ref), custom_call_target="tpu_custom_call" | custom-call | tf_op jit(solution)/shard_map/pallas_call | solution.py:113
  362.8 4.8 collective-permute-start.27
  379.2 5.5 add_convert_fusion.1
  389.3 6.4 %add_convert_fusion = bf16[16,128,1024]{2,1,0:T(8,128)(2,1)} fusion(bf16[16,128,1024]{2,1,0:T(8,128)(2,1)} %collective-permute-done.39, bf16[32,128,1024]{2,1,0:T(8,128)(2,1)S(1)} %bitcast.144), kind=kLoop, calls=%fused_computation | loop fusion | flops 8388608 | bytes 12582912 | tf_op jit(solution)/shard_map/convert_element_type | solution.py:219
  398.8 12.3 %collective-permute-done.15 = bf16[8,256,384]{2,1,0:T(8,128)(2,1)} collective-permute-done((bf16[8,256,384]{2,1,0:T(8,128)(2,1)S(1)}, bf16[8,256,384]{2,1,0:T(8,128)(2,1)}, u32[]{:S(2)}, u32[]{:S(2)}) %collective-permute-start.15) | collective-permute-done | bytes 1572896 | tf_op jit(solution)/shard_map/ppermute | solution.py:217
  416.0 6.3 %add_convert_fusion.3 = bf16[16,256,512]{2,1,0:T(8,128)(2,1)} fusion(bf16[16,256,512]{2,1,0:T(8,128)(2,1)} %collective-permute-done.4, bf16[32,256,512]{2,1,0:T(8,128)(2,1)S(1)} %bitcast.146), kind=kLoop, calls=%fused_computation.3 | loop fusion | flops 8388608 | bytes 12582912 | tf_op jit(solution)/shard_map/convert_element_type | solution.py:219
  431.4 22.2 %collective-permute-done.16 = bf16[4,256,384]{2,1,0:T(8,128)(2,1)S(1)} collective-permute-done((bf16[4,256,384]{2,1,0:T(8,128)(2,1)S(1)}, bf16[4,256,384]{2,1,0:T(8,128)(2,1)S(1)}, u32[]{:S(2)}, u32[]{:S(2)}) %collective-permute-start.16) | collective-permute-done | bytes 786464 | tf_op jit(solution)/shard_map/ppermute | solution.py:217
  457.9 5.0 collective-permute-done.17
  472.2 26.3 %collective-permute-done.5 = bf16[8,256,512]{2,1,0:T(8,128)(2,1)S(1)} collective-permute-done((bf16[8,256,512]{2,1,0:T(8,128)(2,1)S(1)}, bf16[8,256,512]{2,1,0:T(8,128)(2,1)S(1)}, u32[]{:S(2)}, u32[]{:S(2)}) %collective-permute-start.5) | collective-permute-done | bytes 2097184 | tf_op jit(solution)/shard_map/ppermute | solution.py:217
  499.7 5.0 collective-permute-done.10
  508.2 19.1 %collective-permute-done.36 = bf16[4,256,512]{2,1,0:T(8,128)(2,1)S(1)} collective-permute-done((bf16[4,256,512]{2,1,0:T(8,128)(2,1)S(1)}, bf16[4,256,512]{2,1,0:T(8,128)(2,1)S(1)}, u32[]{:S(2)}, u32[]{:S(2)}) %collective-permute-start.36) | collective-permute-done | bytes 1048608 | tf_op jit(solution)/shard_map/ppermute | solution.py:217
  530.4 17.6 %collective-permute-done.6 = bf16[4,256,512]{2,1,0:T(8,128)(2,1)S(1)} collective-permute-done((bf16[4,256,512]{2,1,0:T(8,128)(2,1)S(1)}, bf16[4,256,512]{2,1,0:T(8,128)(2,1)S(1)}, u32[]{:S(2)}, u32[]{:S(2)}) %collective-permute-start.6) | collective-permute-done | bytes 1048608 | tf_op jit(solution)/shard_map/ppermute | solution.py:217
  554.5 21.1 %collective-permute-done.7 = bf16[2,256,512]{2,1,0:T(8,128)(2,1)S(1)} collective-permute-done((bf16[2,256,512]{2,1,0:T(8,128)(2,1)S(1)}, bf16[2,256,512]{2,1,0:T(8,128)(2,1)S(1)}, u32[]{:S(2)}, u32[]{:S(2)}) %collective-permute-start.7) | collective-permute-done | bytes 524320 | tf_op jit(solution)/shard_map/ppermute | solution.py:217
  577.3 7.4 %collective-permute-done.12 = bf16[2,128,1024]{2,1,0:T(8,128)(2,1)S(1)} collective-permute-done((bf16[2,128,1024]{2,1,0:T(8,128)(2,1)S(1)}, bf16[2,128,1024]{2,1,0:T(8,128)(2,1)S(1)}, u32[]{:S(2)}, u32[]{:S(2)}) %collective-permute-start.12) | collective-permute-done | bytes 524320 | tf_op jit(solution)/shard_map/ppermute | solution.py:217
  587.7 14.0 %collective-permute-done.8 = bf16[1,256,512]{2,1,0:T(8,128)(2,1)S(1)} collective-permute-done((bf16[1,256,512]{2,1,0:T(8,128)(2,1)S(1)}, bf16[1,256,512]{2,1,0:T(8,128)(2,1)S(1)}, u32[]{:S(2)}, u32[]{:S(2)}) %collective-permute-start.8) | collective-permute-done | bytes 262176 | tf_op jit(solution)/shard_map/ppermute | solution.py:217
  (423 shorter events, 202.4 us)
Async XLA Ops:
  151.2 20.4 %collective-permute-start.2 = (bf16[2,1024]{1,0:T(2,128)(2,1)S(1)}, bf16[2,1024]{1,0:T(2,128)(2,1)S(1)}, u32[]{:S(2)}, u32[]{:S(2)}) collective-permute-start(bf16[2,1024]{1,0:T(2,128)(2,1)S(1)} %get-tuple-element.71), channel_id=1, source_target_pairs={{1,0},{2,1},{3,2},{5,4},{6,5},{7,6},{9,8},{10,9},{11,10},{13,12},{... | collective-permute-start | bytes 12296 | tf_op jit(solution)/shard_map/ppermute | solution.py:29
  158.2 94.0 %collective-permute-start.29 = (bf16[16,256,128]{2,1,0:T(8,128)(2,1)}, bf16[16,256,128]{2,1,0:T(8,128)(2,1)}, u32[]{:S(2)}, u32[]{:S(2)}) collective-permute-start(bf16[16,256,128]{2,1,0:T(8,128)(2,1)} %slice.558), channel_id=1, source_target_pairs={{0,4},{4,0},{8,12},{12,8},{16,20},{20,16},{24,28},{28,24},{1,5},{5... | collective-permute-start | bytes 3145736 | tf_op jit(solution)/shard_map/ppermute | solution.py:217
  160.5 216.4 %collective-permute-start.34 = (bf16[16,256,512]{2,1,0:T(8,128)(2,1)}, bf16[16,256,512]{2,1,0:T(8,128)(2,1)}, u32[]{:S(2)}, u32[]{:S(2)}) collective-permute-start(bf16[16,256,512]{2,1,0:T(8,128)(2,1)} %slice.568), channel_id=1, source_target_pairs={{0,4},{4,0},{8,12},{12,8},{16,20},{20,16},{24,28},{28,24},{1,5},{5... | collective-permute-start | bytes 12582920 | tf_op jit(solution)/shard_map/ppermute | solution.py:217
  237.5 32.5 %collective-permute-start.19 = (bf16[16,256,128]{2,1,0:T(8,128)(2,1)}, bf16[16,256,128]{2,1,0:T(8,128)(2,1)}, u32[]{:S(2)}, u32[]{:S(2)}) collective-permute-start(bf16[16,256,128]{2,1,0:T(8,128)(2,1)} %slice.538), channel_id=1, source_target_pairs={{0,4},{4,0},{8,12},{12,8},{16,20},{20,16},{24,28},{28,24},{1,5},{5... | collective-permute-start | bytes 3145736 | tf_op jit(solution)/shard_map/ppermute | solution.py:217
  243.0 31.4 %collective-permute-start.24 = (bf16[16,256,256]{2,1,0:T(8,128)(2,1)}, bf16[16,256,256]{2,1,0:T(8,128)(2,1)}, u32[]{:S(2)}, u32[]{:S(2)}) collective-permute-start(bf16[16,256,256]{2,1,0:T(8,128)(2,1)} %slice.548), channel_id=1, source_target_pairs={{0,4},{4,0},{8,12},{12,8},{16,20},{20,16},{24,28},{28,24},{1,5},{5... | collective-permute-start | bytes 6291464 | tf_op jit(solution)/shard_map/ppermute | solution.py:217
  269.9 92.8 %collective-permute-start.14 = (bf16[16,256,384]{2,1,0:T(8,128)(2,1)}, bf16[16,256,384]{2,1,0:T(8,128)(2,1)}, u32[]{:S(2)}, u32[]{:S(2)}) collective-permute-start(bf16[16,256,384]{2,1,0:T(8,128)(2,1)} %slice.528), channel_id=1, source_target_pairs={{0,4},{4,0},{8,12},{12,8},{16,20},{20,16},{24,28},{28,24},{1,5},{5... | collective-permute-start | bytes 9437192 | tf_op jit(solution)/shard_map/ppermute | solution.py:217
  276.8 37.9 %collective-permute-start.25 = (bf16[8,256,256]{2,1,0:T(8,128)(2,1)S(1)}, bf16[8,256,256]{2,1,0:T(8,128)(2,1)S(1)}, u32[]{:S(2)}, u32[]{:S(2)}) collective-permute-start(bf16[8,256,256]{2,1,0:T(8,128)(2,1)S(1)} %slice.550), channel_id=1, source_target_pairs={{0,2},{1,3},{2,0},{3,1},{4,6},{5,7},{6,4},{7,5},{8,10},{9,11},{10,... | collective-permute-start | bytes 3145736 | tf_op jit(solution)/shard_map/ppermute | solution.py:217
  286.1 22.8 %collective-permute-start.21 = (bf16[4,256,128]{2,1,0:T(8,128)(2,1)S(1)}, bf16[4,256,128]{2,1,0:T(8,128)(2,1)S(1)}, u32[]{:S(2)}, u32[]{:S(2)}) collective-permute-start(bf16[4,256,128]{2,1,0:T(8,128)(2,1)S(1)} %slice.542), channel_id=1, source_target_pairs={{0,2},{1,3},{2,0},{3,1},{4,6},{5,7},{6,4},{7,5},{8,10},{9,11},{10,... | collective-permute-start | bytes 786440 | tf_op jit(solution)/shard_map/ppermute | solution.py:217
  291.3 96.6 %collective-permute-start.39 = (bf16[16,128,1024]{2,1,0:T(8,128)(2,1)}, bf16[16,128,1024]{2,1,0:T(8,128)(2,1)}, u32[]{:S(2)}, u32[]{:S(2)}) collective-permute-start(bf16[16,128,1024]{2,1,0:T(8,128)(2,1)} %slice.578), channel_id=1, source_target_pairs={{0,4},{4,0},{8,12},{12,8},{16,20},{20,16},{24,28},{28,24},{1,5},{5... | collective-permute-start | bytes 12582920 | tf_op jit(solution)/shard_map/ppermute | solution.py:217
  332.1 82.5 %collective-permute-start.4 = (bf16[16,256,512]{2,1,0:T(8,128)(2,1)}, bf16[16,256,512]{2,1,0:T(8,128)(2,1)}, u32[]{:S(2)}, u32[]{:S(2)}) collective-permute-start(bf16[16,256,512]{2,1,0:T(8,128)(2,1)} %slice.508), channel_id=1, source_target_pairs={{0,4},{4,0},{8,12},{12,8},{16,20},{20,16},{24,28},{28,24},{1,5},{5... | collective-permute-start | bytes 12582920 | tf_op jit(solution)/shard_map/ppermute | solution.py:217
  333.4 90.6 %collective-permute-start.9 = (bf16[16,128,1024]{2,1,0:T(8,128)(2,1)}, bf16[16,128,1024]{2,1,0:T(8,128)(2,1)}, u32[]{:S(2)}, u32[]{:S(2)}) collective-permute-start(bf16[16,128,1024]{2,1,0:T(8,128)(2,1)} %slice.518), channel_id=1, source_target_pairs={{0,4},{4,0},{8,12},{12,8},{16,20},{20,16},{24,28},{28,24},{1,5},{5... | collective-permute-start | bytes 12582920 | tf_op jit(solution)/shard_map/ppermute | solution.py:217
  374.5 36.5 %collective-permute-start.15 = (bf16[8,256,384]{2,1,0:T(8,128)(2,1)S(1)}, bf16[8,256,384]{2,1,0:T(8,128)(2,1)}, u32[]{:S(2)}, u32[]{:S(2)}) collective-permute-start(bf16[8,256,384]{2,1,0:T(8,128)(2,1)S(1)} %slice.530), channel_id=1, source_target_pairs={{0,2},{1,3},{2,0},{3,1},{4,6},{5,7},{6,4},{7,5},{8,10},{9,11},{10,... | collective-permute-start | bytes 4718600 | tf_op jit(solution)/shard_map/ppermute | solution.py:217
  376.9 52.2 %collective-permute-start.23 = (bf16[1,256,128]{2,1,0:T(8,128)(2,1)}, bf16[1,256,128]{2,1,0:T(8,128)(2,1)S(1)}, u32[]{:S(2)}, u32[]{:S(2)}) collective-permute-start(bf16[1,256,128]{2,1,0:T(8,128)(2,1)} %slice.546), channel_id=1, source_target_pairs={{0,16},{4,20},{8,24},{12,28},{16,0},{20,4},{24,8},{28,12},{1,17},{... | collective-permute-start | bytes 196616 | tf_op jit(solution)/shard_map/ppermute | solution.py:217
  387.9 76.2 %collective-permute-start.35 = (bf16[8,256,512]{2,1,0:T(8,128)(2,1)}, bf16[8,256,512]{2,1,0:T(8,128)(2,1)}, u32[]{:S(2)}, u32[]{:S(2)}) collective-permute-start(bf16[8,256,512]{2,1,0:T(8,128)(2,1)} %slice.570), channel_id=1, source_target_pairs={{0,1},{1,0},{2,3},{3,2},{4,5},{5,4},{6,7},{7,6},{8,9},{9,8},{10,11... | collective-permute-start | bytes 6291464 | tf_op jit(solution)/shard_map/ppermute | solution.py:217
  411.1 57.6 %collective-permute-start.40 = (bf16[8,128,1024]{2,1,0:T(8,128)(2,1)}, bf16[8,128,1024]{2,1,0:T(8,128)(2,1)}, u32[]{:S(2)}, u32[]{:S(2)}) collective-permute-start(bf16[8,128,1024]{2,1,0:T(8,128)(2,1)} %slice.580), channel_id=1, source_target_pairs={{0,2},{1,3},{2,0},{3,1},{4,6},{5,7},{6,4},{7,5},{8,10},{9,11},{10,... | collective-permute-start | bytes 6291464 | tf_op jit(solution)/shard_map/ppermute | solution.py:217
  414.6 38.9 %collective-permute-start.16 = (bf16[4,256,384]{2,1,0:T(8,128)(2,1)S(1)}, bf16[4,256,384]{2,1,0:T(8,128)(2,1)S(1)}, u32[]{:S(2)}, u32[]{:S(2)}) collective-permute-start(bf16[4,256,384]{2,1,0:T(8,128)(2,1)S(1)} %slice.532), channel_id=1, source_target_pairs={{0,1},{1,0},{2,3},{3,2},{4,5},{5,4},{6,7},{7,6},{8,9},{9,8},{10,11... | collective-permute-start | bytes 2359304 | tf_op jit(solution)/shard_map/ppermute | solution.py:217
  424.0 74.5 %collective-permute-start.5 = (bf16[8,256,512]{2,1,0:T(8,128)(2,1)S(1)}, bf16[8,256,512]{2,1,0:T(8,128)(2,1)S(1)}, u32[]{:S(2)}, u32[]{:S(2)}) collective-permute-start(bf16[8,256,512]{2,1,0:T(8,128)(2,1)S(1)} %slice.510), channel_id=1, source_target_pairs={{0,1},{1,0},{2,3},{3,2},{4,5},{5,4},{6,7},{7,6},{8,9},{9,8},{10,11... | collective-permute-start | bytes 6291464 | tf_op jit(solution)/shard_map/ppermute | solution.py:217
  429.1 25.2 %collective-permute-start.28 = (bf16[1,256,256]{2,1,0:T(8,128)(2,1)S(1)}, bf16[1,256,256]{2,1,0:T(8,128)(2,1)S(1)}, u32[]{:S(2)}, u32[]{:S(2)}) collective-permute-start(bf16[1,256,256]{2,1,0:T(8,128)(2,1)S(1)} %slice.556), channel_id=1, source_target_pairs={{0,16},{4,20},{8,24},{12,28},{16,0},{20,4},{24,8},{28,12},{1,17},{... | collective-permute-start | bytes 393224 | tf_op jit(solution)/shard_map/ppermute | solution.py:217
  453.6 51.2 %collective-permute-start.10 = (bf16[8,128,1024]{2,1,0:T(8,128)(2,1)S(1)}, bf16[8,128,1024]{2,1,0:T(8,128)(2,1)S(1)}, u32[]{:S(2)}, u32[]{:S(2)}) collective-permute-start(bf16[8,128,1024]{2,1,0:T(8,128)(2,1)S(1)} %slice.520), channel_id=1, source_target_pairs={{0,2},{1,3},{2,0},{3,1},{4,6},{5,7},{6,4},{7,5},{8,10},{9,11},{10,... | collective-permute-start | bytes 6291464 | tf_op jit(solution)/shard_map/ppermute | solution.py:217
  463.0 44.4 %collective-permute-start.18 = (bf16[1,256,384]{2,1,0:T(8,128)(2,1)S(1)}, bf16[1,256,384]{2,1,0:T(8,128)(2,1)S(1)}, u32[]{:S(2)}, u32[]{:S(2)}) collective-permute-start(bf16[1,256,384]{2,1,0:T(8,128)(2,1)S(1)} %slice.536), channel_id=1, source_target_pairs={{0,16},{4,20},{8,24},{12,28},{16,0},{20,4},{24,8},{28,12},{1,17},{... | collective-permute-start | bytes 589832 | tf_op jit(solution)/shard_map/ppermute | solution.py:217
  466.8 60.5 %collective-permute-start.36 = (bf16[4,256,512]{2,1,0:T(8,128)(2,1)S(1)}, bf16[4,256,512]{2,1,0:T(8,128)(2,1)S(1)}, u32[]{:S(2)}, u32[]{:S(2)}) collective-permute-start(bf16[4,256,512]{2,1,0:T(8,128)(2,1)S(1)} %slice.572), channel_id=1, source_target_pairs={{0,2},{1,3},{2,0},{3,1},{4,6},{5,7},{6,4},{7,5},{8,10},{9,11},{10,... | collective-permute-start | bytes 3145736 | tf_op jit(solution)/shard_map/ppermute | solution.py:217
  471.3 58.5 %collective-permute-start.41 = (bf16[4,128,1024]{2,1,0:T(8,128)(2,1)S(1)}, bf16[4,128,1024]{2,1,0:T(8,128)(2,1)S(1)}, u32[]{:S(2)}, u32[]{:S(2)}) collective-permute-start(bf16[4,128,1024]{2,1,0:T(8,128)(2,1)S(1)} %slice.582), channel_id=1, source_target_pairs={{0,1},{1,0},{2,3},{3,2},{4,5},{5,4},{6,7},{7,6},{8,9},{9,8},{10,11... | collective-permute-start | bytes 3145736 | tf_op jit(solution)/shard_map/ppermute | solution.py:217
  499.2 48.8 %collective-permute-start.6 = (bf16[4,256,512]{2,1,0:T(8,128)(2,1)S(1)}, bf16[4,256,512]{2,1,0:T(8,128)(2,1)S(1)}, u32[]{:S(2)}, u32[]{:S(2)}) collective-permute-start(bf16[4,256,512]{2,1,0:T(8,128)(2,1)S(1)} %slice.512), channel_id=1, source_target_pairs={{0,2},{1,3},{2,0},{3,1},{4,6},{5,7},{6,4},{7,5},{8,10},{9,11},{10,... | collective-permute-start | bytes 3145736 | tf_op jit(solution)/shard_map/ppermute | solution.py:217
  505.8 44.6 %collective-permute-start.11 = (bf16[4,128,1024]{2,1,0:T(8,128)(2,1)S(1)}, bf16[4,128,1024]{2,1,0:T(8,128)(2,1)S(1)}, u32[]{:S(2)}, u32[]{:S(2)}) collective-permute-start(bf16[4,128,1024]{2,1,0:T(8,128)(2,1)S(1)} %slice.522), channel_id=1, source_target_pairs={{0,1},{1,0},{2,3},{3,2},{4,5},{5,4},{6,7},{7,6},{8,9},{9,8},{10,11... | collective-permute-start | bytes 3145736 | tf_op jit(solution)/shard_map/ppermute | solution.py:217
  527.6 23.4 %collective-permute-start.37 = (bf16[2,256,512]{2,1,0:T(8,128)(2,1)S(1)}, bf16[2,256,512]{2,1,0:T(8,128)(2,1)S(1)}, u32[]{:S(2)}, u32[]{:S(2)}) collective-permute-start(bf16[2,256,512]{2,1,0:T(8,128)(2,1)S(1)} %slice.574), channel_id=1, source_target_pairs={{0,8},{4,12},{8,0},{12,4},{16,24},{20,28},{24,16},{28,20},{1,9},{5... | collective-permute-start | bytes 1572872 | tf_op jit(solution)/shard_map/ppermute | solution.py:217
  530.3 23.1 %collective-permute-start.42 = (bf16[2,128,1024]{2,1,0:T(8,128)(2,1)S(1)}, bf16[2,128,1024]{2,1,0:T(8,128)(2,1)S(1)}, u32[]{:S(2)}, u32[]{:S(2)}) collective-permute-start(bf16[2,128,1024]{2,1,0:T(8,128)(2,1)S(1)} %slice.584), channel_id=1, source_target_pairs={{0,8},{4,12},{8,0},{12,4},{16,24},{20,28},{24,16},{28,20},{1,9},{5... | collective-permute-start | bytes 1572872 | tf_op jit(solution)/shard_map/ppermute | solution.py:217
  548.3 27.3 %collective-permute-start.7 = (bf16[2,256,512]{2,1,0:T(8,128)(2,1)S(1)}, bf16[2,256,512]{2,1,0:T(8,128)(2,1)S(1)}, u32[]{:S(2)}, u32[]{:S(2)}) collective-permute-start(bf16[2,256,512]{2,1,0:T(8,128)(2,1)S(1)} %slice.514), channel_id=1, source_target_pairs={{0,8},{4,12},{8,0},{12,4},{16,24},{20,28},{24,16},{28,20},{1,9},{5... | collective-permute-start | bytes 1572872 | tf_op jit(solution)/shard_map/ppermute | solution.py:217
  550.9 33.9 %collective-permute-start.12 = (bf16[2,128,1024]{2,1,0:T(8,128)(2,1)S(1)}, bf16[2,128,1024]{2,1,0:T(8,128)(2,1)S(1)}, u32[]{:S(2)}, u32[]{:S(2)}) collective-permute-start(bf16[2,128,1024]{2,1,0:T(8,128)(2,1)S(1)} %slice.524), channel_id=1, source_target_pairs={{0,8},{4,12},{8,0},{12,4},{16,24},{20,28},{24,16},{28,20},{1,9},{5... | collective-permute-start | bytes 1572872 | tf_op jit(solution)/shard_map/ppermute | solution.py:217
  551.2 34.8 %collective-permute-start.38 = (bf16[1,256,512]{2,1,0:T(8,128)(2,1)S(1)}, bf16[1,256,512]{2,1,0:T(8,128)(2,1)S(1)}, u32[]{:S(2)}, u32[]{:S(2)}) collective-permute-start(bf16[1,256,512]{2,1,0:T(8,128)(2,1)S(1)} %slice.576), channel_id=1, source_target_pairs={{0,16},{4,20},{8,24},{12,28},{16,0},{20,4},{24,8},{28,12},{1,17},{... | collective-permute-start | bytes 786440 | tf_op jit(solution)/shard_map/ppermute | solution.py:217
  553.6 33.2 %collective-permute-start.43 = (bf16[1,128,1024]{2,1,0:T(8,128)(2,1)S(1)}, bf16[1,128,1024]{2,1,0:T(8,128)(2,1)S(1)}, u32[]{:S(2)}, u32[]{:S(2)}) collective-permute-start(bf16[1,128,1024]{2,1,0:T(8,128)(2,1)S(1)} %slice.586), channel_id=1, source_target_pairs={{0,16},{4,20},{8,24},{12,28},{16,0},{20,4},{24,8},{28,12},{1,17},{... | collective-permute-start | bytes 786440 | tf_op jit(solution)/shard_map/ppermute | solution.py:217
  575.8 26.0 %collective-permute-start.8 = (bf16[1,256,512]{2,1,0:T(8,128)(2,1)S(1)}, bf16[1,256,512]{2,1,0:T(8,128)(2,1)S(1)}, u32[]{:S(2)}, u32[]{:S(2)}) collective-permute-start(bf16[1,256,512]{2,1,0:T(8,128)(2,1)S(1)} %slice.516), channel_id=1, source_target_pairs={{0,16},{4,20},{8,24},{12,28},{16,0},{20,4},{24,8},{28,12},{1,17},{... | collective-permute-start | bytes 786440 | tf_op jit(solution)/shard_map/ppermute | solution.py:217
  585.0 20.9 %collective-permute-start.13 = (bf16[1,128,1024]{2,1,0:T(8,128)(2,1)S(1)}, bf16[1,128,1024]{2,1,0:T(8,128)(2,1)S(1)}, u32[]{:S(2)}, u32[]{:S(2)}) collective-permute-start(bf16[1,128,1024]{2,1,0:T(8,128)(2,1)S(1)} %slice.526), channel_id=1, source_target_pairs={{0,16},{4,20},{8,24},{12,28},{16,0},{20,4},{24,8},{28,12},{1,17},{... | collective-permute-start | bytes 786440 | tf_op jit(solution)/shard_map/ppermute | solution.py:217
  (91 other events, 1835.4 us)

commit v3 on v2

--- a/solution.py
+++ b/solution.py
@@ -550,6 +550,208 @@
     return out
 
 
+def flipped(index, places):
+    for bit, flip in places:
+        mine = lax.rem(index // (1 << bit), 2)
+        index = index + flip * (1 - 2 * mine) * (1 << bit)
+    return index
+
+
+def place_of(place, steps, axis, index):
+    flips = []
+    for order, (name, bit) in enumerate(steps):
+        if name == axis:
+            flips.append((bit, lax.rem(place // (1 << (len(steps) - 1 - order)), 2)))
+    return flipped(index, flips)
+
+
+def scatter_kernel(jobs, *refs):
+    count = len(jobs)
+    inputs, outs, scratch = refs[: 2 * count], refs[2 * count : 3 * count], refs[3 * count :]
+    s, b = lax.axis_index("seq"), lax.axis_index("batch")
+    core = lax.rem(b, 2)
+    sibling = (b + 1 - 2 * core, s)
+
+    def partner(step):
+        axis, bit = step
+        if axis == "seq":
+            return (b, flipped(s, [(bit, 1)]))
+        return (flipped(b, [(bit, 1)]), s)
+
+    peers = [sibling] + [partner(step) for step in sorted(jobs[0].steps)]
+    barrier = pltpu.get_barrier_semaphore()
+    for peer in peers:
+        pl.semaphore_signal(barrier, inc=1, device_id=peer, device_id_type=MESH)
+    pl.semaphore_wait(barrier, len(peers))
+
+    works = []
+    for i, job in enumerate(jobs):
+        small_in, big_in = inputs[2 * i : 2 * i + 2]
+        small, big, sending, arrived, local, moves, lands, sends, recvs = scratch[9 * i : 9 * i + 9]
+        frames = small_in.shape[0]
+        span = big_in.shape[1] // job.batches
+        own_rows, far_rows = pl.ds(0, frames), pl.ds(frames, frames)
+        pieces = [(small_in, small.at[own_rows], small_in, small.at[far_rows])]
+        for z in range(job.batches // 2):
+            here = pl.ds(pl.multiple_of((2 * z + core) * span, 128), span)
+            there = pl.ds(pl.multiple_of((2 * z + 1 - core) * span, 128), span)
+            inside = pl.ds(z * span, span)
+            pieces.append(
+                (
+                    big_in.at[:, here],
+                    big.at[own_rows, inside],
+                    big_in.at[:, there],
+                    big.at[far_rows, inside],
+                )
+            )
+        near, far = [], []
+        for n, (own_source, own_place, far_source, far_place) in enumerate(pieces):
+            near.append(pltpu.make_async_copy(own_source, own_place, local.at[n]))
+            far.append(
+                pltpu.make_async_remote_copy(
+                    src_ref=far_source,
+                    dst_ref=far_place,
+                    send_sem=moves.at[n],
+                    recv_sem=lands.at[n],
+                    device_id=sibling,
+                    device_id_type=MESH,
+                )
+            )
+            far[-1].start()
+            near[-1].start()
+        works.append((near, far))
+
+    def copy_of(i, place, step):
+        sending, arrived, sends, recvs = (scratch[9 * i + j] for j in (2, 3, 7, 8))
+        return pltpu.make_async_remote_copy(
+            src_ref=sending.at[place - 1],
+            dst_ref=arrived.at[place - 1],
+            send_sem=sends.at[place - 1],
+            recv_sem=recvs.at[place - 1],
+            device_id=partner(step),
+            device_id_type=MESH,
+        )
+
+    def block_sum(i, place, level):
+        job = jobs[i]
+        small, big, arrived = (scratch[9 * i + j] for j in (0, 1, 3))
+        span = big.shape[1] // (job.batches // 2)
+        row = place_of(place, job.steps, "seq", s)
+        col = place_of(place, job.steps, "batch", b) // 2
+        if job.tall:
+            left = big[:, pl.ds(pl.multiple_of(col * span + row * job.rows, 128), job.rows)]
+            right = small[...]
+        else:
+            left = small[:, pl.ds(pl.multiple_of(row * job.rows, 128), job.rows)]
+            right = big[:, pl.ds(pl.multiple_of(col * span, 128), span)]
+        total = lax.dot_general(
+            left, right, (((0,), (0,)), ((), ())), preferred_element_type=jnp.float32
+        )
+        levels = len(job.steps)
+        for m in range(levels - 1, level, -1):
+            copy_of(i, (1 << m) + place, job.steps[levels - 1 - m]).wait_recv()
+            total = total + arrived[(1 << m) + place - 1].astype(jnp.float32)
+        return total
+
+    levels = len(jobs[0].steps)
+    for level in range(levels - 1, -1, -1):
+
+        def one_place(j, carry, level=level):
+            place = (2 << level) - 1 - j
+            for i, job in enumerate(jobs):
+                if level == levels - 1:
+
+                    @pl.when(j == 0)
+                    def _():
+                        for copy in works[i][0]:
+                            copy.wait()
+                        for copy in works[i][1]:
+                            copy.wait_recv()
+
+                scratch[9 * i + 2][place - 1] = block_sum(i, place, level).astype(jnp.bfloat16)
+                copy_of(i, place, job.steps[levels - 1 - level]).start()
+            return carry
+
+        lax.fori_loop(0, 1 << level, one_place, 0)
+    for i in range(count):
+        outs[i][...] = block_sum(i, 0, -1)
+    for i, (near, far) in enumerate(works):
+        for copy in far:
+            copy.wait_send()
+        for level in range(levels - 1, -1, -1):
+
+            def one_wait(j, carry, level=level, i=i):
+                copy_of(i, (1 << level) + j, jobs[i].steps[levels - 1 - level]).wait_send()
+                return carry
+
+            lax.fori_loop(0, 1 << level, one_wait, 0)
+
+
+class Job:
+    def __init__(self, small, big, tall, order):
+        self.small, self.big, self.tall = small, big, tall
+        self.batches, groups = lax.axis_size("batch"), lax.axis_size("seq")
+        seq_bits = [("seq", k) for k in range(groups.bit_length() - 1)]
+        batch_bits = [("batch", k) for k in range(1, self.batches.bit_length() - 1)]
+        self.order = order
+        if order == "x":
+            self.steps = seq_bits + batch_bits
+        elif order == "y":
+            self.steps = seq_bits[::-1] + batch_bits
+        else:
+            self.steps = batch_bits[:1] + seq_bits + batch_bits[1:]
+        if tall:
+            self.rows = big.shape[1] // (self.batches * groups)
+            self.cols = small.shape[1]
+        else:
+            self.rows = small.shape[1] // groups
+            self.cols = big.shape[1] // self.batches
+
+    def fits(self):
+        return self.rows % 128 == 0 and self.cols % 128 == 0
+
+
+def scatter_sums(jobs, collective_id):
+    if not all(job.fits() for job in jobs):
+        return [
+            owned_sum(
+                *((job.big, job.small) if job.tall else (job.small, job.big)),
+                job.tall,
+                job.order == "y",
+            )
+            for job in jobs
+        ]
+    scratch, operands, flops = [], [], 0
+    for job in jobs:
+        frames = job.small.shape[0]
+        places = 1 << len(job.steps)
+        pieces = 1 + job.batches // 2
+        scratch += [
+            pltpu.VMEM((2 * frames, job.small.shape[1]), jnp.bfloat16),
+            pltpu.VMEM((2 * frames, job.big.shape[1] // 2), jnp.bfloat16),
+            pltpu.VMEM((places - 1, job.rows, job.cols), jnp.bfloat16),
+            pltpu.VMEM((places - 1, job.rows, job.cols), jnp.bfloat16),
+            pltpu.SemaphoreType.DMA((pieces,)),
+            pltpu.SemaphoreType.DMA((pieces,)),
+            pltpu.SemaphoreType.DMA((pieces,)),
+            pltpu.SemaphoreType.DMA((places - 1,)),
+            pltpu.SemaphoreType.DMA((places - 1,)),
+        ]
+        operands += [job.small, job.big]
+        flops += 2 * frames * job.small.shape[1] * job.big.shape[1]
+    return pl.pallas_call(
+        functools.partial(scatter_kernel, jobs),
+        out_shape=[jax.ShapeDtypeStruct((job.rows, job.cols), jnp.float32) for job in jobs],
+        in_specs=[pl.BlockSpec(memory_space=pl.ANY)] * len(operands),
+        out_specs=[pl.BlockSpec(memory_space=pltpu.VMEM)] * len(jobs),
+        scratch_shapes=scratch,
+        compiler_params=pltpu.CompilerParams(
+            collective_id=collective_id, has_side_effects=True, vmem_limit_bytes=56 << 20
+        ),
+        cost_estimate=pl.CostEstimate(flops=flops, bytes_accessed=flops // 512, transcendentals=0),
+    )(*operands)
+
+
 def shards(
     frames_in,
     cotangent,
@@ -706,6 +908,24 @@
     gain_grads = jnp.stack(
         [grad_gain_zero, grad_gain_one, grad_gain_two, grad_gain_three, grad_gain_four], axis=0
     )
+    middle = scatter_sums(
+        [
+            Job(*ffn2_up_pair, False, "x"),
+            Job(*ffn2_down_pair[::-1], True, "y"),
+            Job(conv_in, grad_gl, False, "z"),
+            Job(attn_out, grad_r, False, "z"),
+            Job(conv_act, grad_r2, False, "z"),
+        ],
+        6,
+    )
+    last = scatter_sums(
+        [
+            Job(*ffn1_up_pair, False, "x"),
+            Job(*ffn1_down_pair[::-1], True, "y"),
+            Job(attn_in, grad_qkv, False, "z"),
+        ],
+        7,
+    )
     small_rows = jnp.concatenate([gain_grads, cond_grad_rows, kernel_grads], axis=0)
     small_sums = sum_everywhere(small_rows, 3)
     seq_width = model_width // groups
@@ -718,17 +938,17 @@
         grad_zero.astype(jnp.bfloat16)[None],
         small_piece[5:cond_end],
         small_piece[0:5],
-        owned_sum(*ffn1_up_pair, False, False),
-        owned_sum(*ffn1_down_pair, True, True),
-        owned_sum(attn_in, grad_qkv, False, True),
-        owned_sum(attn_out, grad_r, False, False),
-        owned_sum(conv_in, grad_gl, False, True),
+        last[0],
+        last[1],
+        last[2],
+        middle[3],
+        middle[2],
         small_piece[cond_end : cond_end + taps],
         gradient_normalized_sum,
         gradient_sum_total,
-        owned_sum(conv_act, grad_r2, False, False),
-        owned_sum(*ffn2_up_pair, False, False),
-        owned_sum(*ffn2_down_pair, True, True),
+        middle[4],
+        middle[0],
+        middle[1],
         new_mean,
         new_var,
     )

time: 616 us -> 478 us (0.78)
  Pallas kernels: 160 us -> 350 us
  waiting for transfers between devices: 188 us -> 3 us
  other arithmetic: 81.9 us -> 26.5 us
  starting transfers between devices: 57.8 us -> 11 us
  local copies, waits for them, and re-layouts: 42.9 us -> 18.5 us
  matrix products: 72.6 us -> 57.2 us
    pallas_call x8 -> x2, Pallas kernels: 34.4 us -> 226 us  [scatter_sums(): pl.pallas_call(functools.partial(scatter_kernel, jobs), out_shape=[jax.Sh...]
    ppermute x40 -> x0, waiting for transfers between devices: 188 us -> none  [owned_sum(): arrived = lax.ppermute(blocks[half:], axis, pairs)]
    convert_element_type x32 -> x0, other arithmetic: 46.2 us -> none  [owned_sum(): blocks = total.astype(jnp.bfloat16) if half > 1 else total]
    ppermute x40 -> x0, starting transfers between devices: 45.8 us -> none  [owned_sum(): arrived = lax.ppermute(blocks[half:], axis, pairs)]
    slice x40 -> x0, local copies, waits for them, and re-layouts: 26.4 us -> none  [owned_sum(): arrived = lax.ppermute(blocks[half:], axis, pairs)]
    dot_general x8, matrix products: 47.5 us -> 27.1 us  [times_transposed(): lax.dot_general(left_side, weight, (((1,), (1,)), ((), ())), preferred_el...]
    squeeze x8 -> x0, other arithmetic: 6.32 us -> none  [owned_sum(): return blocks[0]]
    unnamed x158 -> x120, local copies, waits for them, and re-layouts: 10 us -> 14.4 us
  transfers between devices with their start and end apart: 44 -> 4, of which waited for: 16 -> 1; matrix products, arithmetic and copies ran while one was open for 19% -> 1% of each run, Pallas kernels for 16% -> 0%
where the time goes in v3:
time: 478 us; the launch traced here: 470 us
  Pallas kernels  350 us (73%)
  matrix products  57.2 us (12%)
  other arithmetic  26.5 us (6%)
  local copies, waits for them, and re-layouts  18.5 us (4%)
  starting transfers between devices  11 us (2%)
    pallas_call x2, Pallas kernels, scatter_sums(): pl.pallas_call(functools.partial(scatter_kernel, jobs), out_shape=[jax.Sh...  226 us
    pallas_call x1, Pallas kernels, attend_back(): pl.pallas_call(functools.partial(attend_back_kernel, groups, heads), out_...  45.8 us
    pallas_call x3, Pallas kernels, sum_everywhere(): pl.pallas_call(functools.partial(sum_kernel, groups, batches), out_shape=...  43.1 us
    pallas_call x1, Pallas kernels, attend(): pl.pallas_call(functools.partial(attend_kernel, groups, heads), out_shape...  35.7 us
    dot_general x8, matrix products, times_transposed(): lax.dot_general(left_side, weight, (((1,), (1,)), ((), ())), preferred_el...  27.1 us
    dot_general x2, matrix products, ffn_forward(): hidden = jnp.dot(lowered, up_weight, preferred_element_type=jnp.float32)  16.2 us
    unnamed x120, local copies, waits for them, and re-layouts  14.4 us
  transfers between devices with their start and end apart: 4, of which 1 were waited for; matrix products, arithmetic and copies ran while one was open for 1% of the time, Pallas kernels for 0%

profile of v3, /device:TPU:0, one launch (start us, length us, event | category | flops | bytes accessed | tf_op | source)
XLA Modules:
  0.0 470.1 jit_solution(1667579251454764956)
XLA Ops:
  4.7 1.3 fusion.21
  6.0 1.4 multiply_reduce_fusion.16
  7.5 1.5 multiply_convert_fusion.13.refs_0_
  9.0 8.0 %multiply_convert_fusion.1 = (bf16[256,4096]{1,0:T(8,128)(2,1)S(1)}, f32[256,4096]{1,0:T(8,128)}) fusion(bf16[256,1024]{1,0:T(8,128)(2,1)S(1)} %multiply_convert_fusion.13.refs_0_, bf16[1024,4096]{1,0:T(8,128)(2,1)} %param.27), kind=kOutput, calls=%fused_computation.8 | convolution fusion | flops 2152726528 | bytes 15204352 | tf_op jit(solution)/shard_map/dot_general | solution.py:58
  17.0 2.6 fusion.52
  22.2 4.6 fusion.56.qkv_ref
  28.0 35.7 %shard_map.323 = (bf16[1024,768]{1,0:T(8,128)(2,1)S(1)}, bf16[256,1024]{1,0:T(8,128)(2,1)S(1)}) custom-call(s32[1]{0:T(128)} %dynamic_slice.6.length_ref, f32[256,3072]{1,0:T(8,128)S(1)} %fusion.56.qkv_ref, f32[3,256,128]{2,1,0:T(8,128)S(1)} %pad_maximum_fusion.7.cos_ref, f32[3,256,128]{2,1,0:T(8,128)S(1)} %pad_maximum_fusion.8.sin_ref), custom_call_target="tpu_custom_call" | custom-call | flops 1073741824 | bytes 5242880 | tf_op jit(solution)/shard_map/pallas_call | solution.py:358
  70.0 5.4 %collective-permute-start = (bf16[2,1024]{1,0:T(2,128)(2,1)S(1)}, bf16[2,1024]{1,0:T(2,128)(2,1)S(1)}, u32[]{:S(2)}, u32[]{:S(2)}) collective-permute-start(bf16[2,1024]{1,0:T(2,128)(2,1)S(1)} %get-tuple-element.89), channel_id=1, source_target_pairs={{0,1},{1,2},{2,3},{4,5},{5,6},{6,7},{8,9},{9,10},{10,11},{12,13},{... | collective-permute-start | bytes 12296 | tf_op jit(solution)/shard_map/ppermute | solution.py:28
  75.5 1.9 multiply_sine_fusion
  79.7 3.2 multiply_reduce_fusion.13
  82.9 11.6 %shard_map.324 = f32[2,1024]{1,0:T(2,128)S(1)} custom-call(f32[2,1024]{1,0:T(2,128)S(1)} %pad_maximum_fusion.9.rows_ref), custom_call_target="tpu_custom_call" | custom-call | tf_op jit(solution)/shard_map/pallas_call | solution.py:113
  94.9 2.2 fusion.54
  97.7 8.2 %multiply_convert_fusion = (bf16[256,4096]{1,0:T(8,128)(2,1)S(1)}, f32[256,4096]{1,0:T(8,128)}) fusion(bf16[256,1024]{1,0:T(8,128)(2,1)S(1)} %multiply_convert_fusion.8.refs_0_, bf16[1024,4096]{1,0:T(8,128)(2,1)} %param.36), kind=kOutput, calls=%fused_computation.6 | convolution fusion | flops 2152726528 | bytes 15204352 | tf_op jit(solution)/shard_map/dot_general | solution.py:58
  105.9 2.4 fusion.55
  110.5 5.5 %fusion.3.refs_1_ = bf16[256,4096]{1,0:T(8,128)(2,1)S(1)} fusion(bf16[256,1024]{1,0:T(8,128)(2,1)S(1)} %multiply_convert_fusion.6.refs_2_, bf16[4096,1024]{1,0:T(8,128)(2,1)S(1)} %bitcast.190, f32[256,4096]{1,0:T(8,128)} %get-tuple-element.124), kind=kOutput, calls=%fused_computation.5 | convolution fusion | flops 2156920832 | bytes 15204352 | tf_op jit(solution)/shard_map/dot_general | solution.py:50
  116.0 6.8 %multiply_reduce_fusion.1 = (f32[1024]{0:T(1024)S(1)}, f32[256]{0:T(256)S(1)}, f32[256,1024]{1,0:T(8,128)S(1)}) fusion(f32[256,1024]{1,0:T(8,128)S(1)} %get-tuple-element.122, f32[256]{0:T(256)S(1)} %fusion.36, f32[256]{0:T(256)S(1)} %broadcast_multiply_fusion.5, f32[1024]{0:T(1024)S(1)} %bitcast.154, bf16[256,4096]{1,0:T(8,128)(2,1)S(1)} %fusion.3.refs_1_, ...), kind=kOutput, calls=%fused_computation.48 | convolution fusion | flops 2149317376 | bytes 12594176 | tf_op jit(solution)/shard_map/dot_general | solution.py:50
  124.7 9.2 %shard_map.325 = f32[2,1024]{1,0:T(2,128)S(1)} custom-call(f32[2,1024]{1,0:T(2,128)S(1)} %pad_maximum_fusion.10.rows_ref), custom_call_target="tpu_custom_call" | custom-call | tf_op jit(solution)/shard_map/pallas_call | solution.py:113
  135.0 3.0 collective-permute-start.3
  138.0 1.3 collective-permute-start.2
  140.5 3.0 collective-permute-done.2
  144.9 1.6 multiply_reduce_fusion.2
  148.8 45.8 %shard_map.326.refs_5_ = bf16[256,3072]{1,0:T(8,128)(2,1)S(1)} custom-call(s32[1]{0:T(128)} %dynamic_slice.6.length_ref, bf16[1024,768]{1,0:T(8,128)(2,1)S(1)} %copy-done.5, bf16[256,1024]{1,0:T(8,128)(2,1)S(1)} %convolution_convert_fusion.grad_ref, f32[1024,128]{1,0:T(8,128)S(1)} %pad_maximum_fusion.5.cos_ref, f32[1024,128]{1,0:T(8,128)S(1)} %pad_maximum_fusion.6.sin_ref), custom_call_target="tpu_custom_call" | custom-call | flops 2684354560 | bytes 4194304 | tf_op jit(solution)/shard_map/pallas_call | solution.py:522
  194.6 2.1 multiply_reduce_fusion.3
  197.5 1.6 copy-done.47
  199.1 6.6 %fusion.2.refs_1_ = bf16[256,4096]{1,0:T(8,128)(2,1)S(1)} fusion(bf16[256,1024]{1,0:T(8,128)(2,1)S(1)} %get-tuple-element.67.refs_2_, bf16[4096,1024]{1,0:T(8,128)(2,1)} %param.28, f32[256,4096]{1,0:T(8,128)S(1)} %copy-done.47), kind=kOutput, calls=%fused_computation.4 | convolution fusion | flops 2156920832 | bytes 15204352 | tf_op jit(solution)/shard_map/dot_general | solution.py:50
  205.8 2.7 multiply_reduce_fusion.4
  208.5 106.5 %shard_map.328 = (f32[256,512]{1,0:T(8,128)}, f32[128,1024]{1,0:T(8,128)}, f32[256,384]{1,0:T(8,128)}) custom-call(bf16[256,1024]{1,0:T(8,128)(2,1)} %copy-done.23, bf16[256,4096]{1,0:T(8,128)(2,1)} %copy-done.44, bf16[256,1024]{1,0:T(8,128)(2,1)} %copy-done.22, bf16[256,4096]{1,0:T(8,128)(2,1)} %copy-done.46, bf16[256,1024]{1,0:T(8,128)(2,1)} %copy-done.25, ...), custom_call_target="tpu_custom_call" | custom-call | flops 5905580032 | bytes 11534336 | tf_op jit(solution)/shard_map/pallas_call | solution.py:742
  318.0 22.3 %shard_map.327 = f32[23,1024]{1,0:T(8,128)S(1)} custom-call(f32[23,1024]{1,0:T(8,128)S(1)} %concatenate.82.rows_ref), custom_call_target="tpu_custom_call" | custom-call | tf_op jit(solution)/shard_map/pallas_call | solution.py:113
  341.8 119.3 %shard_map.329 = (f32[256,512]{1,0:T(8,128)}, f32[128,1024]{1,0:T(8,128)}, f32[256,256]{1,0:T(8,128)}, f32[256,128]{1,0:T(8,128)}, f32[256,128]{1,0:T(8,128)}) custom-call(bf16[256,1024]{1,0:T(8,128)(2,1)} %copy-done.26, bf16[256,4096]{1,0:T(8,128)(2,1)} %copy-done.43, bf16[256,1024]{1,0:T(8,128)(2,1)} %copy-done.31, bf16[256,4096]{1,0:T(8,128)(2,1)} %copy-done.45, ...), custom_call_target="tpu_custom_call" | custom-call | flops 6442450944 | bytes 12582912 | tf_op jit(solution)/shard_map/pallas_call | solution.py:742
  463.5 1.6 copy.84
  465.0 1.7 copy.85
  466.7 1.6 copy.86
  (215 shorter events, 34.6 us)
Async XLA Ops:
  0.7 94.2 %copy-start = (bf16[1024,1024]{1,0:T(8,128)(2,1)S(1)}, bf16[1024,1024]{1,0:T(8,128)(2,1)}, u32[]{:S(2)}) copy-start(bf16[1024,1024]{1,0:T(8,128)(2,1)} %param.35) | copy-start | bytes 6291460
  7.4 9.6 %slice-start.2 = ((s8[8388608]{0:T(1024)(128)(4,1)}), s8[4194304]{0:T(1024)(128)(4,1)S(1)}, s32[]{:S(2)}) async-start(s8[8388608]{0:T(1024)(128)(4,1)} %bitcast.191), calls=%async_computation.2 | async-start | bytes 8388608
  19.6 44.1 %copy-start.8 = (f32[256,1024]{1,0:T(8,128)}, f32[256,1024]{1,0:T(8,128)S(1)}, u32[]{:S(2)}) copy-start(f32[256,1024]{1,0:T(8,128)S(1)} %get-tuple-element.118) | copy-start | bytes 3145732
  27.9 35.8 %copy-start.17 = (bf16[1024,1024]{1,0:T(8,128)(2,1)S(1)}, bf16[1024,1024]{1,0:T(8,128)(2,1)}, u32[]{:S(2)}) copy-start(bf16[1024,1024]{1,0:T(8,128)(2,1)} %param.30) | copy-start | bytes 6291460
  67.0 8.5 %copy-start.33 = (bf16[5,1024]{1,0:T(8,128)(2,1)S(1)}, bf16[5,1024]{1,0:T(8,128)(2,1)}, u32[]{:S(2)}) copy-start(bf16[5,1024]{1,0:T(8,128)(2,1)} %param.32) | copy-start | bytes 30724
  68.3 9.8 %copy-start.10 = (f32[256,2048]{1,0:T(8,128)}, f32[256,2048]{1,0:T(8,128)S(1)}, u32[]{:S(2)}) copy-start(f32[256,2048]{1,0:T(8,128)S(1)} %fusion.57) | copy-start | bytes 6291460
  68.4 10.6 %copy-start.39 = (bf16[1024]{0:T(1024)(128)(2,1)S(1)}, bf16[1024]{0:T(1024)(128)(2,1)}, u32[]{:S(2)}) copy-start(bf16[1024]{0:T(1024)(128)(2,1)} %param.34) | copy-start | bytes 6148
  68.4 10.6 %copy-start.36 = (bf16[1024]{0:T(1024)(128)(2,1)S(1)}, bf16[1024]{0:T(1024)(128)(2,1)}, u32[]{:S(2)}) copy-start(bf16[1024]{0:T(1024)(128)(2,1)} %param.33) | copy-start | bytes 6148
  68.7 9.4 %copy-start.14 = (bf16[256,1024]{1,0:T(8,128)(2,1)}, bf16[256,1024]{1,0:T(8,128)(2,1)S(1)}, u32[]{:S(2)}) copy-start(bf16[256,1024]{1,0:T(8,128)(2,1)S(1)} %multiply_convert_fusion.10) | copy-start | bytes 1572868
  68.7 10.9 %collective-permute-start.1 = (bf16[2,1024]{1,0:T(2,128)(2,1)S(1)}, bf16[2,1024]{1,0:T(2,128)(2,1)S(1)}, u32[]{:S(2)}, u32[]{:S(2)}) collective-permute-start(bf16[2,1024]{1,0:T(2,128)(2,1)S(1)} %get-tuple-element.90), channel_id=1, source_target_pairs={{1,0},{2,1},{3,2},{5,4},{6,5},{7,6},{9,8},{10,9},{11,10},{13,12},{... | collective-permute-start | bytes 12296 | tf_op jit(solution)/shard_map/ppermute | solution.py:29
  70.0 9.6 %collective-permute-start = (bf16[2,1024]{1,0:T(2,128)(2,1)S(1)}, bf16[2,1024]{1,0:T(2,128)(2,1)S(1)}, u32[]{:S(2)}, u32[]{:S(2)}) collective-permute-start(bf16[2,1024]{1,0:T(2,128)(2,1)S(1)} %get-tuple-element.89), channel_id=1, source_target_pairs={{0,1},{1,2},{2,3},{4,5},{5,6},{6,7},{8,9},{9,10},{10,11},{12,13},{... | collective-permute-start | bytes 12296 | tf_op jit(solution)/shard_map/ppermute | solution.py:28
  94.9 11.0 %copy-start.16 = (bf16[256,1024]{1,0:T(8,128)(2,1)}, bf16[256,1024]{1,0:T(8,128)(2,1)S(1)}, u32[]{:S(2)}) copy-start(bf16[256,1024]{1,0:T(8,128)(2,1)S(1)} %multiply_convert_fusion.9.refs_8_) | copy-start | bytes 1572868
  97.1 8.8 %slice-start = ((s8[8388608]{0:T(1024)(128)(4,1)}), s8[4194304]{0:T(1024)(128)(4,1)S(1)}, s32[]{:S(2)}) async-start(s8[8388608]{0:T(1024)(128)(4,1)} %bitcast.189), calls=%async_computation | async-start | bytes 8388608
  123.4 10.5 %copy-start.15 = (bf16[256,1024]{1,0:T(8,128)(2,1)S(1)}, bf16[256,1024]{1,0:T(8,128)(2,1)}, u32[]{:S(2)}) copy-start(bf16[256,1024]{1,0:T(8,128)(2,1)} %copy-done.14) | copy-start | bytes 1572868
  123.4 15.9 %copy-start.37 = (f32[1024]{0:T(1024)S(1)}, f32[1024]{0:T(1024)}, u32[]{:S(2)}) copy-start(f32[1024]{0:T(1024)} %param.38) | copy-start | bytes 12292
  123.4 16.5 %copy-start.38 = (f32[1024]{0:T(1024)S(1)}, f32[1024]{0:T(1024)}, u32[]{:S(2)}) copy-start(f32[1024]{0:T(1024)} %param.39) | copy-start | bytes 12292
  123.5 20.1 %copy-start.11 = (f32[256,2048]{1,0:T(8,128)S(1)}, f32[256,2048]{1,0:T(8,128)}, u32[]{:S(2)}) copy-start(f32[256,2048]{1,0:T(8,128)} %copy-done.10) | copy-start | bytes 6291460
  133.8 11.0 %copy-start.34 = (f32[1,1024]{1,0:T(1,128)}, f32[1,1024]{1,0:T(1,128)S(1)}, u32[]{:S(2)}) copy-start(f32[1,1024]{1,0:T(1,128)S(1)} %get-tuple-element.109) | copy-start | bytes 12292
  133.9 11.0 %copy-start.35 = (f32[1,1024]{1,0:T(1,128)}, f32[1,1024]{1,0:T(1,128)S(1)}, u32[]{:S(2)}) copy-start(f32[1,1024]{1,0:T(1,128)S(1)} %get-tuple-element.110) | copy-start | bytes 12292
  135.0 9.9 %copy-start.7 = (f32[256,1024]{1,0:T(8,128)S(1)}, f32[256,1024]{1,0:T(8,128)}, u32[]{:S(2)}) copy-start(f32[256,1024]{1,0:T(8,128)} %copy-done.6) | copy-start | bytes 3145732
  135.0 9.9 %copy-start.41 = (bf16[1024,2048]{1,0:T(8,128)(2,1)S(1)}, bf16[1024,2048]{1,0:T(8,128)(2,1)}, u32[]{:S(2)}) copy-start(bf16[1024,2048]{1,0:T(8,128)(2,1)} %param.31) | copy-start | bytes 12582916
  135.0 5.5 %collective-permute-start.3 = (bf16[2,1024]{1,0:T(2,128)(2,1)S(1)}, bf16[2,1024]{1,0:T(2,128)(2,1)S(1)}, u32[]{:S(2)}, u32[]{:S(2)}) collective-permute-start(bf16[2,1024]{1,0:T(2,128)(2,1)S(1)} %get-tuple-element.88), channel_id=1, source_target_pairs={{0,1},{1,2},{2,3},{4,5},{5,6},{6,7},{8,9},{9,10},{10,11},{12,13},{... | collective-permute-start | bytes 12296 | tf_op jit(solution)/shard_map/ppermute | solution.py:28
  138.0 5.5 %collective-permute-start.2 = (bf16[2,1024]{1,0:T(2,128)(2,1)S(1)}, bf16[2,1024]{1,0:T(2,128)(2,1)S(1)}, u32[]{:S(2)}, u32[]{:S(2)}) collective-permute-start(bf16[2,1024]{1,0:T(2,128)(2,1)S(1)} %get-tuple-element.87), channel_id=1, source_target_pairs={{1,0},{2,1},{3,2},{5,4},{6,5},{7,6},{9,8},{10,9},{11,10},{13,12},{... | collective-permute-start | bytes 12296 | tf_op jit(solution)/shard_map/ppermute | solution.py:29
  148.0 46.6 %slice-start.6 = ((s8[6291456]{0:T(1024)(128)(4,1)}), s8[4194304]{0:T(1024)(128)(4,1)S(1)}, s32[]{:S(2)}) async-start(s8[6291456]{0:T(1024)(128)(4,1)} %bitcast.195), calls=%async_computation.6 | async-start | bytes 8388608
  148.8 45.8 %copy-start.9 = (f32[256,1024]{1,0:T(8,128)S(1)}, f32[256,1024]{1,0:T(8,128)}, u32[]{:S(2)}) copy-start(f32[256,1024]{1,0:T(8,128)} %copy-done.8) | copy-start | bytes 3145732
  148.8 45.8 %slice-start.7 = ((s8[6291456]{0:T(1024)(128)(4,1)}), s8[2097152]{0:T(1024)(128)(4,1)S(1)}, s32[]{:S(2)}) async-start(s8[6291456]{0:T(1024)(128)(4,1)} %bitcast.195), calls=%async_computation.7 | async-start | bytes 4194304
  197.2 8.6 %slice-start.4 = ((s8[8388608]{0:T(1024)(128)(4,1)}), s8[4194304]{0:T(1024)(128)(4,1)S(1)}, s32[]{:S(2)}) async-start(s8[8388608]{0:T(1024)(128)(4,1)} %bitcast.193), calls=%async_computation.4 | async-start | bytes 8388608
  197.5 8.3 %copy-start.22 = (bf16[256,1024]{1,0:T(8,128)(2,1)}, bf16[256,1024]{1,0:T(8,128)(2,1)S(1)}, u32[]{:S(2)}) copy-start(bf16[256,1024]{1,0:T(8,128)(2,1)S(1)} %get-tuple-element.67.refs_2_) | copy-start | bytes 1572868
  341.7 119.4 %copy-start.28 = (f32[256,512]{1,0:T(8,128)S(1)}, f32[256,512]{1,0:T(8,128)}, u32[]{:S(2)}) copy-start(f32[256,512]{1,0:T(8,128)} %get-tuple-element.158) | copy-start | bytes 1572868
  341.7 120.2 %copy-start.27 = (f32[128,1024]{1,0:T(8,128)S(1)}, f32[128,1024]{1,0:T(8,128)}, u32[]{:S(2)}) copy-start(f32[128,1024]{1,0:T(8,128)} %get-tuple-element.159) | copy-start | bytes 1572868
  341.7 121.0 %copy-start.32 = (f32[256,384]{1,0:T(8,128)S(1)}, f32[256,384]{1,0:T(8,128)}, u32[]{:S(2)}) copy-start(f32[256,384]{1,0:T(8,128)} %get-tuple-element.160) | copy-start | bytes 1179652
  341.8 128.1 %copy-start.1 = (bf16[1024,1024]{1,0:T(8,128)(2,1)S(1)}, bf16[1024,1024]{1,0:T(8,128)(2,1)}, u32[]{:S(2)}) copy-start(bf16[1024,1024]{1,0:T(8,128)(2,1)} %param.35) | copy-start | bytes 6291460
  (28 other events, 121.1 us)

commit v4 on v2

--- a/solution.py
+++ b/solution.py
@@ -16,6 +16,12 @@
 
 EPSILON = 1e-05
 MASKED_SCORE = -1000000000.0
+
+SEGMENTS = (
+    (0, 3), (1, 3), (2, 3), (2, 2), (0, 2), (1, 2), (5, 3), (2, 1), (4, 3), (0, 1), (3, 3),
+    (0, 0), (5, 2), (3, 2), (0, -1), (3, 1), (5, 1), (5, 0), (4, 2), (2, 0), (4, 1), (1, 1),
+    (3, 0), (4, 0), (1, 0), (5, -1), (2, -1), (4, -1), (3, -1), (1, -1),
+)
 
 
 def extended(array, sides, width):
@@ -72,22 +78,20 @@
     return (grad_in + grad_values, grad_gain, (lowered, grad_hidden), (act_rows, grad_branch))
 
 
-def sum_kernel(groups, batches, rows_ref, total_ref, seq_slots, part, batch_slots, sends, arrivals):
+def sum_kernel(groups, batches, scatter, rows_ref, total_ref, seq_slots, part, batch_slots, sends, arrivals):
     s, b = lax.axis_index("seq"), lax.axis_index("batch")
     peers = [(b, lax.rem(s + k, groups)) for k in range(1, groups)]
     peers += [(lax.rem(b + k, batches), s) for k in range(1, batches)]
-    barrier = pltpu.get_barrier_semaphore()
-    for peer in peers:
-        pl.semaphore_signal(barrier, inc=1, device_id=peer, device_id_type=MESH)
-    pl.semaphore_wait(barrier, len(peers))
-
-    def spread(source, slots, mine, first, count):
-        slots[mine] = source[...]
+    greet(peers)
+    width = seq_slots.shape[2]
+
+    def spread(pick, slots, mine, first, count):
+        slots[mine] = pick(s)[...]
         copies = []
         for k in range(first, first + count):
             copies.append(
                 pltpu.make_async_remote_copy(
-                    src_ref=source,
+                    src_ref=pick(peers[k][1]),
                     dst_ref=slots.at[mine],
                     send_sem=sends.at[k],
                     recv_sem=arrivals.at[k],
@@ -103,22 +107,32 @@
             total = total + slots[i]
         return total
 
-    part[...] = spread(rows_ref, seq_slots, s, 0, groups - 1)
-    total_ref[...] = spread(part, batch_slots, b, groups - 1, batches - 1)
-
-
-def sum_everywhere(rows, collective_id):
+    def columns(owner):
+        if not scatter:
+            return rows_ref
+        return rows_ref.at[:, pl.ds(pl.multiple_of(owner * width, 128), width)]
+
+    part[...] = spread(columns, seq_slots, s, 0, groups - 1)
+    total_ref[...] = spread(lambda owner: part, batch_slots, b, groups - 1, batches - 1)
+
+
+def sum_everywhere(rows, collective_id, scatter=False):
     groups, batches = lax.axis_size("seq"), lax.axis_size("batch")
     copies = groups + batches - 2
-    return pl.pallas_call(
-        functools.partial(sum_kernel, groups, batches),
-        out_shape=jax.ShapeDtypeStruct(rows.shape, jnp.float32),
+    height, width = rows.shape
+    share = width // groups if scatter else width
+    direct = share % 128 == 0
+    if not direct:
+        share = width
+    total = pl.pallas_call(
+        functools.partial(sum_kernel, groups, batches, scatter and direct),
+        out_shape=jax.ShapeDtypeStruct((height, share), jnp.float32),
         in_specs=[pl.BlockSpec(memory_space=pltpu.VMEM)],
         out_specs=pl.BlockSpec(memory_space=pltpu.VMEM),
         scratch_shapes=[
-            pltpu.VMEM((groups, *rows.shape), jnp.float32),
-            pltpu.VMEM(rows.shape, jnp.float32),
-            pltpu.VMEM((batches, *rows.shape), jnp.float32),
+            pltpu.VMEM((groups, height, share), jnp.float32),
+            pltpu.VMEM((height, share), jnp.float32),
+            pltpu.VMEM((batches, height, share), jnp.float32),
             pltpu.SemaphoreType.DMA((copies,)),
             pltpu.SemaphoreType.DMA((copies,)),
         ],
@@ -126,6 +140,10 @@
             collective_id=collective_id, has_side_effects=True, vmem_limit_bytes=32 << 20
         ),
     )(rows)
+    if scatter and not direct:
+        share = width // groups
+        total = lax.dynamic_slice_in_dim(total, lax.axis_index("seq") * share, share, axis=1)
+    return total
 
 
 def halving_steps(first_seq):
@@ -321,12 +339,7 @@
 
 
 def greet_seq(groups, s, b):
-    barrier = pltpu.get_barrier_semaphore()
-    for k in range(1, groups):
-        pl.semaphore_signal(
-            barrier, inc=1, device_id=(b, lax.rem(s + k, groups)), device_id_type=MESH
-        )
-    pl.semaphore_wait(barrier, groups - 1)
+    greet([(b, lax.rem(s + k, groups)) for k in range(1, groups)])
 
 
 def partner_lanes(values):
@@ -550,6 +563,342 @@
     return out
 
 
+def flipped(index, places):
+    for bit, flip in places:
+        mine = lax.rem(index // (1 << bit), 2)
+        index = index + flip * (1 - 2 * mine) * (1 << bit)
+    return index
+
+
+def place_of(place, steps, axis, index):
+    flips = []
+    for order, (name, bit) in enumerate(steps):
+        if name == axis:
+            flips.append((bit, lax.rem(place // (1 << (len(steps) - 1 - order)), 2)))
+    return flipped(index, flips)
+
+
+class Job:
+    def __init__(self, parts, tall, order):
+        self.parts, self.tall, self.arrived = parts, tall, None
+        self.batches, self.groups = lax.axis_size("batch"), lax.axis_size("seq")
+        bits = {
+            "x": [("seq", 0)],
+            "y": [("seq", k) for k in range(1, self.groups.bit_length() - 1)],
+            "1": [("batch", 1)],
+            "2": [("batch", k) for k in range(2, self.batches.bit_length() - 1)],
+        }
+        self.steps = [step for letter in order for step in bits[letter]]
+        self.levels = len(self.steps)
+        self.half = 1 << (self.levels - 1)
+        if tall:
+            ((small, big),) = parts
+            self.rows = big.shape[1] // (self.batches * self.groups)
+            self.widths = [small.shape[1]]
+        else:
+            self.rows = parts[0][0].shape[1] // self.groups
+            self.widths = [big.shape[1] // self.batches for _, big in parts]
+        self.cols = sum(self.widths)
+        self.pieces = len(parts) * (1 + self.batches // 2)
+
+    def fits(self):
+        return self.rows % 128 == 0 and all(width % 128 == 0 for width in self.widths)
+
+    def operands(self):
+        return [array for part in self.parts for array in part]
+
+    def flops(self):
+        return sum(2 * small.size * big.shape[1] for small, big in self.parts)
+
+    def operand_scratch(self):
+        scratch = []
+        for small, big in self.parts:
+            scratch.append(pltpu.VMEM((2 * small.shape[0], small.shape[1]), jnp.bfloat16))
+            scratch.append(pltpu.VMEM((2 * big.shape[0], big.shape[1] // 2), jnp.bfloat16))
+        return scratch + [pltpu.SemaphoreType.DMA((self.pieces,))] * 3
+
+    def step_of(self, level):
+        return self.steps[self.levels - 1 - level]
+
+
+def greet(peers):
+    barrier = pltpu.get_barrier_semaphore()
+    for peer in peers:
+        pl.semaphore_signal(barrier, inc=1, device_id=peer, device_id_type=MESH)
+    pl.semaphore_wait(barrier, len(peers))
+
+
+def sibling_of(s, b):
+    return (b + 1 - 2 * lax.rem(b, 2), s)
+
+
+def partner_of(s, b, step):
+    axis, bit = step
+    if axis == "seq":
+        return (b, flipped(s, [(bit, 1)]))
+    return (flipped(b, [(bit, 1)]), s)
+
+
+def swap_operands(job, inputs, held, s, b):
+    core = lax.rem(b, 2)
+    local, moves, lands = held[2 * len(job.parts) :]
+    near, far = [], []
+
+    def bring(own_source, own_place, far_source, far_place):
+        n = len(near)
+        near.append(pltpu.make_async_copy(own_source, own_place, local.at[n]))
+        far.append(
+            pltpu.make_async_remote_copy(
+                src_ref=far_source,
+                dst_ref=far_place,
+                send_sem=moves.at[n],
+                recv_sem=lands.at[n],
+                device_id=sibling_of(s, b),
+                device_id_type=MESH,
+            )
+        )
+        far[-1].start()
+        near[-1].start()
+
+    for i in range(len(job.parts)):
+        small_in, big_in = inputs[2 * i : 2 * i + 2]
+        small, big = held[2 * i : 2 * i + 2]
+        frames = small_in.shape[0]
+        span = big_in.shape[1] // job.batches
+        own_rows, far_rows = pl.ds(0, frames), pl.ds(frames, frames)
+        bring(small_in, small.at[own_rows], small_in, small.at[far_rows])
+        for z in range(job.batches // 2):
+            here = pl.ds(pl.multiple_of((2 * z + core) * span, 128), span)
+            there = pl.ds(pl.multiple_of((2 * z + 1 - core) * span, 128), span)
+            inside = pl.ds(z * span, span)
+            bring(
+                big_in.at[:, here],
+                big.at[own_rows, inside],
+                big_in.at[:, there],
+                big.at[far_rows, inside],
+            )
+    return near, far
+
+
+def wait_operands(near, far):
+    for copy in near:
+        copy.wait()
+    for copy in far:
+        copy.wait_recv()
+
+
+def block_product(job, held, part, place, s, b):
+    small, big = held[2 * part : 2 * part + 2]
+    span = big.shape[1] // (job.batches // 2)
+    row = place_of(place, job.steps, "seq", s)
+    col = place_of(place, job.steps, "batch", b) // 2
+    if job.tall:
+        left = big[:, pl.ds(pl.multiple_of(col * span + row * job.rows, 128), job.rows)]
+        right = small[...]
+    else:
+        left = small[:, pl.ds(pl.multiple_of(row * job.rows, 128), job.rows)]
+        right = big[:, pl.ds(pl.multiple_of(col * span, 128), span)]
+    return lax.dot_general(
+        left, right, (((0,), (0,)), ((), ())), preferred_element_type=jnp.float32
+    )
+
+
+def columns_of(job, part):
+    start = sum(job.widths[:part])
+    return slice(start, start + job.widths[part])
+
+
+def first_kernel(job, *refs):
+    count = 2 * len(job.parts)
+    inputs, out, held = refs[:count], refs[count], refs[count + 1 :]
+    s, b = lax.axis_index("seq"), lax.axis_index("batch")
+    greet([sibling_of(s, b)])
+    near, far = swap_operands(job, inputs, held, s, b)
+    wait_operands(near, far)
+
+    def one_place(j, carry):
+        for part in range(len(job.parts)):
+            total = block_product(job, held, part, job.half + j, s, b)
+            out[j, :, columns_of(job, part)] = total.astype(jnp.bfloat16)
+        return carry
+
+    lax.fori_loop(0, job.half, one_place, 0)
+    for copy in far:
+        copy.wait_send()
+
+
+def first_blocks(job, collective_id):
+    operands = job.operands()
+    return pl.pallas_call(
+        functools.partial(first_kernel, job),
+        out_shape=jax.ShapeDtypeStruct((job.half, job.rows, job.cols), jnp.bfloat16),
+        in_specs=[pl.BlockSpec(memory_space=pl.ANY)] * len(operands),
+        out_specs=pl.BlockSpec(memory_space=pltpu.VMEM),
+        scratch_shapes=job.operand_scratch(),
+        compiler_params=pltpu.CompilerParams(
+            collective_id=collective_id, has_side_effects=True, vmem_limit_bytes=24 << 20
+        ),
+        cost_estimate=pl.CostEstimate(
+            flops=job.flops() // 2, bytes_accessed=8 << 20, transcendentals=0
+        ),
+    )(*operands)
+
+
+def send_first(job, collective_id):
+    if job.fits():
+        axis, bit = job.steps[0]
+        pairs = [(i, i ^ (1 << bit)) for i in range(lax.axis_size(axis))]
+        job.sent = first_blocks(job, collective_id)
+        job.arrived = lax.ppermute(job.sent, axis, pairs)
+    return job
+
+
+def scatter_kernel(jobs, sequence, *refs):
+    inputs, outs, scratch = [], [], []
+    refs = list(refs)
+    for job in jobs:
+        take = 2 * len(job.parts) + (job.arrived is not None)
+        inputs.append(refs[:take])
+        refs = refs[take:]
+    for job in jobs:
+        outs.append(refs[: len(job.parts)])
+        refs = refs[len(job.parts) :]
+    for job in jobs:
+        take = 2 * len(job.parts) + 3 + 5
+        scratch.append((refs[: take - 5], *refs[take - 5 : take]))
+        refs = refs[take:]
+    s, b = lax.axis_index("seq"), lax.axis_index("batch")
+    greet([sibling_of(s, b)] + [partner_of(s, b, step) for step in sorted(jobs[0].steps)])
+
+    def slot_of(job, place):
+        return lax.rem(place, job.half)
+
+    def copy_of(i, place, level):
+        job = jobs[i]
+        _, sending, arrived, sends, recvs, _ = scratch[i]
+        return pltpu.make_async_remote_copy(
+            src_ref=sending.at[slot_of(job, place)],
+            dst_ref=arrived.at[place - 1],
+            send_sem=sends.at[slot_of(job, place)],
+            recv_sem=recvs.at[place - 1],
+            device_id=partner_of(s, b, job.step_of(level)),
+            device_id_type=MESH,
+        )
+
+    def first_copy(i):
+        job = jobs[i]
+        return pltpu.make_async_copy(
+            inputs[i][-1],
+            scratch[i][2].at[pl.ds(job.half - 1, job.half)],
+            scratch[i][5],
+        )
+
+    works = []
+    for i, job in enumerate(jobs):
+        works.append(swap_operands(job, inputs[i], scratch[i][0], s, b))
+        if job.arrived is not None:
+            first_copy(i).start()
+
+    def block_sums(i, place, level):
+        job = jobs[i]
+        held, _, arrived = scratch[i][:3]
+        for m in range(job.levels - 1, level, -1):
+            if m < job.levels - 1 or job.arrived is None:
+                copy_of(i, (1 << m) + place, m).wait_recv()
+        totals = []
+        for part in range(len(job.parts)):
+            total = block_product(job, held, part, place, s, b)
+            for m in range(job.levels - 1, level, -1):
+                came = arrived[(1 << m) + place - 1, :, columns_of(job, part)]
+                total = total + came.astype(jnp.float32)
+            totals.append(total)
+        return totals
+
+    def send_block(i, place, level):
+        job = jobs[i]
+        sending = scratch[i][1]
+        totals = block_sums(i, place, level)
+        if level < job.levels - 1 and job.arrived is None:
+            copy_of(i, place + job.half, job.levels - 1).wait_send()
+        for part, total in enumerate(totals):
+            sending[slot_of(job, place), :, columns_of(job, part)] = total.astype(jnp.bfloat16)
+        copy_of(i, place, level).start()
+
+    levels = jobs[0].levels
+    ready = set()
+    for i, level in sequence:
+        job = jobs[i]
+        if i not in ready:
+            ready.add(i)
+            wait_operands(*works[i])
+            if job.arrived is not None:
+                first_copy(i).wait()
+        if level < 0:
+            for part, total in enumerate(block_sums(i, 0, -1)):
+                outs[i][part][...] = total
+        elif level < levels - 1 or job.arrived is None:
+
+            def one_place(j, carry, level=level, i=i):
+                send_block(i, (2 << level) - 1 - j, level)
+                return carry
+
+            lax.fori_loop(0, 1 << level, one_place, 0)
+    for i, job in enumerate(jobs):
+        for copy in works[i][1]:
+            copy.wait_send()
+        if job.arrived is None:
+            copy_of(i, job.half, levels - 1).wait_send()
+        for level in range(levels - 1):
+
+            def one_wait(j, carry, level=level, i=i):
+                copy_of(i, (1 << level) + j, level).wait_send()
+                return carry
+
+            lax.fori_loop(0, 1 << level, one_wait, 0)
+
+
+def scatter_sums(jobs, sequence, collective_id):
+    if not all(job.fits() for job in jobs):
+        return [
+            [
+                owned_sum(*((big, small) if job.tall else (small, big)), job.tall, job.tall)
+                for small, big in job.parts
+            ]
+            for job in jobs
+        ]
+    scratch, operands, outs = [], [], []
+    for job in jobs:
+        block = (job.rows, job.cols)
+        scratch += job.operand_scratch()
+        scratch += [
+            pltpu.VMEM((job.half, *block), jnp.bfloat16),
+            pltpu.VMEM((2 * job.half - 1, *block), jnp.bfloat16),
+            pltpu.SemaphoreType.DMA((job.half,)),
+            pltpu.SemaphoreType.DMA((2 * job.half - 1,)),
+            pltpu.SemaphoreType.DMA,
+        ]
+        operands += job.operands()
+        if job.arrived is not None:
+            operands.append(job.arrived)
+        outs += [jax.ShapeDtypeStruct((job.rows, width), jnp.float32) for width in job.widths]
+    results = list(
+        pl.pallas_call(
+            functools.partial(scatter_kernel, jobs, sequence),
+            out_shape=outs,
+            in_specs=[pl.BlockSpec(memory_space=pl.ANY)] * len(operands),
+            out_specs=[pl.BlockSpec(memory_space=pltpu.VMEM)] * len(outs),
+            scratch_shapes=scratch,
+            compiler_params=pltpu.CompilerParams(
+                collective_id=collective_id, has_side_effects=True, vmem_limit_bytes=60 << 20
+            ),
+            cost_estimate=pl.CostEstimate(
+                flops=sum(job.flops() for job in jobs), bytes_accessed=400 << 20, transcendentals=0
+            ),
+        )(*operands)
+    )
+    return [[results.pop(0) for _ in job.parts] for job in jobs]
+
+
 def shards(
     frames_in,
     cotangent,
@@ -706,10 +1055,18 @@
     gain_grads = jnp.stack(
         [grad_gain_zero, grad_gain_one, grad_gain_two, grad_gain_three, grad_gain_four], axis=0
     )
+    jobs = [
+        Job([ffn2_up_pair], False, "yx12"),
+        Job([ffn2_down_pair[::-1]], True, "12xy"),
+        Job([(conv_in, grad_gl), (attn_out, grad_r), (conv_act, grad_r2)], False, "xy12"),
+        Job([(attn_in, grad_qkv)], False, "x12y"),
+        Job([ffn1_down_pair[::-1]], True, "yx12"),
+        Job([ffn1_up_pair], False, "yx12"),
+    ]
+    sums = scatter_sums(jobs, SEGMENTS, 7)
     small_rows = jnp.concatenate([gain_grads, cond_grad_rows, kernel_grads], axis=0)
-    small_sums = sum_everywhere(small_rows, 3)
-    seq_width = model_width // groups
-    small_piece = lax.dynamic_slice_in_dim(small_sums, seq_index * seq_width, seq_width, axis=1)
+    small_rows = jnp.pad(small_rows, ((0, -small_rows.shape[0] % 8), (0, 0)))
+    small_piece = sum_everywhere(small_rows, 3, scatter=True)
     cond_end = 5 + level_count + 1
     new_mean = 0.9 * running_mean + 0.1 * batchnorm_frame_mean
     new_var = 0.9 * running_var + 0.1 * bn_var * count_of_frames / (count_of_frames - 1.0)
@@ -718,17 +1075,17 @@
         grad_zero.astype(jnp.bfloat16)[None],
         small_piece[5:cond_end],
         small_piece[0:5],
-        owned_sum(*ffn1_up_pair, False, False),
-        owned_sum(*ffn1_down_pair, True, True),
-        owned_sum(attn_in, grad_qkv, False, True),
-        owned_sum(attn_out, grad_r, False, False),
-        owned_sum(conv_in, grad_gl, False, True),
+        sums[5][0],
+        sums[4][0],
+        sums[3][0],
+        sums[2][1],
+        sums[2][0],
         small_piece[cond_end : cond_end + taps],
         gradient_normalized_sum,
         gradient_sum_total,
-        owned_sum(conv_act, grad_r2, False, False),
-        owned_sum(*ffn2_up_pair, False, False),
-        owned_sum(*ffn2_down_pair, True, True),
+        sums[2][2],
+        sums[0][0],
+        sums[1][0],
         new_mean,
         new_var,
     )

time: 616 us -> 426 us (0.69)
  waiting for transfers between devices: 188 us -> 3 us
  Pallas kernels: 160 us -> 295 us
  other arithmetic: 81.9 us -> 26.5 us
  starting transfers between devices: 57.8 us -> 11 us
  local copies, waits for them, and re-layouts: 42.9 us -> 21.7 us
  matrix products: 72.6 us -> 57.3 us
    ppermute x40 -> x0, waiting for transfers between devices: 188 us -> none  [owned_sum(): arrived = lax.ppermute(blocks[half:], axis, pairs)]
    pallas_call x11 -> x4, Pallas kernels: 76.7 us -> 214 us  [the longest x1 183 us: scatter_sums(): pl.pallas_call(functools.partial(scatter_kernel, jobs, sequence), out_sha...]
    convert_element_type x32 -> x0, other arithmetic: 46.2 us -> none  [owned_sum(): blocks = total.astype(jnp.bfloat16) if half > 1 else total]
    ppermute x40 -> x0, starting transfers between devices: 45.8 us -> none  [owned_sum(): arrived = lax.ppermute(blocks[half:], axis, pairs)]
    slice x40 -> x0, local copies, waits for them, and re-layouts: 26.4 us -> none  [owned_sum(): arrived = lax.ppermute(blocks[half:], axis, pairs)]
    dot_general x8, matrix products: 47.5 us -> 27.3 us  [times_transposed(): lax.dot_general(left_side, weight, (((1,), (1,)), ((), ())), preferred_el...]
    unnamed x158 -> x122, local copies, waits for them, and re-layouts: 10 us -> 17.7 us
    squeeze x8 -> x0, other arithmetic: 6.32 us -> none  [owned_sum(): return blocks[0]]
  transfers between devices with their start and end apart: 44 -> 4, of which waited for: 16 -> 1; matrix products, arithmetic and copies ran while one was open for 19% -> 1% of each run, Pallas kernels for 16% -> 0%
where the time goes in v4:
time: 426 us; the launch traced here: 418 us
  Pallas kernels  295 us (69%)
  matrix products  57.3 us (13%)
  other arithmetic  26.5 us (6%)
  local copies, waits for them, and re-layouts  21.7 us (5%)
  starting transfers between devices  11 us (3%)
    pallas_call x1, Pallas kernels, scatter_sums(): pl.pallas_call(functools.partial(scatter_kernel, jobs, sequence), out_sha...  183 us
    pallas_call x1, Pallas kernels, attend_back(): pl.pallas_call(functools.partial(attend_back_kernel, groups, heads), out_...  45.7 us
    pallas_call x1, Pallas kernels, attend(): pl.pallas_call(functools.partial(attend_kernel, groups, heads), out_shape...  35.5 us
    pallas_call x3, Pallas kernels, sum_everywhere(): pl.pallas_call(functools.partial(sum_kernel, groups, batches, scatter and...  30.8 us
    dot_general x8, matrix products, times_transposed(): lax.dot_general(left_side, weight, (((1,), (1,)), ((), ())), preferred_el...  27.3 us
    unnamed x122, local copies, waits for them, and re-layouts  17.7 us
    dot_general x2, matrix products, ffn_forward(): hidden = jnp.dot(lowered, up_weight, preferred_element_type=jnp.float32)  16.2 us
  transfers between devices with their start and end apart: 4, of which 1 were waited for; matrix products, arithmetic and copies ran while one was open for 1% of the time, Pallas kernels for 0%

profile of v4, /device:TPU:0, one launch (start us, length us, event | category | flops | bytes accessed | tf_op | source)
XLA Modules:
  0.0 417.8 jit_solution(8787625984241592279)
XLA Ops:
  6.0 1.4 multiply_reduce_fusion.16
  7.5 1.5 multiply_convert_fusion.13.refs_14_
  9.0 8.0 %multiply_convert_fusion.1 = (bf16[256,4096]{1,0:T(8,128)(2,1)S(1)}, f32[256,4096]{1,0:T(8,128)}) fusion(bf16[256,1024]{1,0:T(8,128)(2,1)S(1)} %multiply_convert_fusion.13.refs_14_, bf16[1024,4096]{1,0:T(8,128)(2,1)} %param.27), kind=kOutput, calls=%fused_computation.8 | convolution fusion | flops 2152726528 | bytes 15204352 | tf_op jit(solution)/shard_map/dot_general | solution.py:64
  17.0 2.4 fusion.52
  22.1 4.6 %fusion.56.qkv_ref = f32[256,3072]{1,0:T(8,128)S(1)} fusion(bf16[256,1024]{1,0:T(8,128)(2,1)S(1)} %multiply_convert_fusion.12.refs_10_, bf16[1024,3072]{1,0:T(8,128)(2,1)} %param.29), kind=kOutput, calls=%fused_computation.193 | convolution fusion | flops 1610612736 | bytes 9961472 | tf_op jit(solution)/shard_map/dot_general | solution.py:949
  27.8 35.5 %shard_map.323 = (bf16[1024,768]{1,0:T(8,128)(2,1)S(1)}, bf16[256,1024]{1,0:T(8,128)(2,1)S(1)}) custom-call(s32[1]{0:T(128)} %dynamic_slice.3.length_ref, f32[256,3072]{1,0:T(8,128)S(1)} %fusion.56.qkv_ref, f32[3,256,128]{2,1,0:T(8,128)S(1)} %pad_maximum_fusion.7.cos_ref, f32[3,256,128]{2,1,0:T(8,128)S(1)} %pad_maximum_fusion.8.sin_ref), custom_call_target="tpu_custom_call" | custom-call | flops 1073741824 | bytes 5242880 | tf_op jit(solution)/shard_map/pallas_call | solution.py:371
  69.7 5.4 %collective-permute-start = (bf16[2,1024]{1,0:T(2,128)(2,1)S(1)}, bf16[2,1024]{1,0:T(2,128)(2,1)S(1)}, u32[]{:S(2)}, u32[]{:S(2)}) collective-permute-start(bf16[2,1024]{1,0:T(2,128)(2,1)S(1)} %get-tuple-element.89), channel_id=1, source_target_pairs={{0,1},{1,2},{2,3},{4,5},{5,6},{6,7},{8,9},{9,10},{10,11},{12,13},{... | collective-permute-start | bytes 12296 | tf_op jit(solution)/shard_map/ppermute | solution.py:34
  75.2 1.9 multiply_sine_fusion
  79.3 3.2 multiply_reduce_fusion.13
  82.5 11.6 %shard_map.324 = f32[2,1024]{1,0:T(2,128)S(1)} custom-call(f32[2,1024]{1,0:T(2,128)S(1)} %pad_maximum_fusion.9.rows_ref), custom_call_target="tpu_custom_call" | custom-call | tf_op jit(solution)/shard_map/pallas_call | solution.py:127
  94.5 2.2 fusion.54
  97.3 8.2 %multiply_convert_fusion = (bf16[256,4096]{1,0:T(8,128)(2,1)S(1)}, f32[256,4096]{1,0:T(8,128)}) fusion(bf16[256,1024]{1,0:T(8,128)(2,1)S(1)} %multiply_convert_fusion.8.refs_0_, bf16[1024,4096]{1,0:T(8,128)(2,1)} %param.36), kind=kOutput, calls=%fused_computation.6 | convolution fusion | flops 2152726528 | bytes 15204352 | tf_op jit(solution)/shard_map/dot_general | solution.py:64
  105.5 2.5 fusion.55
  110.2 5.7 %fusion.3.refs_1_ = bf16[256,4096]{1,0:T(8,128)(2,1)S(1)} fusion(bf16[256,1024]{1,0:T(8,128)(2,1)S(1)} %multiply_convert_fusion.6.refs_2_, bf16[4096,1024]{1,0:T(8,128)(2,1)S(1)} %bitcast.190, f32[256,4096]{1,0:T(8,128)} %get-tuple-element.124), kind=kOutput, calls=%fused_computation.5 | convolution fusion | flops 2156920832 | bytes 15204352 | tf_op jit(solution)/shard_map/dot_general | solution.py:56
  115.9 6.7 %multiply_reduce_fusion.1 = (f32[1024]{0:T(1024)S(1)}, f32[256]{0:T(256)S(1)}, f32[256,1024]{1,0:T(8,128)S(1)}) fusion(f32[256,1024]{1,0:T(8,128)S(1)} %get-tuple-element.122, f32[256]{0:T(256)S(1)} %fusion.36, f32[256]{0:T(256)S(1)} %broadcast_multiply_fusion.5, f32[1024]{0:T(1024)S(1)} %bitcast.154, bf16[256,4096]{1,0:T(8,128)(2,1)S(1)} %fusion.3.refs_1_, ...), kind=kOutput, calls=%fused_computation.48 | convolution fusion | flops 2149317376 | bytes 12594176 | tf_op jit(solution)/shard_map/dot_general | solution.py:56
  124.6 9.2 %shard_map.325 = f32[2,1024]{1,0:T(2,128)S(1)} custom-call(f32[2,1024]{1,0:T(2,128)S(1)} %pad_maximum_fusion.10.rows_ref), custom_call_target="tpu_custom_call" | custom-call | tf_op jit(solution)/shard_map/pallas_call | solution.py:127
  134.9 3.0 collective-permute-start.3
  140.4 3.0 collective-permute-done.2
  144.8 1.5 multiply_reduce_fusion.2
  148.7 45.7 %shard_map.326.refs_11_ = bf16[256,3072]{1,0:T(8,128)(2,1)S(1)} custom-call(s32[1]{0:T(128)} %dynamic_slice.3.length_ref, bf16[1024,768]{1,0:T(8,128)(2,1)S(1)} %copy-done.5, bf16[256,1024]{1,0:T(8,128)(2,1)S(1)} %convolution_convert_fusion.grad_ref, f32[1024,128]{1,0:T(8,128)S(1)} %pad_maximum_fusion.5.cos_ref, f32[1024,128]{1,0:T(8,128)S(1)} %pad_maximum_fusion.6.sin_ref), custom_call_target="tpu_custom_call" | custom-call | flops 2684354560 | bytes 4194304 | tf_op jit(solution)/shard_map/pallas_call | solution.py:535
  194.5 2.1 multiply_reduce_fusion.3
  197.3 1.6 copy-done.48
  199.0 6.7 %fusion.2.refs_15_ = bf16[256,4096]{1,0:T(8,128)(2,1)S(1)} fusion(bf16[256,1024]{1,0:T(8,128)(2,1)S(1)} %get-tuple-element.67.refs_12_, bf16[4096,1024]{1,0:T(8,128)(2,1)} %param.28, f32[256,4096]{1,0:T(8,128)S(1)} %copy-done.48), kind=kOutput, calls=%fused_computation.4 | convolution fusion | flops 2156920832 | bytes 15204352 | tf_op jit(solution)/shard_map/dot_general | solution.py:56
  205.7 2.7 multiply_reduce_fusion.4
  210.4 10.0 %shard_map.327 = f32[24,256]{1,0:T(8,128)S(1)} custom-call(f32[24,1024]{1,0:T(8,128)S(1)} %pad.7.rows_ref), custom_call_target="tpu_custom_call" | custom-call | tf_op jit(solution)/shard_map/pallas_call | solution.py:127
  222.8 182.8 %shard_map.328 = (f32[256,512]{1,0:T(8,128)}, f32[128,1024]{1,0:T(8,128)}, f32[256,256]{1,0:T(8,128)}, f32[256,128]{1,0:T(8,128)}, f32[256,128]{1,0:T(8,128)}, /...) custom-call(bf16[256,1024]{1,0:T(8,128)(2,1)} %copy-done.30, bf16[256,4096]{1,0:T(8,128)(2,1)} %copy-done.44, ...), custom_call_target="tpu_custom_call" | custom-call | flops 12348030976 | bytes 419430400 | tf_op jit(solution)/shard_map/pallas_call | solution.py:885
  405.6 2.0 copy.81
  407.6 1.9 copy.82
  409.5 1.8 copy.83
  411.2 1.6 copy.84
  412.8 1.7 copy.85
  414.5 1.6 copy.86
  (217 shorter events, 34.8 us)
Async XLA Ops:
  0.7 93.9 %copy-start = (bf16[1024,1024]{1,0:T(8,128)(2,1)S(1)}, bf16[1024,1024]{1,0:T(8,128)(2,1)}, u32[]{:S(2)}) copy-start(bf16[1024,1024]{1,0:T(8,128)(2,1)} %param.35) | copy-start | bytes 6291460
  7.4 9.5 %slice-start.2 = ((s8[8388608]{0:T(1024)(128)(4,1)}), s8[4194304]{0:T(1024)(128)(4,1)S(1)}, s32[]{:S(2)}) async-start(s8[8388608]{0:T(1024)(128)(4,1)} %bitcast.191), calls=%async_computation.2 | async-start | bytes 8388608
  19.5 43.9 %copy-start.8 = (f32[256,1024]{1,0:T(8,128)}, f32[256,1024]{1,0:T(8,128)S(1)}, u32[]{:S(2)}) copy-start(f32[256,1024]{1,0:T(8,128)S(1)} %get-tuple-element.118) | copy-start | bytes 3145732
  27.8 35.6 %copy-start.17 = (bf16[1024,1024]{1,0:T(8,128)(2,1)S(1)}, bf16[1024,1024]{1,0:T(8,128)(2,1)}, u32[]{:S(2)}) copy-start(bf16[1024,1024]{1,0:T(8,128)(2,1)} %param.30) | copy-start | bytes 6291460
  66.7 8.4 %copy-start.34 = (bf16[5,1024]{1,0:T(8,128)(2,1)S(1)}, bf16[5,1024]{1,0:T(8,128)(2,1)}, u32[]{:S(2)}) copy-start(bf16[5,1024]{1,0:T(8,128)(2,1)} %param.32) | copy-start | bytes 30724
  68.0 9.7 %copy-start.10 = (f32[256,2048]{1,0:T(8,128)}, f32[256,2048]{1,0:T(8,128)S(1)}, u32[]{:S(2)}) copy-start(f32[256,2048]{1,0:T(8,128)S(1)} %fusion.57) | copy-start | bytes 6291460
  68.0 10.6 %copy-start.40 = (bf16[1024]{0:T(1024)(128)(2,1)S(1)}, bf16[1024]{0:T(1024)(128)(2,1)}, u32[]{:S(2)}) copy-start(bf16[1024]{0:T(1024)(128)(2,1)} %param.34) | copy-start | bytes 6148
  68.0 10.6 %copy-start.37 = (bf16[1024]{0:T(1024)(128)(2,1)S(1)}, bf16[1024]{0:T(1024)(128)(2,1)}, u32[]{:S(2)}) copy-start(bf16[1024]{0:T(1024)(128)(2,1)} %param.33) | copy-start | bytes 6148
  68.4 9.4 %copy-start.14 = (bf16[256,1024]{1,0:T(8,128)(2,1)}, bf16[256,1024]{1,0:T(8,128)(2,1)S(1)}, u32[]{:S(2)}) copy-start(bf16[256,1024]{1,0:T(8,128)(2,1)S(1)} %multiply_convert_fusion.10) | copy-start | bytes 1572868
  68.4 10.9 %collective-permute-start.1 = (bf16[2,1024]{1,0:T(2,128)(2,1)S(1)}, bf16[2,1024]{1,0:T(2,128)(2,1)S(1)}, u32[]{:S(2)}, u32[]{:S(2)}) collective-permute-start(bf16[2,1024]{1,0:T(2,128)(2,1)S(1)} %get-tuple-element.90), channel_id=1, source_target_pairs={{1,0},{2,1},{3,2},{5,4},{6,5},{7,6},{9,8},{10,9},{11,10},{13,12},{... | collective-permute-start | bytes 12296 | tf_op jit(solution)/shard_map/ppermute | solution.py:35
  69.7 9.6 %collective-permute-start = (bf16[2,1024]{1,0:T(2,128)(2,1)S(1)}, bf16[2,1024]{1,0:T(2,128)(2,1)S(1)}, u32[]{:S(2)}, u32[]{:S(2)}) collective-permute-start(bf16[2,1024]{1,0:T(2,128)(2,1)S(1)} %get-tuple-element.89), channel_id=1, source_target_pairs={{0,1},{1,2},{2,3},{4,5},{5,6},{6,7},{8,9},{9,10},{10,11},{12,13},{... | collective-permute-start | bytes 12296 | tf_op jit(solution)/shard_map/ppermute | solution.py:34
  94.5 11.0 %copy-start.16 = (bf16[256,1024]{1,0:T(8,128)(2,1)}, bf16[256,1024]{1,0:T(8,128)(2,1)S(1)}, u32[]{:S(2)}) copy-start(bf16[256,1024]{1,0:T(8,128)(2,1)S(1)} %multiply_convert_fusion.9.refs_8_) | copy-start | bytes 1572868
  96.7 8.8 %slice-start = ((s8[8388608]{0:T(1024)(128)(4,1)}), s8[4194304]{0:T(1024)(128)(4,1)S(1)}, s32[]{:S(2)}) async-start(s8[8388608]{0:T(1024)(128)(4,1)} %bitcast.189), calls=%async_computation | async-start | bytes 8388608
  123.3 10.5 %copy-start.15 = (bf16[256,1024]{1,0:T(8,128)(2,1)S(1)}, bf16[256,1024]{1,0:T(8,128)(2,1)}, u32[]{:S(2)}) copy-start(bf16[256,1024]{1,0:T(8,128)(2,1)} %copy-done.14) | copy-start | bytes 1572868
  123.3 15.9 %copy-start.38 = (f32[1024]{0:T(1024)S(1)}, f32[1024]{0:T(1024)}, u32[]{:S(2)}) copy-start(f32[1024]{0:T(1024)} %param.38) | copy-start | bytes 12292
  123.4 16.5 %copy-start.39 = (f32[1024]{0:T(1024)S(1)}, f32[1024]{0:T(1024)}, u32[]{:S(2)}) copy-start(f32[1024]{0:T(1024)} %param.39) | copy-start | bytes 12292
  123.4 20.1 %copy-start.11 = (f32[256,2048]{1,0:T(8,128)S(1)}, f32[256,2048]{1,0:T(8,128)}, u32[]{:S(2)}) copy-start(f32[256,2048]{1,0:T(8,128)} %copy-done.10) | copy-start | bytes 6291460
  133.8 11.0 %copy-start.35 = (f32[1,1024]{1,0:T(1,128)}, f32[1,1024]{1,0:T(1,128)S(1)}, u32[]{:S(2)}) copy-start(f32[1,1024]{1,0:T(1,128)S(1)} %get-tuple-element.109) | copy-start | bytes 12292
  133.8 11.0 %copy-start.36 = (f32[1,1024]{1,0:T(1,128)}, f32[1,1024]{1,0:T(1,128)S(1)}, u32[]{:S(2)}) copy-start(f32[1,1024]{1,0:T(1,128)S(1)} %get-tuple-element.110) | copy-start | bytes 12292
  134.9 9.9 %copy-start.7 = (f32[256,1024]{1,0:T(8,128)S(1)}, f32[256,1024]{1,0:T(8,128)}, u32[]{:S(2)}) copy-start(f32[256,1024]{1,0:T(8,128)} %copy-done.6) | copy-start | bytes 3145732
  134.9 9.9 %copy-start.42 = (bf16[1024,2048]{1,0:T(8,128)(2,1)S(1)}, bf16[1024,2048]{1,0:T(8,128)(2,1)}, u32[]{:S(2)}) copy-start(bf16[1024,2048]{1,0:T(8,128)(2,1)} %param.31) | copy-start | bytes 12582916
  134.9 5.5 %collective-permute-start.3 = (bf16[2,1024]{1,0:T(2,128)(2,1)S(1)}, bf16[2,1024]{1,0:T(2,128)(2,1)S(1)}, u32[]{:S(2)}, u32[]{:S(2)}) collective-permute-start(bf16[2,1024]{1,0:T(2,128)(2,1)S(1)} %get-tuple-element.88), channel_id=1, source_target_pairs={{0,1},{1,2},{2,3},{4,5},{5,6},{6,7},{8,9},{9,10},{10,11},{12,13},{... | collective-permute-start | bytes 12296 | tf_op jit(solution)/shard_map/ppermute | solution.py:34
  137.9 5.5 %collective-permute-start.2 = (bf16[2,1024]{1,0:T(2,128)(2,1)S(1)}, bf16[2,1024]{1,0:T(2,128)(2,1)S(1)}, u32[]{:S(2)}, u32[]{:S(2)}) collective-permute-start(bf16[2,1024]{1,0:T(2,128)(2,1)S(1)} %get-tuple-element.87), channel_id=1, source_target_pairs={{1,0},{2,1},{3,2},{5,4},{6,5},{7,6},{9,8},{10,9},{11,10},{13,12},{... | collective-permute-start | bytes 12296 | tf_op jit(solution)/shard_map/ppermute | solution.py:35
  147.9 46.5 %slice-start.6 = ((s8[6291456]{0:T(1024)(128)(4,1)}), s8[4194304]{0:T(1024)(128)(4,1)S(1)}, s32[]{:S(2)}) async-start(s8[6291456]{0:T(1024)(128)(4,1)} %bitcast.195), calls=%async_computation.6 | async-start | bytes 8388608
  148.7 45.7 %copy-start.9 = (f32[256,1024]{1,0:T(8,128)S(1)}, f32[256,1024]{1,0:T(8,128)}, u32[]{:S(2)}) copy-start(f32[256,1024]{1,0:T(8,128)} %copy-done.8) | copy-start | bytes 3145732
  148.7 45.7 %slice-start.7 = ((s8[6291456]{0:T(1024)(128)(4,1)}), s8[2097152]{0:T(1024)(128)(4,1)S(1)}, s32[]{:S(2)}) async-start(s8[6291456]{0:T(1024)(128)(4,1)} %bitcast.195), calls=%async_computation.7 | async-start | bytes 4194304
  197.0 8.7 %slice-start.4 = ((s8[8388608]{0:T(1024)(128)(4,1)}), s8[4194304]{0:T(1024)(128)(4,1)S(1)}, s32[]{:S(2)}) async-start(s8[8388608]{0:T(1024)(128)(4,1)} %bitcast.193), calls=%async_computation.4 | async-start | bytes 8388608
  208.4 13.3 %copy-start.20 = (bf16[256,1024]{1,0:T(8,128)(2,1)S(1)}, bf16[256,1024]{1,0:T(8,128)(2,1)}, u32[]{:S(2)}) copy-start(bf16[256,1024]{1,0:T(8,128)(2,1)} %copy-done.19) | copy-start | bytes 1572868
  208.4 13.3 %copy-start.23 = (bf16[256,1024]{1,0:T(8,128)(2,1)S(1)}, bf16[256,1024]{1,0:T(8,128)(2,1)}, u32[]{:S(2)}) copy-start(bf16[256,1024]{1,0:T(8,128)(2,1)} %copy-done.22) | copy-start | bytes 1572868
  222.8 194.8 %copy-start.1 = (bf16[1024,1024]{1,0:T(8,128)(2,1)S(1)}, bf16[1024,1024]{1,0:T(8,128)(2,1)}, u32[]{:S(2)}) copy-start(bf16[1024,1024]{1,0:T(8,128)(2,1)} %param.35) | copy-start | bytes 6291460
  405.6 10.4 %copy-start.32 = (f32[256,512]{1,0:T(8,128)S(1)}, f32[256,512]{1,0:T(8,128)}, u32[]{:S(2)}) copy-start(f32[256,512]{1,0:T(8,128)} %get-tuple-element.167) | copy-start | bytes 1572868
  405.6 11.2 %copy-start.31 = (f32[128,1024]{1,0:T(8,128)S(1)}, f32[128,1024]{1,0:T(8,128)}, u32[]{:S(2)}) copy-start(f32[128,1024]{1,0:T(8,128)} %get-tuple-element.168) | copy-start | bytes 1572868
  (29 other events, 118.1 us)
